TPU v7x, 32 devices: a whole 2x2x4 slice. The times are simulated.
32 devices in a mesh: gx: 8 (over z, x), gy: 4 (over y, core).
Axes of the slice: x: 2, y: 2, z: 4, core: 2. Of those that a mesh axis runs over, the one named last changes fastest.
Arguments:
- tokens: bfloat16 [128, 64, 2, 512], P('gx', 'gy'), may hold values from -6 to 6
- cotangent: bfloat16 [128, 64, 2, 512], P('gx', 'gy'), may hold values from -6 to 6
- gain_x: float32 [512], replicated, may hold values from 0.1 to 1.9
- w_qkv_x: bfloat16 [512, 1536], replicated, may hold values from -5 to 5, as said below
- w_out_x: bfloat16 [512, 512], replicated, may hold values from -0.25 to 0.25
- gain_y: float32 [512], replicated, may hold values from 0.1 to 1.9
- w_qkv_y: bfloat16 [512, 1536], replicated, may hold values from -5 to 5, as said below
- w_out_y: bfloat16 [512, 512], replicated, may hold values from -0.25 to 0.25
- gain_mlp: float32 [512], replicated, may hold values from 0.1 to 1.9
- w_up: bfloat16 [512, 2048], replicated, may hold values from -0.25 to 0.25
- w_down: bfloat16 [2048, 512], replicated, may hold values from -0.125 to 0.125
Outputs:
- grad_tokens: bfloat16 [128, 64, 2, 512], P('gx', 'gy')
Inputs may be any that keep to these rules, and one draw needn't show every extreme that they name: `w_qkv_x`: query, key and value projections side by side. `w_qkv_y`: query, key and value projections side by side.
All inputs are finite; a program needn't handle non-finite values.
Results may differ from a plain program's by a relative error of at most 0.013.
Values may be sent and summed in bfloat16 or wider, within the bound.
No kernel may reach another device: no remote copies, remote signals or barrier semaphores. Data moves between devices by JAX's collectives and lax.ppermute only.
A program may use at most 128 MiB of HBM per device.

v0:
```python
from functools import partial

import jax
import jax.numpy as jnp
from jax import lax
from jax.sharding import PartitionSpec as P

D = 512
HEADS = 8


def to_low(tensor):
    return lax.optimization_barrier(tensor.astype(jnp.bfloat16))


def layer_norm(inputs, norm_gain):
    average = jnp.mean(inputs, -1, keepdims=True)
    centred = inputs - average
    variance = jnp.mean(centred * centred, -1, keepdims=True)
    return centred * lax.rsqrt(variance + 1e-05) * norm_gain


def norm_back(inputs, norm_gain, gradient):
    _, pullback = jax.vjp(lambda tensor: layer_norm(tensor, norm_gain), inputs)
    return pullback(gradient)[0]


def project(tensor, weight):
    lead_dims = tensor.shape[:-1]
    flattened = tensor.reshape(-1, tensor.shape[-1])
    result = jnp.dot(flattened, weight, preferred_element_type=jnp.float32)
    return result.reshape(lead_dims + (weight.shape[1],))


def project_back(tensor, weight):
    lead_dims = tensor.shape[:-1]
    flattened = tensor.reshape(-1, tensor.shape[-1])
    result = lax.dot_general(
        flattened, weight, (((1,), (1,)), ((), ())), preferred_element_type=jnp.float32
    )
    return result.reshape(lead_dims + (weight.shape[0],))


def heads_of(tensor, which_part):
    lead_dims = tensor.shape[:-1]
    block_part = tensor[..., which_part * D : (which_part + 1) * D]
    return block_part.reshape(lead_dims + (HEADS, D // HEADS))


def softmax_rows(queries, key_part, layout, key_layout):
    scores = jnp.einsum(
        layout + "hd," + key_layout + "hd->bzhqk",
        queries,
        key_part,
        preferred_element_type=jnp.float32,
    )
    scores = scores * (D // HEADS) ** (-0.5)
    highest = jnp.max(scores, -1, keepdims=True)
    exponent = jnp.exp(scores - highest)
    return exponent / jnp.sum(exponent, -1, keepdims=True)


def attend(qkv_proj, layout):
    key_layout = layout.replace("q", "k")
    queries, key_part, value_part = (
        heads_of(qkv_proj, 0),
        heads_of(qkv_proj, 1),
        heads_of(qkv_proj, 2),
    )
    probs_low = softmax_rows(queries, key_part, layout, key_layout).astype(jnp.bfloat16)
    result = jnp.einsum(
        "bzhqk," + key_layout + "hd->" + layout + "hd",
        probs_low,
        value_part,
        preferred_element_type=jnp.float32,
    )
    return result.reshape(qkv_proj.shape[:-1] + (D,)).astype(jnp.bfloat16)


def attend_back(qkv_proj, grad_out, layout):
    key_layout = layout.replace("q", "k")
    scale = (D // HEADS) ** (-0.5)
    queries, key_part, value_part = (
        heads_of(qkv_proj, 0),
        heads_of(qkv_proj, 1),
        heads_of(qkv_proj, 2),
    )
    probs = softmax_rows(queries, key_part, layout, key_layout)
    probs_low = probs.astype(jnp.bfloat16)
    grad_heads = heads_of(grad_out, 0)
    grad_probs = jnp.einsum(
        layout + "hd," + key_layout + "hd->bzhqk",
        grad_heads,
        value_part,
        preferred_element_type=jnp.float32,
    )
    grad_scores = probs * (grad_probs - jnp.sum(probs * grad_probs, -1, keepdims=True))
    grad_low = grad_scores.astype(jnp.bfloat16)
    grad_q = jnp.einsum(
        "bzhqk," + key_layout + "hd->" + layout + "hd",
        grad_low,
        key_part,
        preferred_element_type=jnp.float32,
    )
    grad_k = jnp.einsum(
        "bzhqk," + layout + "hd->" + key_layout + "hd",
        grad_low,
        queries,
        preferred_element_type=jnp.float32,
    )
    grad_v = jnp.einsum(
        "bzhqk," + layout + "hd->" + key_layout + "hd",
        probs_low,
        grad_heads,
        preferred_element_type=jnp.float32,
    )
    lead_dims = qkv_proj.shape[:-1] + (D,)
    return jnp.concatenate(
        [
            (grad_q * scale).astype(jnp.bfloat16).reshape(lead_dims),
            (grad_k * scale).astype(jnp.bfloat16).reshape(lead_dims),
            grad_v.astype(jnp.bfloat16).reshape(lead_dims),
        ],
        -1,
    )


def sublayer_local(stream, norm_gain, w_qkv, w_out, layout):
    stream_f = stream.astype(jnp.float32)
    normed = layer_norm(stream_f, norm_gain).astype(jnp.bfloat16)
    qkv_proj = project(normed, w_qkv).astype(jnp.bfloat16)
    mixed_out = attend(qkv_proj, layout)
    updated = to_low(stream_f + project(mixed_out, w_out))
    return (updated, qkv_proj)


def sublayer_back_local(stream, gradient, qkv_proj, norm_gain, w_qkv, w_out, layout):
    grad_mixed = project_back(gradient, w_out).astype(jnp.bfloat16)
    grad_qkv = attend_back(qkv_proj, grad_mixed, layout)
    grad_normed = project_back(grad_qkv, w_qkv)
    return to_low(
        gradient.astype(jnp.float32) + norm_back(stream.astype(jnp.float32), norm_gain, grad_normed)
    )


def mlp_back(stream, cotangent, gain_mlp, w_up, w_down):
    stream_f = stream.astype(jnp.float32)
    normed = layer_norm(stream_f, gain_mlp).astype(jnp.bfloat16)
    pre_act = project(normed, w_up)
    grad_act = project_back(cotangent, w_down).astype(jnp.bfloat16)
    _, pullback = jax.vjp(partial(jax.nn.gelu, approximate=True), pre_act)
    grad_pre = pullback(grad_act.astype(jnp.float32))[0].astype(jnp.bfloat16)
    return to_low(
        cotangent.astype(jnp.float32) + norm_back(stream_f, gain_mlp, project_back(grad_pre, w_up))
    )


def body_on_lines(
    tokens, cotangent, gain_x, w_qkv_x, w_out_x, gain_y, w_qkv_y, w_out_y, gain_mlp, w_up, w_down
):
    cot_y = lax.all_to_all(cotangent, "gy", split_axis=0, concat_axis=1, tiled=True)
    tokens_x = lax.all_to_all(tokens, "gx", split_axis=1, concat_axis=0, tiled=True)
    stream_1x, qkv_x = sublayer_local(tokens_x, gain_x, w_qkv_x, w_out_x, "qbz")
    stream_1y = lax.all_to_all(
        lax.all_to_all(stream_1x, "gx", split_axis=0, concat_axis=1, tiled=True),
        "gy",
        split_axis=0,
        concat_axis=1,
        tiled=True,
    )
    stream_2y, qkv_y = sublayer_local(stream_1y, gain_y, w_qkv_y, w_out_y, "bqz")
    grad_2 = mlp_back(stream_2y, cot_y, gain_mlp, w_up, w_down)
    grad_1y = sublayer_back_local(stream_1y, grad_2, qkv_y, gain_y, w_qkv_y, w_out_y, "bqz")
    grad_1x = lax.all_to_all(
        lax.all_to_all(grad_1y, "gy", split_axis=1, concat_axis=0, tiled=True),
        "gx",
        split_axis=1,
        concat_axis=0,
        tiled=True,
    )
    grad_tx = sublayer_back_local(tokens_x, grad_1x, qkv_x, gain_x, w_qkv_x, w_out_x, "qbz")
    return lax.all_to_all(grad_tx, "gx", split_axis=0, concat_axis=1, tiled=True)


def local(
    tokens, cotangent, gain_x, w_qkv_x, w_out_x, gain_y, w_qkv_y, w_out_y, gain_mlp, w_up, w_down
):
    return body_on_lines(
        tokens,
        cotangent,
        gain_x,
        w_qkv_x,
        w_out_x,
        gain_y,
        w_qkv_y,
        w_out_y,
        gain_mlp,
        w_up,
        w_down,
    )


def solution(mesh):
    in_specs = (
        P("gx", "gy", None, None),
        P("gx", "gy", None, None),
        P(),
        P(),
        P(),
        P(),
        P(),
        P(),
        P(),
        P(),
        P(),
    )
    out_specs = P("gx", "gy", None, None)
    return jax.shard_map(local, mesh=mesh, in_specs=in_specs, out_specs=out_specs, check_vma=False)
```

profile of v0, /device:TPU:0, one launch (start us, length us, event | category | flops | bytes accessed | tf_op | source)
XLA Modules:
  0.0 203.7 jit_solution(5757763057011695554)
XLA Ops:
  0.0 1.7 copy.134
  1.7 21.6 %all_to_all.108 = bf16[16,16,2,512]{3,2,0,1:T(2,128)(2,1)S(1)} all-to-all(bf16[16,16,2,512]{3,2,0,1:T(2,128)(2,1)S(1)} %copy.134), channel_id=1, replica_groups=mesh['gx'=8,'gy'=4] {'gx'}, dimensions={1} | all-to-all | bytes 1048576 | tf_op jit(solution)/shard_map/all_to_all | solution.py:162
  23.3 0.8 copy-done.6
  25.3 1.3 copy.135
  26.9 1.0 convolution_convert_fusion.1
  27.9 1.2 fusion.116
  29.0 2.0 %copy.137 = bf16[128,2,2,512]{0,3,2,1:T(8,128)(2,1)} copy(bf16[128,2,2,512]{3,0,2,1:T(8,128)(2,1)} %get-tuple-element.9) | data formatting | bytes 1048576 | tf_op jit(solution)/shard_map/slice | solution.py:46
  31.1 2.1 %copy.138 = bf16[128,2,2,512]{0,3,2,1:T(8,128)(2,1)} copy(bf16[128,2,2,512]{3,0,2,1:T(8,128)(2,1)} %get-tuple-element.8) | data formatting | bytes 1048576 | tf_op jit(solution)/shard_map/slice | solution.py:46
  33.1 2.0 %copy.136 = bf16[128,2,2,512]{0,3,2,1:T(8,128)(2,1)} copy(bf16[128,2,2,512]{3,0,2,1:T(8,128)(2,1)} %get-tuple-element.10) | data formatting | bytes 1048576 | tf_op jit(solution)/shard_map/slice | solution.py:46
  35.2 3.4 %fusion.118 = (f32[2,2,8,128]{3,2,1,0:T(8,128)S(1)}, f32[2,2,8,128,128]{3,4,2,1,0:T(8,128)}) fusion(bf16[128,2,2,8,64]{0,4,3,2,1:T(8,128)(2,1)} %bitcast.212, bf16[128,2,2,8,64]{0,4,3,2,1:T(8,128)(2,1)} %bitcast.214), kind=kOutput, calls=%fused_computation.151 | convolution fusion | flops 68681856 | bytes 3162112 | tf_op jit(solution)/shard_map/sub | solution.py:59
  38.6 2.2 %convolution_convert_fusion.8 = bf16[2,2,8,64,128]{4,3,2,1,0:T(8,128)(2,1)S(1)} fusion(bf16[128,2,2,8,64]{0,4,3,2,1:T(8,128)(2,1)} %bitcast.223, f32[2,2,8,128,128]{3,4,2,1,0:T(8,128)} %get-tuple-element.14, f32[2,2,8,128]{3,2,1,0:T(8,128)S(1)} %get-tuple-element.13), kind=kOutput, calls=%fused_computation.78 | convolution fusion | flops 68419584 | bytes 3162112 | tf_op jit(solution)/shard_map/bzhqk,kbzhd->qbzhd/dot_general | solution.py:71
  41.3 0.5 copy.141
  41.8 17.6 %all_to_all.109 = bf16[128,2,2,512]{3,2,1,0:T(2,128)(2,1)} all-to-all(bf16[128,2,2,512]{3,2,1,0:T(2,128)(2,1)S(1)} %copy.141), channel_id=1, replica_groups=mesh['gx'=8,'gy'=4] {'gx'}, dimensions={0} | all-to-all | bytes 1048576 | tf_op jit(solution)/shard_map/all_to_all | solution.py:165
  59.5 4.1 %all-to-all-start = ((bf16[16,16,2,512]{3,2,1,0:T(2,128)(2,1)}), bf16[16,16,2,512]{3,2,1,0:T(2,128)(2,1)}, u32[]{:S(2)}, u32[]{:S(2)}) async-start(bf16[16,16,2,512]{3,2,1,0:T(2,128)(2,1)} %param.12), calls=%async_computation | async-start | bytes 1048576 | tf_op jit(solution)/shard_map/all_to_all | solution.py:161
  63.6 1.1 copy.142
  64.8 1.4 copy.144
  66.2 6.4 %all-to-all-done = bf16[16,16,2,512]{3,2,1,0:T(2,128)(2,1)} async-done(((bf16[16,16,2,512]{3,2,1,0:T(2,128)(2,1)}), bf16[16,16,2,512]{3,2,1,0:T(2,128)(2,1)}, u32[]{:S(2)}, u32[]{:S(2)}) %all-to-all-start) | async-done | bytes 524320 | tf_op jit(solution)/shard_map/all_to_all | solution.py:161
  72.5 4.1 %all-to-all-start.3 = ((bf16[16,16,2,512]{3,2,1,0:T(2,128)(2,1)}), bf16[16,16,2,512]{3,2,1,0:T(2,128)(2,1)}, u32[]{:S(2)}, u32[]{:S(2)}) async-start(bf16[16,16,2,512]{3,2,1,0:T(2,128)(2,1)} %copy.144), calls=%async_computation.3 | async-start | bytes 1048576 | tf_op jit(solution)/shard_map/all_to_all | solution.py:164
  76.7 1.1 copy.133
  77.8 0.8 copy-done.18
  78.6 2.6 %convolution_convert_fusion.2 = bf16[4,64,2,2048]{3,1,2,0:T(8,128)(2,1)} fusion(bf16[4,64,2,512]{3,1,2,0:T(8,128)(2,1)S(1)} %bitcast.205, bf16[2048,512]{1,0:T(8,128)(2,1)S(1)} %copy-done), kind=kOutput, calls=%fused_computation.18 | convolution fusion | flops 1074790400 | bytes 4718592 | tf_op jit(solution)/shard_map/dot_general | solution.py:38
  81.2 4.3 %all-to-all-done.3 = bf16[16,16,2,512]{3,2,1,0:T(2,128)(2,1)} async-done(((bf16[16,16,2,512]{3,2,1,0:T(2,128)(2,1)}), bf16[16,16,2,512]{3,2,1,0:T(2,128)(2,1)}, u32[]{:S(2)}, u32[]{:S(2)}) %all-to-all-start.3) | async-done | bytes 524320 | tf_op jit(solution)/shard_map/all_to_all | solution.py:164
  85.6 1.2 fusion.117
  87.8 1.2 copy-done.29
  89.0 1.1 convolution_convert_fusion
  90.0 1.2 fusion.115
  91.2 1.5 copy.200
  92.7 2.8 %copy.201 = bf16[4,64,2,512]{1,3,2,0:T(8,128)(2,1)} copy(bf16[4,64,2,512]{3,1,2,0:T(8,128)(2,1)} %get-tuple-element.5) | data formatting | bytes 1048576 | tf_op jit(solution)/shard_map/reshape | solution.py:47
  95.5 2.4 %reshape.278 = bf16[4,64,2,8,64]{4,3,1,2,0:T(8,128)(2,1)} reshape(bf16[4,64,2,512]{3,1,2,0:T(8,128)(2,1)} %get-tuple-element.7) | data formatting | bytes 1048576 | tf_op jit(solution)/shard_map/reshape | solution.py:47
  97.9 3.5 %fusion.119 = (f32[4,2,8,64]{3,2,1,0:T(8,128)S(1)}, f32[4,2,8,64,64]{3,4,2,1,0:T(8,128)}) fusion(bf16[4,64,2,8,64]{1,4,3,2,0:T(8,128)(2,1)S(1)} %bitcast.197, bf16[4,64,2,8,64]{1,4,3,2,0:T(8,128)(2,1)} %bitcast.199), kind=kOutput, calls=%fused_computation.152 | convolution fusion | flops 34340928 | bytes 2113536 | tf_op jit(solution)/shard_map/sub | solution.py:59
  101.4 2.5 %convolution_convert_fusion.4 = bf16[4,2,8,64,64]{4,3,2,1,0:T(8,128)(2,1)S(1)} fusion(bf16[4,64,2,8,64]{4,3,1,2,0:T(8,128)(2,1)} %reshape.278, f32[4,2,8,64,64]{3,4,2,1,0:T(8,128)} %get-tuple-element.16, f32[4,2,8,64]{3,2,1,0:T(8,128)S(1)} %get-tuple-element.15), kind=kOutput, calls=%fused_computation.56 | convolution fusion | flops 34340864 | bytes 2113536 | tf_op jit(solution)/shard_map/bzhqk,bkzhd->bqzhd/dot_general | solution.py:71
  104.9 7.9 %fusion.70 = (f32[4,64,2]{1,2,0:T(2,128)S(1)}, f32[4,64,2,512]{3,1,2,0:T(8,128)}) fusion(bf16[4,64,2,512]{3,1,2,0:T(8,128)(2,1)S(1)} %fusion.63, f32[4,64,2]{1,2,0:T(2,128)S(1)} %broadcast_multiply_fusion.2, f32[512]{0:T(512)S(1)} %copy-done.31, bf16[512,2048]{1,0:T(8,128)(2,1)} %param.20, bf16[4,64,2,2048]{3,1,2,0:T(8,128)(2,1)} %convolution_convert_fusion.2, ...), kind=kOutput, calls=%fused_computation.83 | convolution fusion | flops 2172124672 | bytes 5775360 | tf_op jit(solution)/shard_map/dot_general | solution.py:38
  112.8 1.8 fusion.97
  114.6 1.5 add_convert_fusion.2
  116.5 1.3 copy.202
  117.9 3.0 %multiply_reduce_fusion.1 = (f32[4,2,8,64]{3,2,1,0:T(8,128)S(1)}, f32[4,2,8,64,64]{3,4,2,1,0:T(8,128)S(1)}) fusion(f32[4,2,8,64,64]{3,4,2,1,0:T(8,128)} %get-tuple-element.16, f32[4,2,8,64]{3,2,1,0:T(8,128)S(1)} %get-tuple-element.15, bf16[4,64,2,8,64]{1,4,3,2,0:T(8,128)(2,1)} %bitcast.219, bf16[4,64,2,8,64]{4,3,1,2,0:T(8,128)(2,1)} %reshape.278), kind=kOutput, calls=%fused_computation.29 | convolution fusion | flops 34336768 | bytes 3178496 | tf_op jit(solution)/shard_map/bqzhd,bkzhd->bzhqk/dot_general | solution.py:91
  120.9 0.7 multiply_convert_fusion.3
  121.6 0.5 copy-done.4
  122.1 0.7 fusion.40
  122.8 0.5 copy-done.3
  123.3 1.7 fusion.41
  125.0 1.7 convolution_convert_fusion.3
  126.7 1.7 copy.159
  128.4 2.5 %concatenate.22 = bf16[4,64,2,512]{3,1,2,0:T(8,128)(2,1)} reshape(bf16[4,64,2,8,64]{4,3,1,2,0:T(8,128)(2,1)} %copy.159) | data formatting | bytes 1048576 | tf_op jit(solution)/shard_map/concatenate | solution.py:118
  130.9 1.7 copy.163
  132.6 2.6 %concatenate.23 = bf16[4,64,2,512]{3,1,2,0:T(8,128)(2,1)} reshape(bf16[4,64,2,8,64]{4,3,1,2,0:T(8,128)(2,1)} %copy.163) | data formatting | bytes 1048576 | tf_op jit(solution)/shard_map/concatenate | solution.py:118
  135.3 2.3 %copy.166 = bf16[4,64,2,512]{3,1,2,0:T(8,128)(2,1)} copy(bf16[4,64,2,512]{1,3,2,0:T(8,128)(2,1)} %bitcast.221) | data formatting | bytes 1048576 | tf_op jit(solution)/shard_map/concatenate | solution.py:118
  137.6 3.1 %multiply_reduce_fusion.5 = (f32[4,64,2]{1,2,0:T(2,128)S(1)}, f32[4,64,2,512]{3,1,2,0:T(8,128)S(1)}) fusion(f32[4,64,2,512]{3,1,2,0:T(8,128)S(1)} %copy-done.13, f32[512]{0:T(512)S(1)} %copy-done.32, bf16[512,1536]{1,0:T(8,128)(2,1)} %param.17, bf16[4,64,2,512]{3,1,2,0:T(8,128)(2,1)} %copy.166, bf16[4,64,2,512]{3,1,2,0:T(8,128)(2,1)} %concatenate.23, ...), kind=kOutput, calls=%fused_computation.94 | convolution fusion | flops 810810880 | bytes 5246976 | tf_op jit(solution)/shard_map/dot_general | solution.py:38
  141.1 0.6 copy-done.8
  142.1 0.5 copy.167
  142.7 11.2 %all_to_all.110 = bf16[4,64,2,512]{3,2,0,1:T(2,128)(2,1)S(1)} all-to-all(bf16[4,64,2,512]{3,2,0,1:T(2,128)(2,1)S(1)} %copy.167), channel_id=1, replica_groups=mesh['gx'=8,'gy'=4] {'gy'}, dimensions={1} | all-to-all | bytes 1048576 | tf_op jit(solution)/shard_map/all_to_all | solution.py:175
  154.1 0.5 copy.170
  154.7 17.6 %all_to_all.111 = bf16[16,16,2,512]{3,2,0,1:T(2,128)(2,1)S(1)} all-to-all(bf16[16,16,2,512]{3,2,0,1:T(2,128)(2,1)S(1)} %copy.170), channel_id=1, replica_groups=mesh['gx'=8,'gy'=4] {'gx'}, dimensions={1} | all-to-all | bytes 1048576 | tf_op jit(solution)/shard_map/all_to_all | solution.py:174
  172.4 0.5 convolution_convert_fusion.5
  173.2 2.5 %multiply_reduce_fusion = (f32[2,2,8,128]{3,2,1,0:T(8,128)S(1)}, f32[2,2,8,128,128]{3,4,2,1,0:T(8,128)S(1)}) fusion(f32[2,2,8,128,128]{3,4,2,1,0:T(8,128)} %get-tuple-element.14, f32[2,2,8,128]{3,2,1,0:T(8,128)S(1)} %get-tuple-element.13, bf16[128,2,2,8,64]{0,4,3,2,1:T(8,128)(2,1)S(1)} %bitcast.225, bf16[128,2,2,8,64]{0,4,3,2,1:T(8,128)(2,1)} %bitcast.224), kind=kOutput, calls=%fused_computation.25 | convolution fusion | flops 68677632 | bytes 5275648 | tf_op jit(solution)/shard_map/qbzhd,kbzhd->bzhqk/dot_general | solution.py:91
  175.7 0.6 multiply_convert_fusion
  176.8 1.2 fusion.64
  178.0 0.8 fusion.65
  178.8 0.8 convolution_convert_fusion.7
  180.5 2.5 %multiply_reduce_fusion.4 = (f32[128,2,2]{0,2,1:T(2,128)S(1)}, f32[128,2,2,512]{3,0,2,1:T(8,128)S(1)}) fusion(f32[16,8,2,2,512]{4,0,1,3,2:T(8,128)S(1)} %copy.135, f32[128,2,2]{0,2,1:T(2,128)S(1)} %div.89, f32[512]{0:T(512)S(1)} %copy-done.28, bf16[512,1536]{1,0:T(8,128)(2,1)} %param.14, bf16[128,2,2,512]{3,0,2,1:T(8,128)(2,1)S(1)} %copy.179, ...), kind=kOutput, calls=%fused_computation.92 | convolution fusion | flops 811073024 | bytes 5249024 | tf_op jit(solution)/shard_map/dot_general | solution.py:38
  183.4 0.6 copy-done.10
  184.5 0.5 copy.180
  185.0 17.4 %all_to_all.112 = bf16[128,2,2,512]{3,2,1,0:T(2,128)(2,1)S(1)} all-to-all(bf16[128,2,2,512]{3,2,1,0:T(2,128)(2,1)S(1)} %copy.180), channel_id=1, replica_groups=mesh['gx'=8,'gy'=4] {'gx'}, dimensions={0} | all-to-all | bytes 1048576 | tf_op jit(solution)/shard_map/all_to_all | solution.py:182
  202.4 1.3 copy.181
  (105 shorter events, 7.9 us)
Async XLA Ops:
  0.0 78.6 %copy-start = (bf16[2048,512]{1,0:T(8,128)(2,1)S(1)}, bf16[2048,512]{1,0:T(8,128)(2,1)}, u32[]{:S(2)}) copy-start(bf16[2048,512]{1,0:T(8,128)(2,1)} %param.21) | copy-start | bytes 6291460
  23.3 0.8 copy-start.6
  24.5 2.1 %copy-start.28 = (f32[512]{0:T(512)S(1)}, f32[512]{0:T(512)}, u32[]{:S(2)}) copy-start(f32[512]{0:T(512)} %param.13) | copy-start | bytes 6148
  25.3 1.6 copy-start.30
  38.6 2.2 %copy-start.16 = (bf16[512,512]{1,0:T(8,128)(2,1)S(1)}, bf16[512,512]{1,0:T(8,128)(2,1)}, u32[]{:S(2)}) copy-start(bf16[512,512]{1,0:T(8,128)(2,1)} %param.15) | copy-start | bytes 1572868
  59.5 13.1 %all-to-all-start = ((bf16[16,16,2,512]{3,2,1,0:T(2,128)(2,1)}), bf16[16,16,2,512]{3,2,1,0:T(2,128)(2,1)}, u32[]{:S(2)}, u32[]{:S(2)}) async-start(bf16[16,16,2,512]{3,2,1,0:T(2,128)(2,1)} %param.12), calls=%async_computation | async-start | bytes 1048576 | tf_op jit(solution)/shard_map/all_to_all | solution.py:161
  72.5 13.0 %all-to-all-start.3 = ((bf16[16,16,2,512]{3,2,1,0:T(2,128)(2,1)}), bf16[16,16,2,512]{3,2,1,0:T(2,128)(2,1)}, u32[]{:S(2)}, u32[]{:S(2)}) async-start(bf16[16,16,2,512]{3,2,1,0:T(2,128)(2,1)} %copy.144), calls=%async_computation.3 | async-start | bytes 1048576 | tf_op jit(solution)/shard_map/all_to_all | solution.py:164
  77.8 0.8 copy-start.18
  87.5 1.4 copy-start.29
  87.5 1.4 copy-start.32
  89.0 1.1 copy-start.12
  92.7 8.7 %copy-start.2 = (bf16[4,64,2,512]{1,3,2,0:T(8,128)(2,1)}, bf16[4,64,2,512]{1,3,2,0:T(8,128)(2,1)S(1)}, u32[]{:S(2)}) copy-start(bf16[4,64,2,512]{1,3,2,0:T(8,128)(2,1)S(1)} %copy.200) | copy-start | bytes 1572868
  101.4 2.5 %copy-start.20 = (bf16[512,512]{1,0:T(8,128)(2,1)S(1)}, bf16[512,512]{1,0:T(8,128)(2,1)}, u32[]{:S(2)}) copy-start(bf16[512,512]{1,0:T(8,128)(2,1)} %param.18) | copy-start | bytes 1572868
  103.9 1.0 copy-start.31
  112.8 1.8 copy-start.15
  112.8 3.3 %copy-start.21 = (bf16[512,512]{1,0:T(8,128)(2,1)S(1)}, bf16[512,512]{1,0:T(8,128)(2,1)}, u32[]{:S(2)}) copy-start(bf16[512,512]{1,0:T(8,128)(2,1)} %param.18) | copy-start | bytes 1572868
  116.1 4.8 %copy-start.7 = (bf16[4,64,2,512]{3,1,2,0:T(8,128)(2,1)}, bf16[4,64,2,512]{3,1,2,0:T(8,128)(2,1)S(1)}, u32[]{:S(2)}) copy-start(bf16[4,64,2,512]{3,1,2,0:T(8,128)(2,1)S(1)} %add_convert_fusion.2) | copy-start | bytes 1572868
  117.9 3.0 %copy-start.5 = (f32[4,2,8,64,64]{3,4,2,1,0:T(8,128)S(1)}, f32[4,2,8,64,64]{3,4,2,1,0:T(8,128)}, u32[]{:S(2)}) copy-start(f32[4,2,8,64,64]{3,4,2,1,0:T(8,128)} %get-tuple-element.16) | copy-start | bytes 3145732
  120.9 1.2 copy-start.4
  122.1 1.2 copy-start.3
  123.3 1.7 copy-start.25
  126.7 4.2 %copy-start.11 = (bf16[4,64,2,8,64]{4,1,3,2,0:T(8,128)(2,1)S(1)}, bf16[4,64,2,8,64]{4,1,3,2,0:T(8,128)(2,1)}, u32[]{:S(2)}) copy-start(bf16[4,64,2,8,64]{4,1,3,2,0:T(8,128)(2,1)} %fusion.41) | copy-start | bytes 1572868
  132.6 5.0 %copy-start.13 = (f32[4,64,2,512]{3,1,2,0:T(8,128)S(1)}, f32[4,64,2,512]{3,1,2,0:T(8,128)}, u32[]{:S(2)}) copy-start(f32[4,64,2,512]{3,1,2,0:T(8,128)} %copy-done.12) | copy-start | bytes 3145732
  137.6 3.1 %copy-start.14 = (f32[4,64,2,512]{3,1,2,0:T(8,128)S(1)}, f32[4,64,2,512]{3,1,2,0:T(8,128)}, u32[]{:S(2)}) copy-start(f32[4,64,2,512]{3,1,2,0:T(8,128)} %copy-done.12) | copy-start | bytes 3145732
  140.7 1.0 copy-start.8
  154.1 18.3 %copy-start.17 = (bf16[512,512]{1,0:T(8,128)(2,1)S(1)}, bf16[512,512]{1,0:T(8,128)(2,1)}, u32[]{:S(2)}) copy-start(bf16[512,512]{1,0:T(8,128)(2,1)} %param.15) | copy-start | bytes 1572868
  172.4 3.3 %copy-start.9 = (bf16[8,16,2,2,512]{4,1,0,3,2:T(8,128)(2,1)}, bf16[8,16,2,2,512]{4,1,0,3,2:T(8,128)(2,1)S(1)}, u32[]{:S(2)}) copy-start(bf16[8,16,2,2,512]{4,1,0,3,2:T(8,128)(2,1)S(1)} %copy.172) | copy-start | bytes 1572868
  173.1 2.6 %copy-start.26 = (bf16[128,2,2,512]{0,3,2,1:T(8,128)(2,1)}, bf16[128,2,2,512]{0,3,2,1:T(8,128)(2,1)S(1)}, u32[]{:S(2)}) copy-start(bf16[128,2,2,512]{0,3,2,1:T(8,128)(2,1)S(1)} %copy.173) | copy-start | bytes 1572868
  173.1 2.6 %copy-start.19 = (f32[2,2,8,128,128]{3,4,2,1,0:T(8,128)S(1)}, f32[2,2,8,128,128]{3,4,2,1,0:T(8,128)}, u32[]{:S(2)}) copy-start(f32[2,2,8,128,128]{3,4,2,1,0:T(8,128)} %get-tuple-element.14) | copy-start | bytes 6291460
  175.7 1.0 copy-start.23
  176.8 1.2 copy-start.22
  176.8 2.0 copy-start.27
  178.8 1.0 copy-start.24
  183.0 1.0 copy-start.10
  184.1 19.7 %copy-start.1 = (bf16[2048,512]{1,0:T(8,128)(2,1)S(1)}, bf16[2048,512]{1,0:T(8,128)(2,1)}, u32[]{:S(2)}) copy-start(bf16[2048,512]{1,0:T(8,128)(2,1)} %param.21) | copy-start | bytes 6291460
where the time goes:
time: 205 us; the launch traced here: 204 us
  blocking collectives  85.4 us (42%)
  local copies, waits for them, and re-layouts  45 us (22%)
  matrix products  44 us (21%)
  waiting for transfers between devices  10.7 us (5%)
  other arithmetic  9.68 us (5%)
  starting transfers between devices  8.28 us (4%)
    all_to_all x1, blocking collectives, body_on_lines(): lax.all_to_all(tokens, 'gx', split_axis=1, concat_axis=0, tiled=True)  21.6 us
    all_to_all x1, blocking collectives, body_on_lines(): lax.all_to_all(stream_1x, 'gx', split_axis=0, concat_axis=1, tiled=True)  17.6 us
    all_to_all x1, blocking collectives, body_on_lines(): lax.all_to_all(lax.all_to_all(grad_1y, 'gy', split_axis=1, concat_axis=0,...  17.6 us
    all_to_all x1, blocking collectives, body_on_lines(): lax.all_to_all(grad_tx, 'gx', split_axis=0, concat_axis=1, tiled=True)  17.4 us
    dot_general x6, matrix products, project_back(): lax.dot_general(flattened, weight, (((1,), (1,)), ((), ())), preferred_el...  17 us
    all_to_all x1, blocking collectives, body_on_lines(): lax.all_to_all(grad_1y, 'gy', split_axis=1, concat_axis=0, tiled=True)  11.2 us
    slice x5, local copies, waits for them, and re-layouts, heads_of(): block_part = tensor[..., which_part * D:(which_part + 1) * D]  8.48 us
    concatenate x6, local copies, waits for them, and re-layouts, attend_back(): jnp.concatenate([(grad_q * scale).astype(jnp.bfloat16).reshape(lead_dims)...  8.16 us
  transfers between devices with their start and end apart: 2, of which 2 were waited for; matrix products, arithmetic and copies ran while one was open for 3% of the time, Pallas kernels for 0%

commit v1 on v0

v1 whole, which is shorter than its diff:
```python
import jax
import jax.numpy as jnp
import numpy as np
from jax import lax
from jax.experimental import pallas as pl
from jax.experimental.pallas import tpu as pltpu
from jax.sharding import Mesh
from jax.sharding import PartitionSpec as P

HEADS = 8
NZ = 2
EPS = 1e-05
F32 = jnp.float32
BF16 = jnp.bfloat16
VMEM_LIMIT = 56 * 1024 * 1024


def dot(a, b):
    return jnp.dot(a, b, preferred_element_type=F32)


def dot_t(a, b):
    return lax.dot_general(a, b, (((1,), (1,)), ((), ())), preferred_element_type=F32)


def dot_lt(a, b):
    return lax.dot_general(a, b, (((0,), (0,)), ((), ())), preferred_element_type=F32)


def one_hot(target):
    size = target.shape[1]
    rows = lax.broadcasted_iota(jnp.int32, (size, size), 0)
    return jnp.where(rows == target, 1.0, 0.0).astype(BF16)


def standardize(x):
    centred = x - jnp.mean(x, -1, keepdims=True)
    inv = lax.rsqrt(jnp.mean(centred * centred, -1, keepdims=True) + EPS)
    return centred * inv, inv


def norm_back(x, gain, grad):
    unit, inv = standardize(x)
    scaled = grad * gain
    return inv * (
        scaled
        - jnp.mean(scaled, -1, keepdims=True)
        - unit * jnp.mean(scaled * unit, -1, keepdims=True)
    )


def group_of(length, dim):
    return 4 if length * 4 <= 256 and HEADS % 4 == 0 else 2


def spread(block, count):
    width = block.shape[1] // count
    lane = lax.broadcasted_iota(jnp.int32, block.shape, 1)
    zero = jnp.zeros_like(block)
    return jnp.concatenate(
        [
            jnp.where((lane >= i * width) & (lane < (i + 1) * width), block, zero)
            for i in range(count)
        ],
        0,
    )


def gather(block, count):
    rows = block.shape[0] // count
    width = block.shape[1] // count
    lane = lax.broadcasted_iota(jnp.int32, (rows, block.shape[1]), 1)
    result = block[:rows]
    for i in range(1, count):
        result = jnp.where(lane >= i * width, block[i * rows : (i + 1) * rows], result)
    return result


def probs_t(q_wide, k):
    scores = dot_t(k, q_wide)
    exponent = jnp.exp(scores - jnp.max(scores, 0, keepdims=True))
    return exponent * (1.0 / jnp.sum(exponent, 0, keepdims=True))


def attend_line(qkv, rows, dim, length, mixed, keep=None):
    count = group_of(length, dim)
    width = dim // HEADS * count
    scale = (dim // HEADS) ** -0.5
    for j in range(HEADS // count):
        q = qkv[rows, j * width : (j + 1) * width] * jnp.array(scale, BF16)
        k = qkv[rows, dim + j * width : dim + (j + 1) * width]
        v = qkv[rows, 2 * dim + j * width : 2 * dim + (j + 1) * width]
        probs = probs_t(spread(q, count), k)
        if keep is not None:
            keep(j, probs)
        out = dot_lt(probs.astype(BF16), v)
        mixed[rows, j * width : (j + 1) * width] = gather(out, count).astype(BF16)


def attend_back_line(qkv, rows, dim, length, grad, grad_qkv, kept=None):
    count = group_of(length, dim)
    width = dim // HEADS * count
    scale = (dim // HEADS) ** -0.5
    for j in range(HEADS // count):
        lanes = slice(j * width, (j + 1) * width)
        q = qkv[rows, lanes] * jnp.array(scale, BF16)
        k = qkv[rows, dim + j * width : dim + (j + 1) * width]
        v = qkv[rows, 2 * dim + j * width : 2 * dim + (j + 1) * width]
        q_wide = spread(q, count)
        g_wide = spread(grad[rows, lanes], count)
        probs = probs_t(q_wide, k) if kept is None else kept(j)
        g_probs = dot_t(v, g_wide)
        weighted = probs * g_probs
        g_scores = (weighted - probs * jnp.sum(weighted, 0, keepdims=True)).astype(BF16)
        g_q = gather(dot_lt(g_scores, k), count) * scale
        g_k = dot(g_scores, q_wide)
        g_v = dot(probs.astype(BF16), g_wide)
        grad_qkv[rows, lanes] = g_q.astype(BF16)
        grad_qkv[rows, dim + j * width : dim + (j + 1) * width] = g_k.astype(BF16)
        grad_qkv[rows, 2 * dim + j * width : 2 * dim + (j + 1) * width] = g_v.astype(BF16)


def line_rows(i, length):
    return pl.ds(pl.multiple_of(i * length, length), length)


def reorder_body(target, src, out):
    out[...] = dot(one_hot(target[...]), src[...]).astype(BF16)


def reorder(target, src):
    return pl.pallas_call(
        reorder_body,
        out_shape=jax.ShapeDtypeStruct(src.shape, BF16),
        compiler_params=pltpu.CompilerParams(vmem_limit_bytes=VMEM_LIMIT),
        name="reorder",
    )(target, src)


def x_forward_body(target, tok, gain, w_qkv, w_out, sent, qkv, normed, mixed):
    blocks, lines, part, dim = tok.shape
    length = blocks * part

    def norm_line(i, _):
        x = tok[:, i].reshape(length, dim).astype(F32)
        unit, _ = standardize(x)
        normed[line_rows(i, length), :] = (unit * gain[...]).astype(BF16)
        return 0

    lax.fori_loop(0, lines, norm_line, 0)
    for j in range(3):
        cols = slice(j * dim, (j + 1) * dim)
        qkv[:, cols] = dot(normed[...], w_qkv[:, cols]).astype(BF16)

    def attend(i, _):
        attend_line(qkv, line_rows(i, length), dim, length, mixed)
        return 0

    lax.fori_loop(0, lines, attend, 0)

    def project(i, _):
        rows = line_rows(i, length)
        x = tok[:, i].reshape(length, dim).astype(F32)
        normed[rows, :] = (x + dot(mixed[rows, :], w_out[...])).astype(BF16)
        return 0

    lax.fori_loop(0, lines, project, 0)
    sent[...] = dot(one_hot(target[...]), normed[...]).astype(BF16)


def middle_body(
    to_line, to_sent, s1_in, cot_in, gain_y, w_qkv, w_out, gain_m, w_up, w_down, sent,
    s1, cot, normed, qkv, mixed, s2, probs_kept, acc, grad, grad_qkv,
):
    blocks, lines, part, dim = cot_in.shape
    length = blocks * part
    hidden = w_up.shape[1]
    s1[...] = dot(one_hot(to_line[...]), s1_in[...]).astype(BF16)

    def norm_line(i, _):
        rows = line_rows(i, length)
        cot[rows, :] = cot_in[:, i].reshape(length, dim)
        unit, _ = standardize(s1[rows, :].astype(F32))
        normed[rows, :] = (unit * gain_y[...]).astype(BF16)
        return 0

    lax.fori_loop(0, lines, norm_line, 0)
    for j in range(3):
        cols = slice(j * dim, (j + 1) * dim)
        qkv[:, cols] = dot(normed[...], w_qkv[:, cols]).astype(BF16)

    def attend(i, _):
        def keep(j, probs):
            probs_kept[i, j] = probs

        attend_line(qkv, line_rows(i, length), dim, length, mixed, keep)
        return 0

    lax.fori_loop(0, lines, attend, 0)
    tile = 128
    tiles = s1.shape[0] // tile

    def project(i, _):
        rows = line_rows(i, tile)
        low = (s1[rows, :].astype(F32) + dot(mixed[rows, :], w_out[...])).astype(BF16)
        s2[rows, :] = low
        unit, _ = standardize(low.astype(F32))
        normed[rows, :] = (unit * gain_m[...]).astype(BF16)
        return 0

    lax.fori_loop(0, tiles, project, 0)

    chunk = 512 if hidden % 512 == 0 else hidden
    c0 = 0.7978845608028654
    c1 = 0.044715
    for c in range(hidden // chunk):
        cols = slice(c * chunk, (c + 1) * chunk)

        def mlp(i, _):
            rows = line_rows(i, tile)
            pre = dot(normed[rows, :], w_up[:, cols])
            g_act = dot_t(cot[rows, :], w_down[cols, :]).astype(BF16).astype(F32)
            square = pre * pre
            half = 0.5 * jnp.tanh(pre * (c0 + (c0 * c1) * square)) + 0.5
            slope = half + pre * (half - half * half) * (2 * c0 + (6 * c0 * c1) * square)
            g_pre = (g_act * slope).astype(BF16)
            part_sum = dot_t(g_pre, w_up[:, cols])
            acc[rows, :] = part_sum if c == 0 else acc[rows, :] + part_sum
            return 0

        lax.fori_loop(0, tiles, mlp, 0)

    def back_norm_mlp(i, _):
        rows = line_rows(i, tile)
        g2 = cot[rows, :].astype(F32) + norm_back(
            s2[rows, :].astype(F32), gain_m[...], acc[rows, :]
        )
        cot[rows, :] = g2.astype(BF16)
        grad[rows, :] = dot_t(cot[rows, :], w_out[...]).astype(BF16)
        return 0

    lax.fori_loop(0, tiles, back_norm_mlp, 0)

    def attend_back(i, _):
        attend_back_line(
            qkv, line_rows(i, length), dim, length, grad, grad_qkv, lambda j: probs_kept[i, j]
        )
        return 0

    lax.fori_loop(0, lines, attend_back, 0)

    def back_norm(i, _):
        rows = line_rows(i, tile)
        g_normed = dot_t(grad_qkv[rows, :], w_qkv[...])
        g1 = cot[rows, :].astype(F32) + norm_back(
            s1[rows, :].astype(F32), gain_y[...], g_normed
        )
        normed[rows, :] = g1.astype(BF16)
        return 0

    lax.fori_loop(0, tiles, back_norm, 0)
    sent[...] = dot(one_hot(to_sent[...]), normed[...]).astype(BF16)


def x_back_body(to_line, g1_in, tok, qkv, gain, w_qkv, w_out, sent, g1, grad, grad_qkv):
    blocks, lines, part, dim = tok.shape
    length = blocks * part
    g1[...] = dot(one_hot(to_line[...]), g1_in[...]).astype(BF16)
    grad[...] = dot_t(g1[...], w_out[...]).astype(BF16)

    def attend_back(i, _):
        attend_back_line(qkv, line_rows(i, length), dim, length, grad, grad_qkv)
        return 0

    lax.fori_loop(0, lines, attend_back, 0)

    def back_norm(i, _):
        rows = line_rows(i, length)
        x = tok[:, i].reshape(length, dim).astype(F32)
        g_normed = dot_t(grad_qkv[rows, :], w_qkv[...])
        total = g1[rows, :].astype(F32) + norm_back(x, gain[...], g_normed)
        sent[:, i] = total.astype(BF16).reshape(blocks, part, dim)
        return 0

    lax.fori_loop(0, lines, back_norm, 0)


def call(body, outs, scratch, name, flops, *args):
    return pl.pallas_call(
        body,
        out_shape=outs,
        scratch_shapes=scratch,
        compiler_params=pltpu.CompilerParams(vmem_limit_bytes=VMEM_LIMIT),
        cost_estimate=pl.CostEstimate(flops=flops, bytes_accessed=4000000, transcendentals=0),
        name=name,
    )(*args)


def inverse(order):
    result = np.empty_like(order)
    result[order] = np.arange(order.size, dtype=order.dtype)
    return result


def row(order):
    return np.asarray(order, np.int32).reshape(1, -1)


def make_local(halves, gh, gy):
    gx = halves * gh

    def local(
        tokens, cotangent, gain_x, w_qkv_x, w_out_x, gain_y, w_qkv_y, w_out_y, gain_mlp, w_up,
        w_down,
    ):
        tx, ty, tz, dim = tokens.shape
        count = tx * ty * tz
        y_lines = ty // gh
        x_lines = tz * tx // gy
        len_x, len_y = tx * gx, ty * gy
        mine = lax.axis_index("gz")

        tile_row = np.arange(count).reshape(tx, ty, tz)
        tok_order = tile_row.reshape(tx, gh, y_lines, tz).transpose(3, 1, 2, 0).reshape(-1)
        cot_orders = [
            tile_row.transpose(2, 0, 1)[[z, 1 - z]].reshape(-1) for z in range(halves)
        ]
        line_row = np.arange(count).reshape(y_lines, halves, gh, tx)
        out_orders = []
        for z in range(halves):
            own_first = line_row[:, [z, 1 - z]]
            cut = own_first.transpose(0, 2, 1, 3).reshape(y_lines, gh, gy, x_lines)
            out_orders.append(cut.transpose(2, 1, 0, 3).reshape(-1))
        y_order = np.arange(count).reshape(gy * gh * y_lines, x_lines).T.reshape(-1)

        def pick(options):
            return jnp.where(mine == 0, row(options[0]), row(options[1]))

        def vm(shape, dtype=BF16):
            return pltpu.VMEM(shape, dtype)

        flat = jax.ShapeDtypeStruct((count, dim), BF16)
        gain_x, gain_y, gain_mlp = (g.reshape(1, dim) for g in (gain_x, gain_y, gain_mlp))

        tok_sent = reorder(row(inverse(tok_order)), tokens.reshape(count, dim))
        tok_x = lax.all_to_all(
            tok_sent.reshape(gx, count // gx, dim), ("gz", "gh"), 0, 0, tiled=True
        ).reshape(gx, y_lines, tx, dim)

        cot_sent = reorder(pick([inverse(o) for o in cot_orders]), cotangent.reshape(count, dim))
        other = lax.ppermute(cot_sent[count // 2 :], "gz", [(0, 1), (1, 0)])
        cot_pair = jnp.concatenate([cot_sent[: count // 2], other], 0)
        cot_y = lax.all_to_all(
            cot_pair.reshape(gy, count // gy, dim), "gy", 0, 0, tiled=True
        ).reshape(gy, x_lines, ty, dim)

        sent, qkv_x = call(
            x_forward_body,
            (flat, jax.ShapeDtypeStruct((count, 3 * dim), BF16)),
            [vm((count, dim)), vm((count, dim))],
            "x_forward",
            3 * 10**9,
            pick([inverse(o) for o in out_orders]),
            tok_x, gain_x, w_qkv_x, w_out_x,
        )
        s1_y = lax.all_to_all(
            sent.reshape(gh * gy, count // (gh * gy), dim), ("gy", "gh"), 0, 0, tiled=True
        ).reshape(count, dim)

        group = group_of(len_y, dim)
        g1_sent = call(
            middle_body,
            flat,
            [
                vm((count, dim)),
                vm((count, dim)),
                vm((count, dim)),
                vm((count, 3 * dim)),
                vm((count, dim)),
                vm((count, dim)),
                vm((x_lines, HEADS // group, len_y, group * len_y), F32),
                vm((count, dim), F32),
                vm((count, dim)),
                vm((count, 3 * dim)),
            ],
            "middle",
            9 * 10**9,
            row(inverse(y_order)), row(y_order),
            s1_y, cot_y, gain_y, w_qkv_y, w_out_y, gain_mlp, w_up, w_down,
        )
        g1_x = lax.all_to_all(
            g1_sent.reshape(gh * gy, count // (gh * gy), dim), ("gy", "gh"), 0, 0, tiled=True
        ).reshape(count, dim)

        gt_sent = call(
            x_back_body,
            jax.ShapeDtypeStruct(tok_x.shape, BF16),
            [vm((count, dim)), vm((count, dim)), vm((count, 3 * dim))],
            "x_back",
            3 * 10**9,
            pick(out_orders),
            g1_x, tok_x, qkv_x, gain_x, w_qkv_x, w_out_x,
        )
        gt = lax.all_to_all(
            gt_sent.reshape(gx, count // gx, dim), ("gz", "gh"), 0, 0, tiled=True
        ).reshape(count, dim)
        return reorder(row(tok_order), gt).reshape(tx, ty, tz, dim)

    return local


def solution(mesh):
    gx, gy = mesh.shape["gx"], mesh.shape["gy"]
    halved = Mesh(mesh.devices.reshape(NZ, gx // NZ, gy), ("gz", "gh", "gy"))
    tile = P(("gz", "gh"), "gy", None, None)
    return jax.shard_map(
        make_local(NZ, gx // NZ, gy),
        mesh=halved,
        in_specs=(tile, tile) + (P(),) * 9,
        out_specs=tile,
        check_vma=False,
    )
```

time: 205 us -> 152 us (0.74)
  Pallas kernels: 0 us -> 64.7 us
  blocking collectives: 85.4 us -> 32.9 us
  matrix products: 44 us -> 0 us
  local copies, waits for them, and re-layouts: 45 us -> 7.04 us
  waiting for transfers between devices: 10.7 us -> 26.3 us
  starting transfers between devices: 8.28 us -> 17.3 us
  other arithmetic: 9.68 us -> 2.6 us
    pallas_call x0 -> x6, Pallas kernels: none -> 64.7 us  [the longest x3 57.8 us: call(): pl.pallas_call(body, out_shape=outs, scratch_shapes=scratch, compiler_par...]
    all_to_all x5 -> x2, blocking collectives: 85.4 us -> 32.9 us  [the longest x1 19.3 us: local(): lax.all_to_all(gt_sent.reshape(gx, count // gx, dim), ('gz', 'gh'), 0, 0,...]
    dot_general x20 -> x0, matrix products: 37.1 us -> none  [the longest x6 17 us: project_back(): lax.dot_general(flattened, weight, (((1,), (1,)), ((), ())), preferred_el...]
    ppermute x0 -> x1, waiting for transfers between devices: none -> 17.8 us  [local(): other = lax.ppermute(cot_sent[count // 2:], 'gz', [(0, 1), (1, 0)])]
    concatenate x6 -> x0, local copies, waits for them, and re-layouts: 8.16 us -> none  [attend_back(): jnp.concatenate([(grad_q * scale).astype(jnp.bfloat16).reshape(lead_dims)...]
    slice x5 -> x1, local copies, waits for them, and re-layouts: 8.48 us -> 1.09 us  [local(): cot_pair = jnp.concatenate([cot_sent[:count // 2], other], 0)]
    sub x2 -> x0, matrix products: 6.91 us -> none  [softmax_rows(): exponent = jnp.exp(scores - highest)]
    unnamed x67 -> x20, local copies, waits for them, and re-layouts: 7.47 us -> 0.84 us
  transfers between devices with their start and end apart: 2 -> 4, of which waited for: 2 -> 2; matrix products, arithmetic and copies ran while one was open for 3% -> 3% of each run, Pallas kernels for 0% -> 7%
where the time goes in v1:
time: 152 us; the launch traced here: 151 us
  Pallas kernels  64.7 us (43%)
  blocking collectives  32.9 us (22%)
  waiting for transfers between devices  26.3 us (17%)
  starting transfers between devices  17.3 us (11%)
  local copies, waits for them, and re-layouts  7.04 us (5%)
  other arithmetic  2.6 us (2%)
    pallas_call x3, Pallas kernels, call(): pl.pallas_call(body, out_shape=outs, scratch_shapes=scratch, compiler_par...  57.8 us
    all_to_all x1, blocking collectives, local(): lax.all_to_all(gt_sent.reshape(gx, count // gx, dim), ('gz', 'gh'), 0, 0,...  19.3 us
    ppermute x1, waiting for transfers between devices, local(): other = lax.ppermute(cot_sent[count // 2:], 'gz', [(0, 1), (1, 0)])  17.8 us
    all_to_all x1, blocking collectives, local(): lax.all_to_all(sent.reshape(gh * gy, count // (gh * gy), dim), ('gy', 'gh...  13.7 us
    all_to_all x1, waiting for transfers between devices, local(): lax.all_to_all(g1_sent.reshape(gh * gy, count // (gh * gy), dim), ('gy',...  8.59 us
    all_to_all x1, starting transfers between devices, local(): lax.all_to_all(tok_sent.reshape(gx, count // gx, dim), ('gz', 'gh'), 0, 0...  7.25 us
    pallas_call x3, Pallas kernels, reorder(): pl.pallas_call(reorder_body, out_shape=jax.ShapeDtypeStruct(src.shape, BF...  6.91 us
    all_to_all x1, starting transfers between devices, local(): lax.all_to_all(g1_sent.reshape(gh * gy, count // (gh * gy), dim), ('gy',...  3.57 us
  transfers between devices with their start and end apart: 4, of which 2 were waited for; matrix products, arithmetic and copies ran while one was open for 3% of the time, Pallas kernels for 7%

profile of v1, /device:TPU:0, one launch (start us, length us, event | category | flops | bytes accessed | tf_op | source)
XLA Modules:
  0.0 151.0 jit_solution(7130030534033806164)
XLA Ops:
  0.0 0.0 copy-start
  0.0 2.1 %reshape.48.src = bf16[512,512]{1,0:T(8,128)(2,1)} reshape(bf16[16,16,2,512]{3,2,1,0:T(2,128)(2,1)} %param.21) | data formatting | bytes 1048576 | tf_op jit(solution)/shard_map/reshape | solution.py:345
  2.1 0.0 copy-start.8
  2.1 0.0 copy-start.9
  2.1 2.3 %reorder.3 = bf16[512,512]{1,0:T(8,128)(2,1)} custom-call(s32[1,512]{1,0:T(1,128)} %constant.28.clone.target, bf16[512,512]{1,0:T(8,128)(2,1)} %reshape.48.src), custom_call_target="tpu_custom_call" | custom-call | tf_op jit(solution)/shard_map/reorder/pallas_call | solution.py:132
  4.4 7.3 %all-to-all-start = ((bf16[8,64,512]{2,1,0:T(8,128)(2,1)}), bf16[8,64,512]{2,1,0:T(8,128)(2,1)S(1)}, u32[]{:S(2)}, u32[]{:S(2)}) async-start(bf16[8,64,512]{2,1,0:T(8,128)(2,1)} %bitcast.13), calls=%async_computation | async-start | bytes 1048576 | tf_op jit(solution)/shard_map/all_to_all | solution.py:346
  11.7 0.0 copy-done
  11.7 1.0 reshape.54.src
  12.7 0.0 copy-done.8
  12.7 0.0 copy-done.9
  12.7 0.6 broadcast_select_fusion.target
  13.3 2.3 %reorder.4 = bf16[512,512]{1,0:T(8,128)(2,1)} custom-call(s32[1,512]{1,0:T(1,128)} %broadcast_select_fusion.target, bf16[512,512]{1,0:T(8,128)(2,1)} %reshape.54.src), custom_call_target="tpu_custom_call" | custom-call | tf_op jit(solution)/shard_map/reorder/pallas_call | solution.py:132
  15.6 0.0 copy-start.6
  15.6 0.0 copy-start.7
  15.6 1.1 fusion
  16.7 3.0 %collective-permute-start = (bf16[256,512]{1,0:T(8,128)(2,1)S(1)}, bf16[256,512]{1,0:T(8,128)(2,1)S(1)}, u32[]{:S(2)}, u32[]{:S(2)}) collective-permute-start(bf16[256,512]{1,0:T(8,128)(2,1)S(1)} %get-tuple-element.10), channel_id=1, source_target_pairs={{0,16},{16,0},{1,17},{17,1},{2,18},{18,2},{3,19},{19,3},{4,20},{20... | collective-permute-start | bytes 786440 | tf_op jit(solution)/shard_map/ppermute | solution.py:351
  19.6 17.8 %collective-permute-done = bf16[256,512]{1,0:T(8,128)(2,1)S(1)} collective-permute-done((bf16[256,512]{1,0:T(8,128)(2,1)S(1)}, bf16[256,512]{1,0:T(8,128)(2,1)S(1)}, u32[]{:S(2)}, u32[]{:S(2)}) %collective-permute-start) | collective-permute-done | bytes 262176 | tf_op jit(solution)/shard_map/ppermute | solution.py:351
  37.4 0.8 pad_maximum_fusion
  38.2 0.0 all-to-all-done
  38.2 0.0 copy-start.1
  38.2 3.5 %all-to-all-start.2 = ((bf16[4,128,512]{2,1,0:T(8,128)(2,1)}), bf16[4,128,512]{2,1,0:T(8,128)(2,1)S(1)}, u32[]{:S(2)}, u32[]{:S(2)}) async-start(bf16[4,128,512]{2,1,0:T(8,128)(2,1)} %bitcast.5), calls=%async_computation.2 | async-start | bytes 1048576 | tf_op jit(solution)/shard_map/all_to_all | solution.py:353
  41.7 0.0 copy-done.6
  41.7 0.0 copy-done.7
  41.7 0.6 broadcast_select_fusion.1.target
  42.3 0.0 copy-done.1
  42.3 8.9 %x_forward.1 = (bf16[512,512]{1,0:T(8,128)(2,1)}, bf16[512,1536]{1,0:T(8,128)(2,1)}) custom-call(s32[1,512]{1,0:T(1,128)} %broadcast_select_fusion.1.target, bf16[8,4,16,512]{3,2,1,0:T(8,128)(2,1)} %bitcast.15, f32[1,512]{1,0:T(1,128)} %bitcast.25, bf16[512,1536]{1,0:T(8,128)(2,1)} %w_qkv.5, bf16[512,512]{1,0:T(8,128)(2,1)} %w_out.5), custom_call_target="tpu_custom_call" | custom-call | flops 3000000000 | bytes 4000000 | tf_op jit(solution)/shard_map/x_forward/pallas_call | solution.py:289
  51.2 0.0 all-to-all-done.2
  51.2 0.0 copy-start.2
  51.2 13.7 %all_to_all.25 = bf16[16,32,512]{2,1,0:T(8,128)(2,1)} all-to-all(bf16[16,32,512]{2,1,0:T(8,128)(2,1)} %bitcast.20), channel_id=1, replica_groups=mesh['gz'=2,'gh'=4,'gy'=4] {'gy','gh'}, dimensions={0} | all-to-all | bytes 1048576 | tf_op jit(solution)/shard_map/all_to_all | solution.py:366
  64.9 0.0 copy-done.2
  64.9 0.0 copy-start.4
  64.9 0.0 copy-start.5
  64.9 36.6 %middle.1 = bf16[512,512]{1,0:T(8,128)(2,1)} custom-call(s32[1,512]{1,0:T(1,128)} %constant.33.clone.to_line, s32[1,512]{1,0:T(1,128)} %constant.34.clone.to_sent, bf16[512,512]{1,0:T(8,128)(2,1)} %bitcast.21, bf16[4,8,16,512]{3,2,1,0:T(8,128)(2,1)} %bitcast.17, f32[1,512]{1,0:T(1,128)} %bitcast.23, bf16[512,1536]{1,0:T(8,128)(2,1)} %w_qkv.4, ...), custom_call_target="tpu_custom_call" | custom-call | flops 8999999488 | bytes 4000000 | tf_op jit(solution)/shard_map/middle/pallas_call | solution.py:289
  101.5 3.6 %all-to-all-start.3 = ((bf16[16,32,512]{2,1,0:T(8,128)(2,1)}), bf16[16,32,512]{2,1,0:T(8,128)(2,1)S(1)}, u32[]{:S(2)}, u32[]{:S(2)}) async-start(bf16[16,32,512]{2,1,0:T(8,128)(2,1)} %bitcast.19), calls=%async_computation.3 | async-start | bytes 1048576 | tf_op jit(solution)/shard_map/all_to_all | solution.py:391
  105.1 0.0 copy-done.4
  105.1 0.0 copy-done.5
  105.1 0.6 broadcast_select_fusion.2.to_line
  105.7 8.6 %all-to-all-done.3 = bf16[16,32,512]{2,1,0:T(8,128)(2,1)S(1)} async-done(((bf16[16,32,512]{2,1,0:T(8,128)(2,1)}), bf16[16,32,512]{2,1,0:T(8,128)(2,1)S(1)}, u32[]{:S(2)}, u32[]{:S(2)}) %all-to-all-start.3) | async-done | bytes 524320 | tf_op jit(solution)/shard_map/all_to_all | solution.py:391
  114.3 0.0 copy-start.3
  114.3 0.8 copy-done.3
  115.1 12.3 %x_back.1 = bf16[8,4,16,512]{3,2,1,0:T(8,128)(2,1)} custom-call(s32[1,512]{1,0:T(1,128)} %broadcast_select_fusion.2.to_line, bf16[512,512]{1,0:T(8,128)(2,1)} %bitcast.18, bf16[8,4,16,512]{3,2,1,0:T(8,128)(2,1)} %bitcast.16, bf16[512,1536]{1,0:T(8,128)(2,1)} %get-tuple-element.8.qkv, f32[1,512]{1,0:T(1,128)} %bitcast.26, bf16[512,1536]{1,0:T(8,128)(2,1)} %w_qkv.5, ...), custom_call_target="tpu_custom_call" | custom-call | flops 3000000000 | bytes 4000000 | tf_op jit(solution)/shard_map/x_back/pallas_call | solution.py:289
  127.4 19.3 %all_to_all.26 = bf16[8,64,512]{2,1,0:T(8,128)(2,1)} all-to-all(bf16[8,64,512]{2,1,0:T(8,128)(2,1)} %bitcast.22), channel_id=1, replica_groups=mesh['gz'=2,'gh'=4,'gy'=4] {'gz','gh'}, dimensions={0} | all-to-all | bytes 1048576 | tf_op jit(solution)/shard_map/all_to_all | solution.py:404
  146.6 2.3 %reorder.5 = bf16[512,512]{1,0:T(8,128)(2,1)} custom-call(s32[1,512]{1,0:T(1,128)} %constant.37.clone.target, bf16[512,512]{1,0:T(8,128)(2,1)} %bitcast.14), custom_call_target="tpu_custom_call" | custom-call | tf_op jit(solution)/shard_map/reorder/pallas_call | solution.py:132
  148.9 2.0 %reshape.63 = bf16[16,16,2,512]{3,2,1,0:T(2,128)(2,1)} reshape(bf16[512,512]{1,0:T(8,128)(2,1)} %reorder.5) | data formatting | bytes 1048576 | tf_op jit(solution)/shard_map/reshape | solution.py:407
Async XLA Ops:
  0.0 11.7 %copy-start = (bf16[16,16,2,512]{3,2,1,0:T(2,128)(2,1)S(1)}, bf16[16,16,2,512]{3,2,1,0:T(2,128)(2,1)}, u32[]{:S(2)}) copy-start(bf16[16,16,2,512]{3,2,1,0:T(2,128)(2,1)} %param.22) | copy-start | bytes 1572868
  2.1 10.6 %copy-start.8 = (s32[1,512]{1,0:T(1,128)S(1)}, s32[1,512]{1,0:T(1,128)}, u32[]{:S(2)}) copy-start(s32[1,512]{1,0:T(1,128)} %constant.29.clone) | copy-start | bytes 6148
  2.1 10.6 %copy-start.9 = (s32[1,512]{1,0:T(1,128)S(1)}, s32[1,512]{1,0:T(1,128)}, u32[]{:S(2)}) copy-start(s32[1,512]{1,0:T(1,128)} %constant.30.clone) | copy-start | bytes 6148
  4.4 33.8 %all-to-all-start = ((bf16[8,64,512]{2,1,0:T(8,128)(2,1)}), bf16[8,64,512]{2,1,0:T(8,128)(2,1)S(1)}, u32[]{:S(2)}, u32[]{:S(2)}) async-start(bf16[8,64,512]{2,1,0:T(8,128)(2,1)} %bitcast.13), calls=%async_computation | async-start | bytes 1048576 | tf_op jit(solution)/shard_map/all_to_all | solution.py:346
  15.6 26.2 %copy-start.6 = (s32[1,512]{1,0:T(1,128)S(1)}, s32[1,512]{1,0:T(1,128)}, u32[]{:S(2)}) copy-start(s32[1,512]{1,0:T(1,128)} %constant.31.clone) | copy-start | bytes 6148
  15.6 26.2 %copy-start.7 = (s32[1,512]{1,0:T(1,128)S(1)}, s32[1,512]{1,0:T(1,128)}, u32[]{:S(2)}) copy-start(s32[1,512]{1,0:T(1,128)} %constant.32.clone) | copy-start | bytes 6148
  16.7 20.7 %collective-permute-start = (bf16[256,512]{1,0:T(8,128)(2,1)S(1)}, bf16[256,512]{1,0:T(8,128)(2,1)S(1)}, u32[]{:S(2)}, u32[]{:S(2)}) collective-permute-start(bf16[256,512]{1,0:T(8,128)(2,1)S(1)} %get-tuple-element.10), channel_id=1, source_target_pairs={{0,16},{16,0},{1,17},{17,1},{2,18},{18,2},{3,19},{19,3},{4,20},{20... | collective-permute-start | bytes 786440 | tf_op jit(solution)/shard_map/ppermute | solution.py:351
  38.2 4.1 %copy-start.1 = (bf16[8,64,512]{2,1,0:T(8,128)(2,1)}, bf16[8,64,512]{2,1,0:T(8,128)(2,1)S(1)}, u32[]{:S(2)}) copy-start(bf16[8,64,512]{2,1,0:T(8,128)(2,1)S(1)} %all-to-all-done) | copy-start | bytes 1572868
  38.2 13.0 %all-to-all-start.2 = ((bf16[4,128,512]{2,1,0:T(8,128)(2,1)}), bf16[4,128,512]{2,1,0:T(8,128)(2,1)S(1)}, u32[]{:S(2)}, u32[]{:S(2)}) async-start(bf16[4,128,512]{2,1,0:T(8,128)(2,1)} %bitcast.5), calls=%async_computation.2 | async-start | bytes 1048576 | tf_op jit(solution)/shard_map/all_to_all | solution.py:353
  51.2 13.7 %copy-start.2 = (bf16[4,128,512]{2,1,0:T(8,128)(2,1)}, bf16[4,128,512]{2,1,0:T(8,128)(2,1)S(1)}, u32[]{:S(2)}) copy-start(bf16[4,128,512]{2,1,0:T(8,128)(2,1)S(1)} %all-to-all-done.2) | copy-start | bytes 1572868
  64.9 40.2 %copy-start.4 = (s32[1,512]{1,0:T(1,128)S(1)}, s32[1,512]{1,0:T(1,128)}, u32[]{:S(2)}) copy-start(s32[1,512]{1,0:T(1,128)} %constant.35.clone) | copy-start | bytes 6148
  64.9 40.2 %copy-start.5 = (s32[1,512]{1,0:T(1,128)S(1)}, s32[1,512]{1,0:T(1,128)}, u32[]{:S(2)}) copy-start(s32[1,512]{1,0:T(1,128)} %constant.36.clone) | copy-start | bytes 6148
  101.5 12.8 %all-to-all-start.3 = ((bf16[16,32,512]{2,1,0:T(8,128)(2,1)}), bf16[16,32,512]{2,1,0:T(8,128)(2,1)S(1)}, u32[]{:S(2)}, u32[]{:S(2)}) async-start(bf16[16,32,512]{2,1,0:T(8,128)(2,1)} %bitcast.19), calls=%async_computation.3 | async-start | bytes 1048576 | tf_op jit(solution)/shard_map/all_to_all | solution.py:391
  114.3 0.8 copy-start.3

commit v2 on v1

v2 whole, which is shorter than its diff:
```python
import jax
import jax.numpy as jnp
import numpy as np
from jax import lax
from jax.experimental import pallas as pl
from jax.experimental.pallas import tpu as pltpu
from jax.sharding import Mesh
from jax.sharding import PartitionSpec as P

HEADS = 8
NZ = 2
EPS = 1e-05
F32 = jnp.float32
BF16 = jnp.bfloat16
VMEM_LIMIT = 56 * 1024 * 1024


def dot(a, b):
    return jnp.dot(a, b, preferred_element_type=F32)


def dot_t(a, b):
    return lax.dot_general(a, b, (((1,), (1,)), ((), ())), preferred_element_type=F32)


def dot_lt(a, b):
    return lax.dot_general(a, b, (((0,), (0,)), ((), ())), preferred_element_type=F32)


def one_hot(target):
    size = target.shape[1]
    rows = lax.broadcasted_iota(jnp.int32, (size, size), 0)
    return jnp.where(rows == target, 1.0, 0.0).astype(BF16)


def standardize(x):
    centred = x - jnp.mean(x, -1, keepdims=True)
    inv = lax.rsqrt(jnp.mean(centred * centred, -1, keepdims=True) + EPS)
    return centred * inv, inv


def norm_back(x, gain, grad):
    unit, inv = standardize(x)
    scaled = grad * gain
    return inv * (
        scaled
        - jnp.mean(scaled, -1, keepdims=True)
        - unit * jnp.mean(scaled * unit, -1, keepdims=True)
    )


def group_of(length):
    return 4 if length * 4 <= 256 and HEADS % 4 == 0 else 2


def spread(block, count):
    width = block.shape[1] // count
    lane = lax.broadcasted_iota(jnp.int32, block.shape, 1)
    zero = jnp.zeros_like(block)
    return jnp.concatenate(
        [
            jnp.where((lane >= i * width) & (lane < (i + 1) * width), block, zero)
            for i in range(count)
        ],
        0,
    )


def gather(block, count):
    rows = block.shape[0] // count
    width = block.shape[1] // count
    lane = lax.broadcasted_iota(jnp.int32, (rows, block.shape[1]), 1)
    result = block[:rows]
    for i in range(1, count):
        result = jnp.where(lane >= i * width, block[i * rows : (i + 1) * rows], result)
    return result


class Blocks:
    def __init__(self, count, dim, length):
        self.group = group_of(length)
        self.dim = dim
        self.width = dim // HEADS * self.group
        self.scale = (dim // HEADS) ** -0.5
        self.items = [
            (slice(i * length, (i + 1) * length), j)
            for i in range(count // length)
            for j in range(HEADS // self.group)
        ]

    def lanes(self, j, part=0):
        return slice(part * self.dim + j * self.width, part * self.dim + (j + 1) * self.width)

    def q_wide(self, qkv, rows, j):
        return spread(qkv[rows, self.lanes(j)] * jnp.array(self.scale, BF16), self.group)


def softmax_rows(scores):
    exponent = jnp.exp(scores - jnp.max(scores, 0, keepdims=True))
    return exponent * (1.0 / jnp.sum(exponent, 0, keepdims=True))


def attend(blocks, qkv, mixed, keep=None):
    scores = [
        dot_t(qkv[rows, blocks.lanes(j, 1)], blocks.q_wide(qkv, rows, j))
        for rows, j in blocks.items
    ]
    lows = []
    for i, score in enumerate(scores):
        probs = softmax_rows(score)
        if keep is not None:
            keep[i] = probs
        lows.append(probs.astype(BF16))
    for (rows, j), low in zip(blocks.items, lows):
        out = dot_lt(low, qkv[rows, blocks.lanes(j, 2)])
        mixed[rows, blocks.lanes(j)] = gather(out, blocks.group).astype(BF16)


def attend_back(blocks, qkv, grad, grad_qkv, kept=None):
    probs_all, g_probs_all = [], []
    for i, (rows, j) in enumerate(blocks.items):
        if kept is None:
            probs_all.append(dot_t(qkv[rows, blocks.lanes(j, 1)], blocks.q_wide(qkv, rows, j)))
        g_wide = spread(grad[rows, blocks.lanes(j)], blocks.group)
        g_probs_all.append(dot_t(qkv[rows, blocks.lanes(j, 2)], g_wide))
    lows, g_scores_all = [], []
    for i, g_probs in enumerate(g_probs_all):
        probs = softmax_rows(probs_all[i]) if kept is None else kept[i]
        weighted = probs * g_probs
        total = jnp.sum(weighted, 0, keepdims=True)
        g_scores_all.append((weighted - probs * total).astype(BF16))
        lows.append(probs.astype(BF16))
    for (rows, j), low, g_scores in zip(blocks.items, lows, g_scores_all):
        g_q = gather(dot_lt(g_scores, qkv[rows, blocks.lanes(j, 1)]), blocks.group)
        grad_qkv[rows, blocks.lanes(j)] = (g_q * blocks.scale).astype(BF16)
        g_k = dot(g_scores, blocks.q_wide(qkv, rows, j))
        grad_qkv[rows, blocks.lanes(j, 1)] = g_k.astype(BF16)
        g_v = dot(low, spread(grad[rows, blocks.lanes(j)], blocks.group))
        grad_qkv[rows, blocks.lanes(j, 2)] = g_v.astype(BF16)


def fetch(sems, *pairs):
    copies = [
        pltpu.make_async_copy(source, target, sems.at[i])
        for i, (source, target) in enumerate(pairs)
    ]
    for copy in copies:
        copy.start()
    return copies


def project_qkv(normed, w_qkv, qkv):
    dim = w_qkv.shape[0]
    for j in range(3):
        cols = slice(j * dim, (j + 1) * dim)
        qkv[:, cols] = dot(normed[...], w_qkv[:, cols]).astype(BF16)


def unpack_body(slab_target, target, packed, out, rows):
    slab = slab_target.shape[1]
    blocks = out.shape[1] // 128
    step = slab // blocks
    pick = one_hot(slab_target[...])
    for s in range(packed.shape[0] // slab):
        found = dot(pick, packed[s * slab : (s + 1) * slab, :]).astype(BF16)
        for c in range(blocks):
            rows[s * step : (s + 1) * step, c * 128 : (c + 1) * 128] = found[
                c * step : (c + 1) * step
            ]
    out[...] = dot(one_hot(target[...]), rows[...]).astype(BF16)


def pack_body(slab_target, target, source, packed, rows):
    slab = slab_target.shape[1]
    blocks = source.shape[1] // 128
    step = slab // blocks
    rows[...] = dot(one_hot(target[...]), source[...]).astype(BF16)
    pick = one_hot(slab_target[...])
    for s in range(packed.shape[0] // slab):
        found = jnp.concatenate(
            [rows[s * step : (s + 1) * step, c * 128 : (c + 1) * 128] for c in range(blocks)], 0
        )
        packed[s * slab : (s + 1) * slab, :] = dot(pick, found).astype(BF16)


def x_forward_body(
    target, tok, gain, w_qkv_hbm, w_out_hbm, sent, qkv, normed, mixed, w_qkv, w_out, sems
):
    copies = fetch(sems, (w_qkv_hbm, w_qkv), (w_out_hbm, w_out))
    blocks, lines, part, dim = tok.shape
    length = blocks * part
    for i in range(lines):
        x = tok[:, i].reshape(length, dim).astype(F32)
        unit, _ = standardize(x)
        normed[i * length : (i + 1) * length, :] = (unit * gain[...]).astype(BF16)
    copies[0].wait()
    project_qkv(normed, w_qkv, qkv)
    attend(Blocks(normed.shape[0], dim, length), qkv, mixed)
    copies[1].wait()
    out = dot(mixed[...], w_out[...])
    for i in range(lines):
        rows = slice(i * length, (i + 1) * length)
        x = tok[:, i].reshape(length, dim).astype(F32)
        normed[rows, :] = (x + out[rows]).astype(BF16)
    sent[...] = dot(one_hot(target[...]), normed[...]).astype(BF16)


def middle_body(
    pieces, length, to_line, to_sent, s1_in, cot_other, *refs
):
    (
        gain_y, gain_m, w_qkv_hbm, w_out_hbm, w_up_hbm, w_down_hbm, sent,
        s1, cot, normed, qkv, mixed, s2, probs, acc, grad, grad_qkv,
        w_qkv, w_out, w_up, w_down, sems,
    ) = refs[pieces:]
    cot_own = refs[:pieces]
    copies = fetch(
        sems, (w_qkv_hbm, w_qkv), (w_out_hbm, w_out), (w_up_hbm, w_up), (w_down_hbm, w_down)
    )
    count, dim = s1.shape
    hidden = w_up.shape[1]
    part = length // pieces
    lines = count // length
    s1[...] = dot(one_hot(to_line[...]), s1_in[...]).astype(BF16)
    unit, _ = standardize(s1[...].astype(F32))
    normed[...] = (unit * gain_y[...]).astype(BF16)
    for i in range(lines):
        for k in range(pieces):
            source = cot_own[k] if i < lines // 2 else cot_other
            start = (i if i < lines // 2 else (k - 1) * (lines // 2) + i) * part
            cot[i * length + k * part : i * length + (k + 1) * part, :] = source[
                start : start + part, :
            ]
    copies[0].wait()
    project_qkv(normed, w_qkv, qkv)
    blocks = Blocks(count, dim, length)
    attend(blocks, qkv, mixed, probs)
    copies[1].wait()
    low = (s1[...].astype(F32) + dot(mixed[...], w_out[...])).astype(BF16)
    s2[...] = low
    unit, _ = standardize(low.astype(F32))
    normed[...] = (unit * gain_m[...]).astype(BF16)

    copies[2].wait()
    copies[3].wait()
    chunk = 512 if hidden % 512 == 0 else hidden
    c0 = 0.7978845608028654
    c1 = 0.044715
    for c in range(hidden // chunk):
        cols = slice(c * chunk, (c + 1) * chunk)
        pre = dot(normed[...], w_up[:, cols])
        g_act = dot_t(cot[...], w_down[cols, :]).astype(BF16).astype(F32)
        square = pre * pre
        half = 0.5 * jnp.tanh(pre * (c0 + (c0 * c1) * square)) + 0.5
        slope = half + pre * (half - half * half) * (2 * c0 + (6 * c0 * c1) * square)
        g_pre = (g_act * slope).astype(BF16)
        part_sum = dot_t(g_pre, w_up[:, cols])
        acc[...] = part_sum if c == 0 else acc[...] + part_sum

    back = norm_back(s2[...].astype(F32), gain_m[...], acc[...])
    cot[...] = (cot[...].astype(F32) + back).astype(BF16)
    grad[...] = dot_t(cot[...], w_out[...]).astype(BF16)
    attend_back(blocks, qkv, grad, grad_qkv, probs)
    acc[...] = dot_t(grad_qkv[...], w_qkv[...])
    back = norm_back(s1[...].astype(F32), gain_y[...], acc[...])
    normed[...] = (cot[...].astype(F32) + back).astype(BF16)
    sent[...] = dot(one_hot(to_sent[...]), normed[...]).astype(BF16)


def x_back_body(
    to_line, g1_in, tok_hbm, qkv_hbm, gain, w_qkv_hbm, w_out_hbm, sent,
    g1, grad, grad_qkv, acc, tok, qkv, w_qkv, w_out, sems,
):
    copies = fetch(
        sems, (w_out_hbm, w_out), (qkv_hbm, qkv), (w_qkv_hbm, w_qkv), (tok_hbm, tok)
    )
    blocks, lines, part, dim = tok.shape
    length = blocks * part
    g1[...] = dot(one_hot(to_line[...]), g1_in[...]).astype(BF16)
    copies[0].wait()
    grad[...] = dot_t(g1[...], w_out[...]).astype(BF16)
    copies[1].wait()
    attend_back(Blocks(g1.shape[0], dim, length), qkv, grad, grad_qkv)
    copies[2].wait()
    copies[3].wait()
    acc[...] = dot_t(grad_qkv[...], w_qkv[...])
    for i in range(lines):
        rows = slice(i * length, (i + 1) * length)
        x = tok[:, i].reshape(length, dim).astype(F32)
        total = g1[rows, :].astype(F32) + norm_back(x, gain[...], acc[rows, :])
        sent[:, i] = total.astype(BF16).reshape(blocks, part, dim)


def call(body, name, outs, scratch, args, in_hbm=(), flops=10**9):
    vmem = pl.BlockSpec(memory_space=pltpu.VMEM)
    return pl.pallas_call(
        body,
        out_shape=outs,
        in_specs=[
            pl.BlockSpec(memory_space=pl.ANY) if i in in_hbm else vmem for i in range(len(args))
        ],
        scratch_shapes=scratch,
        compiler_params=pltpu.CompilerParams(vmem_limit_bytes=VMEM_LIMIT),
        cost_estimate=pl.CostEstimate(flops=flops, bytes_accessed=4000000, transcendentals=0),
        name=name,
    )(*args)


def inverse(order):
    result = np.empty_like(order)
    result[order] = np.arange(order.size, dtype=order.dtype)
    return result


def row(order):
    return np.asarray(order, np.int32).reshape(1, -1)


def make_local(gh, gy):
    gx = NZ * gh

    def local(
        tokens, cotangent, gain_x, w_qkv_x, w_out_x, gain_y, w_qkv_y, w_out_y, gain_mlp, w_up,
        w_down,
    ):
        tx, ty, tz, dim = tokens.shape
        hidden = w_up.shape[1]
        count = tx * ty * tz
        y_lines = ty // gh
        own = tx // gy
        x_lines = tz * own
        len_x, len_y = tx * gx, ty * gy
        half, mine = lax.axis_index("gz"), lax.axis_index("gy")

        def vm(shape, dtype=BF16):
            return pltpu.VMEM(shape, dtype)

        def pick(options, index):
            table = jnp.asarray(np.stack([row(o) for o in options]))
            return lax.dynamic_index_in_dim(table, index, keepdims=False)

        tile_row = np.arange(count).reshape(tx, ty, tz)
        tok_order = tile_row.reshape(tx, gh, y_lines, tz).transpose(3, 1, 2, 0).reshape(-1)
        cot_orders = []
        for z in range(NZ):
            for g in range(gy):
                cut = tile_row.reshape(gy, own, ty, tz).transpose(0, 3, 1, 2)
                cut = cut[[g ^ k for k in range(gy)]][:, [z, 1 - z]]
                cot_orders.append(cut.reshape(-1))
        line_row = np.arange(count).reshape(y_lines, NZ, gh, gy, own)
        out_orders = [
            line_row[:, [z, 1 - z]].transpose(3, 2, 0, 1, 4).reshape(-1) for z in range(NZ)
        ]
        come_row = np.arange(count).reshape(gy, gh * y_lines, x_lines)
        y_orders = [
            come_row[[g ^ k for k in range(gy)]].transpose(2, 0, 1).reshape(-1)
            for g in range(gy)
        ]
        lane_blocks = dim // 128
        slab = 32 * tz * lane_blocks
        slab_order = np.arange(slab).reshape(32, lane_blocks, tz).transpose(1, 0, 2).reshape(-1)

        def packed(array):
            split = array.reshape(tx, ty, tz, lane_blocks, 128).transpose(0, 1, 3, 2, 4)
            return split.reshape(count * lane_blocks, 128)

        def unpack(array, target):
            return call(
                unpack_body, "unpack", flat, [vm((count, dim))],
                (row(inverse(slab_order)), target, packed(array)),
            )

        flat = jax.ShapeDtypeStruct((count, dim), BF16)
        gain_x, gain_y, gain_mlp = (g.reshape(1, dim) for g in (gain_x, gain_y, gain_mlp))

        tok_sent = unpack(tokens, row(inverse(tok_order)))
        tok_x = lax.all_to_all(
            tok_sent.reshape(gx, count // gx, dim), ("gz", "gh"), 0, 0, tiled=True
        ).reshape(gx, y_lines, tx, dim)

        cot_sent = unpack(
            cotangent, pick([inverse(o) for o in cot_orders], half * gy + mine)
        ).reshape(gy, count // gy, dim)
        cot_own = [cot_sent[0]] + [
            lax.ppermute(cot_sent[k], "gy", [(i, i ^ k) for i in range(gy)])
            for k in range(1, gy)
        ]
        cot_other = lax.ppermute(
            jnp.concatenate([piece[piece.shape[0] // 2 :] for piece in cot_own], 0),
            "gz",
            [(0, 1), (1, 0)],
        )

        sent, qkv_x = call(
            x_forward_body,
            "x_forward",
            (flat, jax.ShapeDtypeStruct((count, 3 * dim), BF16)),
            [
                vm((count, dim)),
                vm((count, dim)),
                vm((dim, 3 * dim)),
                vm((dim, dim)),
                pltpu.SemaphoreType.DMA((2,)),
            ],
            (pick([inverse(o) for o in out_orders], half), tok_x, gain_x, w_qkv_x, w_out_x),
            in_hbm=(3, 4),
            flops=3 * 10**9,
        )
        s1_y = lax.all_to_all(
            sent.reshape(gh * gy, count // (gh * gy), dim), ("gy", "gh"), 0, 0, tiled=True
        ).reshape(count, dim)

        group = group_of(len_y)
        g1_sent = call(
            lambda *refs: middle_body(gy, len_y, *refs),
            "middle",
            flat,
            [
                vm((count, dim)),
                vm((count, dim)),
                vm((count, dim)),
                vm((count, 3 * dim)),
                vm((count, dim)),
                vm((count, dim)),
                vm((x_lines * HEADS // group, len_y, group * len_y), F32),
                vm((count, dim), F32),
                vm((count, dim)),
                vm((count, 3 * dim)),
                vm((dim, 3 * dim)),
                vm((dim, dim)),
                vm((dim, hidden)),
                vm((hidden, dim)),
                pltpu.SemaphoreType.DMA((4,)),
            ],
            (
                pick([inverse(o) for o in y_orders], mine),
                pick(y_orders, mine),
                s1_y,
                cot_other,
                *cot_own,
                gain_y, gain_mlp, w_qkv_y, w_out_y, w_up, w_down,
            ),
            in_hbm=tuple(range(gy + 6, gy + 10)),
            flops=9 * 10**9,
        )
        g1_x = lax.all_to_all(
            g1_sent.reshape(gh * gy, count // (gh * gy), dim), ("gy", "gh"), 0, 0, tiled=True
        ).reshape(count, dim)

        gt_sent = call(
            x_back_body,
            "x_back",
            jax.ShapeDtypeStruct(tok_x.shape, BF16),
            [
                vm((count, dim)),
                vm((count, dim)),
                vm((count, 3 * dim)),
                vm((count, dim), F32),
                vm(tok_x.shape),
                vm((count, 3 * dim)),
                vm((dim, 3 * dim)),
                vm((dim, dim)),
                pltpu.SemaphoreType.DMA((4,)),
            ],
            (pick(out_orders, half), g1_x, tok_x, qkv_x, gain_x, w_qkv_x, w_out_x),
            in_hbm=(2, 3, 5, 6),
            flops=3 * 10**9,
        )
        gt = lax.all_to_all(
            gt_sent.reshape(gx, count // gx, dim), ("gz", "gh"), 0, 0, tiled=True
        ).reshape(count, dim)
        out = call(
            pack_body,
            "pack",
            jax.ShapeDtypeStruct((count * lane_blocks, 128), BF16),
            [vm((count, dim))],
            (row(slab_order), row(tok_order), gt),
        )
        split = out.reshape(tx, ty, lane_blocks, tz, 128).transpose(0, 1, 3, 2, 4)
        return split.reshape(tx, ty, tz, dim)

    return local


def solution(mesh):
    gx, gy = mesh.shape["gx"], mesh.shape["gy"]
    halved = Mesh(mesh.devices.reshape(NZ, gx // NZ, gy), ("gz", "gh", "gy"))
    tile = P(("gz", "gh"), "gy", None, None)
    return jax.shard_map(
        make_local(gx // NZ, gy),
        mesh=halved,
        in_specs=(tile, tile) + (P(),) * 9,
        out_specs=tile,
        check_vma=False,
    )
```

time: 152 us -> 124 us (0.82)
  Pallas kernels: 64.7 us -> 35.7 us
  waiting for transfers between devices: 26.3 us -> 41.4 us
  blocking collectives: 32.9 us -> 19.5 us
  other arithmetic: 2.6 us -> 0.02 us
    pallas_call x6, Pallas kernels: 64.7 us -> 35.7 us  [call(): pl.pallas_call(body, out_shape=outs, in_specs=[pl.BlockSpec(memory_space=...]
    all_to_all x1, waiting for transfers between devices: 0.01 us -> 13.9 us  [local(): lax.all_to_all(tok_sent.reshape(gx, count // gx, dim), ('gz', 'gh'), 0, 0...]
    all_to_all x1 -> x0, blocking collectives: 13.7 us -> none  [local(): lax.all_to_all(sent.reshape(gh * gy, count // (gh * gy), dim), ('gy', 'gh...]
    reshape x3 -> x0, local copies, waits for them, and re-layouts: 5.11 us -> none  [the longest x1 2.09 us: local(): tok_sent = reorder(row(inverse(tok_order)), tokens.reshape(count, dim))]
    squeeze x0 -> x4, local copies, waits for them, and re-layouts: none -> 3.73 us  [pick(): return lax.dynamic_index_in_dim(table, index, keepdims=False)]
    select_n x3 -> x0, other arithmetic: 1.76 us -> none  [pick(): return jnp.where(mine == 0, row(options[0]), row(options[1]))]
    unnamed x20 -> x18, local copies, waits for them, and re-layouts: 0.84 us -> 2.44 us
    ppermute x1 -> x4, waiting for transfers between devices: 17.8 us -> 19.1 us  [the longest x1 12.1 us: local(): lax.ppermute(jnp.concatenate([piece[piece.shape[0] // 2:] for piece in co...]
  transfers between devices with their start and end apart: 4 -> 7, of which waited for: 2 -> 5; matrix products, arithmetic and copies ran while one was open for 3% -> 5% of each run, Pallas kernels for 7% -> 2%
where the time goes in v2:
time: 124 us; the launch traced here: 123 us
  waiting for transfers between devices  41.4 us (33%)
  Pallas kernels  35.7 us (29%)
  blocking collectives  19.5 us (16%)
  starting transfers between devices  18.5 us (15%)
  local copies, waits for them, and re-layouts  8 us (6%)
    pallas_call x6, Pallas kernels, call(): pl.pallas_call(body, out_shape=outs, in_specs=[pl.BlockSpec(memory_space=...  35.7 us
    all_to_all x1, blocking collectives, local(): lax.all_to_all(gt_sent.reshape(gx, count // gx, dim), ('gz', 'gh'), 0, 0,...  19.5 us
    all_to_all x1, waiting for transfers between devices, local(): lax.all_to_all(tok_sent.reshape(gx, count // gx, dim), ('gz', 'gh'), 0, 0...  13.9 us
    ppermute x1, waiting for transfers between devices, local(): lax.ppermute(jnp.concatenate([piece[piece.shape[0] // 2:] for piece in co...  12.1 us
    all_to_all x1, waiting for transfers between devices, local(): lax.all_to_all(g1_sent.reshape(gh * gy, count // (gh * gy), dim), ('gy',...  8.4 us
    all_to_all x1, starting transfers between devices, local(): lax.all_to_all(tok_sent.reshape(gx, count // gx, dim), ('gz', 'gh'), 0, 0...  7.25 us
    ppermute x3, waiting for transfers between devices, local(): lax.ppermute(cot_sent[k], 'gy', [(i, i ^ k) for i in range(gy)])  7.01 us
    all_to_all x1, starting transfers between devices, local(): lax.all_to_all(sent.reshape(gh * gy, count // (gh * gy), dim), ('gy', 'gh...  3.82 us
  transfers between devices with their start and end apart: 7, of which 5 were waited for; matrix products, arithmetic and copies ran while one was open for 5% of the time, Pallas kernels for 2%

profile of v2, /device:TPU:0, one launch (start us, length us, event | category | flops | bytes accessed | tf_op | source)
XLA Modules:
  0.0 123.2 jit_solution(2090739081055846904)
XLA Ops:
  0.0 0.0 copy-start.7
  0.0 2.6 %unpack.2 = bf16[512,512]{1,0:T(8,128)(2,1)} custom-call(s32[1,256]{1,0:T(1,128)} %constant.49.clone.slab_target, s32[1,512]{1,0:T(1,128)} %constant.50.clone.target, bf16[2048,128]{1,0:T(8,128)(2,1)} %bitcast.45), custom_call_target="tpu_custom_call" | custom-call | flops 1000000000 | bytes 4000000 | tf_op jit(solution)/shard_map/unpack/pallas_call | solution.py:296
  2.6 7.3 %all-to-all-start = ((bf16[8,64,512]{2,1,0:T(8,128)(2,1)}), bf16[8,64,512]{2,1,0:T(8,128)(2,1)S(1)}, u32[]{:S(2)}, u32[]{:S(2)}) async-start(bf16[8,64,512]{2,1,0:T(8,128)(2,1)} %bitcast.40), calls=%async_computation | async-start | bytes 1048576 | tf_op jit(solution)/shard_map/all_to_all | solution.py:377
  9.9 0.0 copy-done.7
  9.9 0.6 dynamic-slice_bitcast_fusion.1.target
  10.5 13.9 %all-to-all-done = bf16[8,64,512]{2,1,0:T(8,128)(2,1)S(1)} async-done(((bf16[8,64,512]{2,1,0:T(8,128)(2,1)}), bf16[8,64,512]{2,1,0:T(8,128)(2,1)S(1)}, u32[]{:S(2)}, u32[]{:S(2)}) %all-to-all-start) | async-done | bytes 524320 | tf_op jit(solution)/shard_map/all_to_all | solution.py:377
  24.3 0.0 copy-start
  24.4 0.8 copy-done
  25.1 6.0 %x_forward.1 = (bf16[512,512]{1,0:T(8,128)(2,1)}, bf16[512,1536]{1,0:T(8,128)(2,1)}) custom-call(s32[1,512]{1,0:T(1,128)} %dynamic-slice_bitcast_fusion.1.target, bf16[8,4,16,512]{3,2,1,0:T(8,128)(2,1)} %bitcast.36, f32[1,512]{1,0:T(1,128)} %bitcast.49, bf16[512,1536]{1,0:T(8,128)(2,1)} %w_qkv_hbm.3, bf16[512,512]{1,0:T(8,128)(2,1)} %w_out_hbm.3), custom_call_target="tpu_custom_call" | custom-call | flops 3000000000 | bytes 4000000 | tf_op jit(solution)/shard_map/x_forward/pallas_call | solution.py:296
  31.1 3.8 %all-to-all-start.1 = ((bf16[16,32,512]{2,1,0:T(8,128)(2,1)}), bf16[16,32,512]{2,1,0:T(8,128)(2,1)S(1)}, u32[]{:S(2)}, u32[]{:S(2)}) async-start(bf16[16,32,512]{2,1,0:T(8,128)(2,1)} %bitcast.39), calls=%async_computation.1 | async-start | bytes 1048576 | tf_op jit(solution)/shard_map/all_to_all | solution.py:409
  35.0 1.3 %dynamic-slice_bitcast_fusion.target = s32[1,512]{1,0:T(1,128)} fusion(s32[8,1,512]{2,1,0:T(1,128)} %constant.51.clone, s32[]{:T(128)S(6)} %select_n.16), kind=kLoop, calls=%fused_computation.1 | loop fusion | bytes 4100 | tf_op jit(solution)/shard_map/jit(dynamic_index_in_dim)/squeeze | solution.py:340
  36.3 2.6 %unpack.3 = bf16[512,512]{1,0:T(8,128)(2,1)} custom-call(s32[1,256]{1,0:T(1,128)} %constant.49.clone.slab_target, s32[1,512]{1,0:T(1,128)} %dynamic-slice_bitcast_fusion.target, bf16[2048,128]{1,0:T(8,128)(2,1)} %bitcast.46), custom_call_target="tpu_custom_call" | custom-call | flops 1000000000 | bytes 4000000 | tf_op jit(solution)/shard_map/unpack/pallas_call | solution.py:296
  38.8 0.0 slice-start
  38.8 1.8 %fusion = (bf16[128,512]{1,0:T(8,128)(2,1)}, bf16[128,512]{1,0:T(8,128)(2,1)S(1)}, bf16[128,512]{1,0:T(8,128)(2,1)S(1)}, bf16[128,512]{1,0:T(8,128)(2,1)S(1)}) fusion(bf16[512,512]{1,0:T(8,128)(2,1)} %unpack.3), kind=kLoop, calls=%fused_computation.6 | loop fusion | bytes 1048576 | tf_op jit(solution)/shard_map/slice | solution.py:384
  40.6 0.4 collective-permute-start
  41.0 1.7 %collective-permute-start.1 = (bf16[128,512]{1,0:T(8,128)(2,1)S(1)}, bf16[128,512]{1,0:T(8,128)(2,1)S(1)}, u32[]{:S(2)}, u32[]{:S(2)}) collective-permute-start(bf16[128,512]{1,0:T(8,128)(2,1)S(1)} %get-tuple-element.11), channel_id=1, source_target_pairs={{0,2},{1,3},{2,0},{3,1},{4,6},{5,7},{6,4},{7,5},{8,10},{9,11},{10,... | collective-permute-start | bytes 393224 | tf_op jit(solution)/shard_map/ppermute | solution.py:385
  42.7 0.0 collective-permute-start.2
  42.7 0.0 collective-permute-done.refs_5_
  42.7 0.0 copy-start.3
  42.7 4.7 %collective-permute-done.1.refs_6_ = bf16[128,512]{1,0:T(8,128)(2,1)S(1)} collective-permute-done((bf16[128,512]{1,0:T(8,128)(2,1)S(1)}, bf16[128,512]{1,0:T(8,128)(2,1)S(1)}, u32[]{:S(2)}, u32[]{:S(2)}) %collective-permute-start.1) | collective-permute-done | bytes 131104 | tf_op jit(solution)/shard_map/ppermute | solution.py:385
  47.4 0.0 copy-start.4
  47.4 2.3 %collective-permute-done.2.refs_7_ = bf16[128,512]{1,0:T(8,128)(2,1)S(1)} collective-permute-done((bf16[128,512]{1,0:T(8,128)(2,1)S(1)}, bf16[128,512]{1,0:T(8,128)(2,1)S(1)}, u32[]{:S(2)}, u32[]{:S(2)}) %collective-permute-start.2) | collective-permute-done | bytes 131104 | tf_op jit(solution)/shard_map/ppermute | solution.py:385
  49.8 0.0 copy-start.5
  49.8 0.0 slice-done
  49.8 1.5 %collective-permute-start.3 = (bf16[256,512]{1,0:T(8,128)(2,1)S(1)}, bf16[256,512]{1,0:T(8,128)(2,1)S(1)}, u32[]{:S(2)}, u32[]{:S(2)}) collective-permute-start(bf16[256,512]{1,0:T(8,128)(2,1)S(1)} %pad_maximum_fusion), channel_id=1, source_target_pairs={{0,16},{16,0},{1,17},{17,1},{2,18},{18,2},{3,19},{19,3},{4,20},{20... | collective-permute-start | bytes 786440 | tf_op jit(solution)/shard_map/ppermute | solution.py:388
  51.3 1.3 %dynamic-slice_bitcast_fusion.2 = (s32[1,512]{1,0:T(1,128)}, s32[1,512]{1,0:T(1,128)}) fusion(s32[4,1,512]{2,1,0:T(1,128)} %constant.54.clone, s32[]{:T(128)S(6)} %select_n.15, s32[4,1,512]{2,1,0:T(1,128)} %constant.53.clone), kind=kLoop, calls=%fused_computation.3 | loop fusion | bytes 8196 | tf_op jit(solution)/shard_map/jit(dynamic_index_in_dim)/squeeze | solution.py:340
  52.6 12.1 %collective-permute-done.3.refs_3_ = bf16[256,512]{1,0:T(8,128)(2,1)S(1)} collective-permute-done((bf16[256,512]{1,0:T(8,128)(2,1)S(1)}, bf16[256,512]{1,0:T(8,128)(2,1)S(1)}, u32[]{:S(2)}, u32[]{:S(2)}) %collective-permute-start.3) | collective-permute-done | bytes 262176 | tf_op jit(solution)/shard_map/ppermute | solution.py:388
  64.7 0.0 copy-start.8
  64.7 0.0 all-to-all-done.1
  64.7 0.0 copy-start.1
  64.7 0.0 copy-done.3
  64.7 0.0 copy-done.4
  64.7 0.0 copy-done.5
  64.7 0.7 copy-done.8
  65.4 0.2 copy-done.1
  65.6 0.0 copy-start.6
  65.6 14.8 %middle.1 = bf16[512,512]{1,0:T(8,128)(2,1)} custom-call(s32[1,512]{1,0:T(1,128)} %get-tuple-element.14.refs_0_, s32[1,512]{1,0:T(1,128)} %get-tuple-element.13.refs_1_, bf16[512,512]{1,0:T(8,128)(2,1)} %bitcast.38, bf16[256,512]{1,0:T(8,128)(2,1)} %copy-done.8, bf16[128,512]{1,0:T(8,128)(2,1)} %get-tuple-element.9.refs_4_, bf16[128,512]{1,0:T(8,128)(2,1)} %copy-done.3, ...), custom_call_target="tpu_custom_call" | custom-call | flops 8999999488 | bytes 4000000 | tf_op jit(solution)/shard_map/middle/pallas_call | solution.py:296
  80.4 3.8 %all-to-all-start.2 = ((bf16[16,32,512]{2,1,0:T(8,128)(2,1)}), bf16[16,32,512]{2,1,0:T(8,128)(2,1)S(1)}, u32[]{:S(2)}, u32[]{:S(2)}) async-start(bf16[16,32,512]{2,1,0:T(8,128)(2,1)} %bitcast.41), calls=%async_computation.2 | async-start | bytes 1048576 | tf_op jit(solution)/shard_map/all_to_all | solution.py:446
  84.2 0.0 copy-done.6
  84.2 0.6 dynamic-slice_bitcast_fusion.4.to_line
  84.8 8.4 %all-to-all-done.2 = bf16[16,32,512]{2,1,0:T(8,128)(2,1)S(1)} async-done(((bf16[16,32,512]{2,1,0:T(8,128)(2,1)}), bf16[16,32,512]{2,1,0:T(8,128)(2,1)S(1)}, u32[]{:S(2)}, u32[]{:S(2)}) %all-to-all-start.2) | async-done | bytes 524320 | tf_op jit(solution)/shard_map/all_to_all | solution.py:446
  93.2 0.0 copy-start.2
  93.2 0.8 copy-done.2
  94.0 7.1 %x_back.1 = bf16[8,4,16,512]{3,2,1,0:T(8,128)(2,1)} custom-call(s32[1,512]{1,0:T(1,128)} %dynamic-slice_bitcast_fusion.4.to_line, bf16[512,512]{1,0:T(8,128)(2,1)} %bitcast.42, bf16[8,4,16,512]{3,2,1,0:T(8,128)(2,1)} %bitcast.37, bf16[512,1536]{1,0:T(8,128)(2,1)} %get-tuple-element.8.qkv_hbm, f32[1,512]{1,0:T(1,128)} %bitcast.50, ...), custom_call_target="tpu_custom_call" | custom-call | flops 3000000000 | bytes 4000000 | tf_op jit(solution)/shard_map/x_back/pallas_call | solution.py:296
  101.1 19.5 %all_to_all.20 = bf16[8,64,512]{2,1,0:T(8,128)(2,1)} all-to-all(bf16[8,64,512]{2,1,0:T(8,128)(2,1)} %bitcast.43), channel_id=1, replica_groups=mesh['gz'=2,'gh'=4,'gy'=4] {'gz','gh'}, dimensions={0} | all-to-all | bytes 1048576 | tf_op jit(solution)/shard_map/all_to_all | solution.py:469
  120.6 2.6 %pack.1 = bf16[2048,128]{1,0:T(8,128)(2,1)} custom-call(s32[1,256]{1,0:T(1,128)} %constant.56.clone.slab_target, s32[1,512]{1,0:T(1,128)} %constant.57.clone.target, bf16[512,512]{1,0:T(8,128)(2,1)} %bitcast.44), custom_call_target="tpu_custom_call" | custom-call | flops 1000000000 | bytes 4000000 | tf_op jit(solution)/shard_map/pack/pallas_call | solution.py:296
  (4 shorter events, 0.0 us)
Async XLA Ops:
  0.0 9.9 %copy-start.7 = (s32[2,1,512]{2,1,0:T(1,128)S(1)}, s32[2,1,512]{2,1,0:T(1,128)}, u32[]{:S(2)}) copy-start(s32[2,1,512]{2,1,0:T(1,128)} %constant.52.clone) | copy-start | bytes 12292
  2.6 21.7 %all-to-all-start = ((bf16[8,64,512]{2,1,0:T(8,128)(2,1)}), bf16[8,64,512]{2,1,0:T(8,128)(2,1)S(1)}, u32[]{:S(2)}, u32[]{:S(2)}) async-start(bf16[8,64,512]{2,1,0:T(8,128)(2,1)} %bitcast.40), calls=%async_computation | async-start | bytes 1048576 | tf_op jit(solution)/shard_map/all_to_all | solution.py:377
  24.3 0.8 copy-start
  31.1 33.6 %all-to-all-start.1 = ((bf16[16,32,512]{2,1,0:T(8,128)(2,1)}), bf16[16,32,512]{2,1,0:T(8,128)(2,1)S(1)}, u32[]{:S(2)}, u32[]{:S(2)}) async-start(bf16[16,32,512]{2,1,0:T(8,128)(2,1)} %bitcast.39), calls=%async_computation.1 | async-start | bytes 1048576 | tf_op jit(solution)/shard_map/all_to_all | solution.py:409
  38.8 10.9 %slice-start = ((bf16[512,512]{1,0:T(8,128)(2,1)}), bf16[64,512]{1,0:T(8,128)(2,1)S(1)}, s32[]{:S(2)}) async-start(bf16[512,512]{1,0:T(8,128)(2,1)} %unpack.3), calls=%async_computation.4 | async-start | bytes 131072 | tf_op jit(solution)/shard_map/slice | solution.py:389
  40.6 2.1 %collective-permute-start = (bf16[128,512]{1,0:T(8,128)(2,1)S(1)}, bf16[128,512]{1,0:T(8,128)(2,1)S(1)}, u32[]{:S(2)}, u32[]{:S(2)}) collective-permute-start(bf16[128,512]{1,0:T(8,128)(2,1)S(1)} %get-tuple-element.12), channel_id=1, source_target_pairs={{0,1},{1,0},{2,3},{3,2},{4,5},{5,4},{6,7},{7,6},{8,9},{9,8},{10,11... | collective-permute-start | bytes 393224 | tf_op jit(solution)/shard_map/ppermute | solution.py:385
  41.0 6.4 %collective-permute-start.1 = (bf16[128,512]{1,0:T(8,128)(2,1)S(1)}, bf16[128,512]{1,0:T(8,128)(2,1)S(1)}, u32[]{:S(2)}, u32[]{:S(2)}) collective-permute-start(bf16[128,512]{1,0:T(8,128)(2,1)S(1)} %get-tuple-element.11), channel_id=1, source_target_pairs={{0,2},{1,3},{2,0},{3,1},{4,6},{5,7},{6,4},{7,5},{8,10},{9,11},{10,... | collective-permute-start | bytes 393224 | tf_op jit(solution)/shard_map/ppermute | solution.py:385
  42.7 7.0 %collective-permute-start.2 = (bf16[128,512]{1,0:T(8,128)(2,1)S(1)}, bf16[128,512]{1,0:T(8,128)(2,1)S(1)}, u32[]{:S(2)}, u32[]{:S(2)}) collective-permute-start(bf16[128,512]{1,0:T(8,128)(2,1)S(1)} %get-tuple-element.10), channel_id=1, source_target_pairs={{0,3},{1,2},{2,1},{3,0},{4,7},{5,6},{6,5},{7,4},{8,11},{9,10},{10,... | collective-permute-start | bytes 393224 | tf_op jit(solution)/shard_map/ppermute | solution.py:385
  42.7 22.0 %copy-start.3 = (bf16[128,512]{1,0:T(8,128)(2,1)}, bf16[128,512]{1,0:T(8,128)(2,1)S(1)}, u32[]{:S(2)}) copy-start(bf16[128,512]{1,0:T(8,128)(2,1)S(1)} %collective-permute-done.refs_5_) | copy-start | bytes 393220
  47.4 17.3 %copy-start.4 = (bf16[128,512]{1,0:T(8,128)(2,1)}, bf16[128,512]{1,0:T(8,128)(2,1)S(1)}, u32[]{:S(2)}) copy-start(bf16[128,512]{1,0:T(8,128)(2,1)S(1)} %collective-permute-done.1.refs_6_) | copy-start | bytes 393220
  49.8 15.0 %copy-start.5 = (bf16[128,512]{1,0:T(8,128)(2,1)}, bf16[128,512]{1,0:T(8,128)(2,1)S(1)}, u32[]{:S(2)}) copy-start(bf16[128,512]{1,0:T(8,128)(2,1)S(1)} %collective-permute-done.2.refs_7_) | copy-start | bytes 393220
  49.8 14.9 %collective-permute-start.3 = (bf16[256,512]{1,0:T(8,128)(2,1)S(1)}, bf16[256,512]{1,0:T(8,128)(2,1)S(1)}, u32[]{:S(2)}, u32[]{:S(2)}) collective-permute-start(bf16[256,512]{1,0:T(8,128)(2,1)S(1)} %pad_maximum_fusion), channel_id=1, source_target_pairs={{0,16},{16,0},{1,17},{17,1},{2,18},{18,2},{3,19},{19,3},{4,20},{20... | collective-permute-start | bytes 786440 | tf_op jit(solution)/shard_map/ppermute | solution.py:388
  64.7 0.7 copy-start.8
  64.7 0.9 copy-start.1
  65.6 18.6 %copy-start.6 = (s32[2,1,512]{2,1,0:T(1,128)S(1)}, s32[2,1,512]{2,1,0:T(1,128)}, u32[]{:S(2)}) copy-start(s32[2,1,512]{2,1,0:T(1,128)} %constant.55.clone) | copy-start | bytes 12292
  80.4 12.8 %all-to-all-start.2 = ((bf16[16,32,512]{2,1,0:T(8,128)(2,1)}), bf16[16,32,512]{2,1,0:T(8,128)(2,1)S(1)}, u32[]{:S(2)}, u32[]{:S(2)}) async-start(bf16[16,32,512]{2,1,0:T(8,128)(2,1)} %bitcast.41), calls=%async_computation.2 | async-start | bytes 1048576 | tf_op jit(solution)/shard_map/all_to_all | solution.py:446
  93.2 0.8 copy-start.2

commit v3 on v2

--- a/solution.py
+++ b/solution.py
@@ -12,7 +12,7 @@
 EPS = 1e-05
 F32 = jnp.float32
 BF16 = jnp.bfloat16
-VMEM_LIMIT = 56 * 1024 * 1024
+MIB = 1024 * 1024
 
 
 def dot(a, b):
@@ -206,7 +206,7 @@
 
 
 def middle_body(
-    pieces, length, to_line, to_sent, s1_in, cot_other, *refs
+    pieces, length, to_line, to_sent, s1_in, cot_other_a, cot_other_b, *refs
 ):
     (
         gain_y, gain_m, w_qkv_hbm, w_out_hbm, w_up_hbm, w_down_hbm, sent,
@@ -226,8 +226,11 @@
     normed[...] = (unit * gain_y[...]).astype(BF16)
     for i in range(lines):
         for k in range(pieces):
-            source = cot_own[k] if i < lines // 2 else cot_other
-            start = (i if i < lines // 2 else (k - 1) * (lines // 2) + i) * part
+            if i < lines // 2:
+                source, start = cot_own[k], i * part
+            else:
+                source = cot_other_a if k < pieces // 2 else cot_other_b
+                start = (k % (pieces // 2) * (lines // 2) + i - lines // 2) * part
             cot[i * length + k * part : i * length + (k + 1) * part, :] = source[
                 start : start + part, :
             ]
@@ -291,7 +294,7 @@
         sent[:, i] = total.astype(BF16).reshape(blocks, part, dim)
 
 
-def call(body, name, outs, scratch, args, in_hbm=(), flops=10**9):
+def call(body, name, outs, scratch, args, vmem_mib, in_hbm=(), flops=10**9):
     vmem = pl.BlockSpec(memory_space=pltpu.VMEM)
     return pl.pallas_call(
         body,
@@ -300,7 +303,7 @@
             pl.BlockSpec(memory_space=pl.ANY) if i in in_hbm else vmem for i in range(len(args))
         ],
         scratch_shapes=scratch,
-        compiler_params=pltpu.CompilerParams(vmem_limit_bytes=VMEM_LIMIT),
+        compiler_params=pltpu.CompilerParams(vmem_limit_bytes=vmem_mib * MIB),
         cost_estimate=pl.CostEstimate(flops=flops, bytes_accessed=4000000, transcendentals=0),
         name=name,
     )(*args)
@@ -368,6 +371,7 @@
             return call(
                 unpack_body, "unpack", flat, [vm((count, dim))],
                 (row(inverse(slab_order)), target, packed(array)),
+                vmem_mib=10,
             )
 
         flat = jax.ShapeDtypeStruct((count, dim), BF16)
@@ -385,11 +389,12 @@
             lax.ppermute(cot_sent[k], "gy", [(i, i ^ k) for i in range(gy)])
             for k in range(1, gy)
         ]
-        cot_other = lax.ppermute(
-            jnp.concatenate([piece[piece.shape[0] // 2 :] for piece in cot_own], 0),
-            "gz",
-            [(0, 1), (1, 0)],
-        )
+        parts = [
+            jnp.concatenate([piece[piece.shape[0] // 2 :] for piece in pieces], 0)
+            for pieces in (cot_own[: gy // 2], cot_own[gy // 2 :])
+        ]
+        *parts, tok_x = lax.optimization_barrier((*parts, tok_x))
+        cot_other = [lax.ppermute(part, "gz", [(0, 1), (1, 0)]) for part in parts]
 
         sent, qkv_x = call(
             x_forward_body,
@@ -403,9 +408,11 @@
                 pltpu.SemaphoreType.DMA((2,)),
             ],
             (pick([inverse(o) for o in out_orders], half), tok_x, gain_x, w_qkv_x, w_out_x),
+            vmem_mib=52,
             in_hbm=(3, 4),
             flops=3 * 10**9,
         )
+        sent, cot_other[0] = lax.optimization_barrier((sent, cot_other[0]))
         s1_y = lax.all_to_all(
             sent.reshape(gh * gy, count // (gh * gy), dim), ("gy", "gh"), 0, 0, tiled=True
         ).reshape(count, dim)
@@ -436,11 +443,12 @@
                 pick([inverse(o) for o in y_orders], mine),
                 pick(y_orders, mine),
                 s1_y,
-                cot_other,
+                *cot_other,
                 *cot_own,
                 gain_y, gain_mlp, w_qkv_y, w_out_y, w_up, w_down,
             ),
-            in_hbm=tuple(range(gy + 6, gy + 10)),
+            vmem_mib=52,
+            in_hbm=tuple(range(gy + 7, gy + 11)),
             flops=9 * 10**9,
         )
         g1_x = lax.all_to_all(
@@ -463,6 +471,7 @@
                 pltpu.SemaphoreType.DMA((4,)),
             ],
             (pick(out_orders, half), g1_x, tok_x, qkv_x, gain_x, w_qkv_x, w_out_x),
+            vmem_mib=52,
             in_hbm=(2, 3, 5, 6),
             flops=3 * 10**9,
         )
@@ -475,6 +484,7 @@
             jax.ShapeDtypeStruct((count * lane_blocks, 128), BF16),
             [vm((count, dim))],
             (row(slab_order), row(tok_order), gt),
+            vmem_mib=10,
         )
         split = out.reshape(tx, ty, lane_blocks, tz, 128).transpose(0, 1, 3, 2, 4)
         return split.reshape(tx, ty, tz, dim)

time: 124 us -> 102 us (0.82)
  waiting for transfers between devices: 41.4 us -> 31.8 us
  Pallas kernels: 35.7 us -> 28 us
  local copies, waits for them, and re-layouts: 8 us -> 3.9 us
  blocking collectives: 19.5 us -> 17.5 us
    all_to_all x1, waiting for transfers between devices: 13.9 us -> 5.56 us  [local(): lax.all_to_all(tok_sent.reshape(gx, count // gx, dim), ('gz', 'gh'), 0, 0...]
    pallas_call x6, Pallas kernels: 35.7 us -> 28 us  [call(): pl.pallas_call(body, out_shape=outs, in_specs=[pl.BlockSpec(memory_space=...]
    ppermute x1 -> x2, waiting for transfers between devices: 12.1 us -> 9.19 us  [local(): cot_other = [lax.ppermute(part, 'gz', [(0, 1), (1, 0)]) for part in parts]]
    all_to_all x1, waiting for transfers between devices: 0.01 us -> 2.62 us  [local(): lax.all_to_all(sent.reshape(gh * gy, count // (gh * gy), dim), ('gy', 'gh...]
    squeeze x4, local copies, waits for them, and re-layouts: 3.73 us -> 1.4 us  [pick(): return lax.dynamic_index_in_dim(table, index, keepdims=False)]
    all_to_all x1, blocking collectives: 19.5 us -> 17.5 us  [local(): lax.all_to_all(gt_sent.reshape(gx, count // gx, dim), ('gz', 'gh'), 0, 0,...]
    ppermute x3, waiting for transfers between devices: 7.01 us -> 5.13 us  [local(): lax.ppermute(cot_sent[k], 'gy', [(i, i ^ k) for i in range(gy)])]
    slice x1, local copies, waits for them, and re-layouts: 1.81 us -> 0.04 us  [local(): cot_sent[0]]
  transfers between devices with their start and end apart: 7 -> 8, of which waited for: 5 -> 7; matrix products, arithmetic and copies ran while one was open for 5% -> 1% of each run, Pallas kernels for 2% -> 6%
where the time goes in v3:
time: 102 us; the launch traced here: 101 us
  waiting for transfers between devices  31.8 us (31%)
  Pallas kernels  28 us (27%)
  starting transfers between devices  19.6 us (19%)
  blocking collectives  17.5 us (17%)
  local copies, waits for them, and re-layouts  3.9 us (4%)
    pallas_call x6, Pallas kernels, call(): pl.pallas_call(body, out_shape=outs, in_specs=[pl.BlockSpec(memory_space=...  28 us
    all_to_all x1, blocking collectives, local(): lax.all_to_all(gt_sent.reshape(gx, count // gx, dim), ('gz', 'gh'), 0, 0,...  17.5 us
    all_to_all x1, waiting for transfers between devices, local(): lax.all_to_all(g1_sent.reshape(gh * gy, count // (gh * gy), dim), ('gy',...  9.26 us
    ppermute x2, waiting for transfers between devices, local(): cot_other = [lax.ppermute(part, 'gz', [(0, 1), (1, 0)]) for part in parts]  9.19 us
    all_to_all x1, starting transfers between devices, local(): lax.all_to_all(tok_sent.reshape(gx, count // gx, dim), ('gz', 'gh'), 0, 0...  7.25 us
    all_to_all x1, waiting for transfers between devices, local(): lax.all_to_all(tok_sent.reshape(gx, count // gx, dim), ('gz', 'gh'), 0, 0...  5.56 us
    ppermute x3, waiting for transfers between devices, local(): lax.ppermute(cot_sent[k], 'gy', [(i, i ^ k) for i in range(gy)])  5.13 us
    all_to_all x1, starting transfers between devices, local(): lax.all_to_all(sent.reshape(gh * gy, count // (gh * gy), dim), ('gy', 'gh...  4.48 us
  transfers between devices with their start and end apart: 8, of which 7 were waited for; matrix products, arithmetic and copies ran while one was open for 1% of the time, Pallas kernels for 6%

profile of v3, /device:TPU:0, one launch (start us, length us, event | category | flops | bytes accessed | tf_op | source)
XLA Modules:
  0.0 100.9 jit_solution(17509322831518910011)
XLA Ops:
  0.0 0.0 copy-start
  0.0 1.0 %copy-done = bf16[16,16,2,512]{3,2,1,0:T(2,128)(2,1)S(1)} copy-done((bf16[16,16,2,512]{3,2,1,0:T(2,128)(2,1)S(1)}, bf16[16,16,2,512]{3,2,1,0:T(2,128)(2,1)}, u32[]{:S(2)}) %copy-start) | copy-done | bytes 524312
  1.0 0.0 copy-start.7
  1.0 0.7 copy-done.7
  1.7 0.0 copy-start.9
  1.7 0.7 copy-done.9
  2.4 0.0 copy-start.1
  2.4 0.0 copy-start.10
  2.4 1.5 %unpack.3 = bf16[512,512]{1,0:T(8,128)(2,1)} custom-call(s32[1,256]{1,0:T(1,128)S(1)} %copy-done.9, s32[1,512]{1,0:T(1,128)S(1)} %copy-done.7, bf16[2048,128]{1,0:T(8,128)(2,1)S(1)} %bitcast.42), custom_call_target="tpu_custom_call" | custom-call | flops 1000000000 | bytes 4000000 | tf_op jit(solution)/shard_map/unpack/pallas_call | solution.py:299
  3.9 7.3 %all-to-all-start = ((bf16[8,64,512]{2,1,0:T(8,128)(2,1)}), bf16[8,64,512]{2,1,0:T(8,128)(2,1)S(1)}, u32[]{:S(2)}, u32[]{:S(2)}) async-start(bf16[8,64,512]{2,1,0:T(8,128)(2,1)} %bitcast.11), calls=%async_computation | async-start | bytes 1048576 | tf_op jit(solution)/shard_map/all_to_all | solution.py:381
  11.2 0.7 dynamic-slice_bitcast_fusion.target
  11.9 0.0 copy-done.1
  11.9 0.0 copy-done.10
  11.9 0.0 copy-start.12
  11.9 0.7 unpack.2
  12.6 0.0 copy-start.2
  12.6 0.0 copy-start.5
  12.7 1.6 %collective-permute-start.1 = (bf16[128,512]{1,0:T(8,128)(2,1)S(1)}, bf16[128,512]{1,0:T(8,128)(2,1)S(1)}, u32[]{:S(2)}, u32[]{:S(2)}) collective-permute-start(bf16[128,512]{1,0:T(8,128)(2,1)S(1)} %get-tuple-element.21), channel_id=1, source_target_pairs={{0,2},{1,3},{2,0},{3,1},{4,6},{5,7},{6,4},{7,5},{8,10},{9,11},{10,... | collective-permute-start | bytes 393224 | tf_op jit(solution)/shard_map/ppermute | solution.py:389
  14.3 0.0 collective-permute-start.2
  14.3 0.6 collective-permute-start
  14.9 0.0 copy-done.12
  14.9 3.3 %collective-permute-done.1.refs_7_ = bf16[128,512]{1,0:T(8,128)(2,1)S(1)} collective-permute-done((bf16[128,512]{1,0:T(8,128)(2,1)S(1)}, bf16[128,512]{1,0:T(8,128)(2,1)S(1)}, u32[]{:S(2)}, u32[]{:S(2)}) %collective-permute-start.1) | collective-permute-done | bytes 131104 | tf_op jit(solution)/shard_map/ppermute | solution.py:389
  18.2 1.9 %collective-permute-done.2.refs_8_ = bf16[128,512]{1,0:T(8,128)(2,1)S(1)} collective-permute-done((bf16[128,512]{1,0:T(8,128)(2,1)S(1)}, bf16[128,512]{1,0:T(8,128)(2,1)S(1)}, u32[]{:S(2)}, u32[]{:S(2)}) %collective-permute-start.2) | collective-permute-done | bytes 131104 | tf_op jit(solution)/shard_map/ppermute | solution.py:389
  20.1 0.0 collective-permute-done.refs_6_
  20.1 5.6 %all-to-all-done = bf16[8,64,512]{2,1,0:T(8,128)(2,1)S(1)} async-done(((bf16[8,64,512]{2,1,0:T(8,128)(2,1)}), bf16[8,64,512]{2,1,0:T(8,128)(2,1)S(1)}, u32[]{:S(2)}, u32[]{:S(2)}) %all-to-all-start) | async-done | bytes 524320 | tf_op jit(solution)/shard_map/all_to_all | solution.py:381
  25.7 0.1 collective-permute-start.3
  25.8 0.0 copy-done.2
  25.8 0.0 copy-done.5
  25.8 0.0 copy-start.3
  25.8 0.0 copy-start.4
  25.8 5.2 %x_forward.1 = (bf16[512,512]{1,0:T(8,128)(2,1)}, bf16[512,1536]{1,0:T(8,128)(2,1)}) custom-call(s32[1,512]{1,0:T(1,128)S(1)} %dynamic-slice_bitcast_fusion.1.target, bf16[8,4,16,512]{3,2,1,0:T(8,128)(2,1)S(1)} %bitcast.36, f32[1,512]{1,0:T(1,128)S(1)} %bitcast.46, bf16[512,1536]{1,0:T(8,128)(2,1)} %w_qkv_hbm.3, bf16[512,512]{1,0:T(8,128)(2,1)S(1)} %copy-done.2), custom_call_target="tpu_custom_call" | custom-call | flops 3000000000 | bytes 4000000 | tf_op jit(solution)/shard_map/x_forward/pallas_call | solution.py:299
  31.1 1.9 %collective-permute-done.3.refs_3_ = bf16[128,512]{1,0:T(8,128)(2,1)S(1)} collective-permute-done((bf16[128,512]{1,0:T(8,128)(2,1)S(1)}, bf16[128,512]{1,0:T(8,128)(2,1)S(1)}, u32[]{:S(2)}, u32[]{:S(2)}) %collective-permute-start.3) | collective-permute-done | bytes 131104 | tf_op jit(solution)/shard_map/ppermute | solution.py:397
  32.9 4.5 %all-to-all-start.1 = ((bf16[16,32,512]{2,1,0:T(8,128)(2,1)}), bf16[16,32,512]{2,1,0:T(8,128)(2,1)S(1)}, u32[]{:S(2)}, u32[]{:S(2)}) async-start(bf16[16,32,512]{2,1,0:T(8,128)(2,1)} %bitcast.14), calls=%async_computation.1 | async-start | bytes 1048576 | tf_op jit(solution)/shard_map/all_to_all | solution.py:416
  37.4 1.5 %collective-permute-start.4 = (bf16[128,512]{1,0:T(8,128)(2,1)S(1)}, bf16[128,512]{1,0:T(8,128)(2,1)S(1)}, u32[]{:S(2)}, u32[]{:S(2)}) collective-permute-start(bf16[128,512]{1,0:T(8,128)(2,1)S(1)} %pad_maximum_fusion.1), channel_id=1, source_target_pairs={{0,16},{16,0},{1,17},{17,1},{2,18},{18,2},{3,19},{19,3},{4,20},{20... | collective-permute-start | bytes 393224 | tf_op jit(solution)/shard_map/ppermute | solution.py:397
  38.9 0.7 dynamic-slice_bitcast_fusion.2
  39.6 7.3 %collective-permute-done.4.refs_4_ = bf16[128,512]{1,0:T(8,128)(2,1)S(1)} collective-permute-done((bf16[128,512]{1,0:T(8,128)(2,1)S(1)}, bf16[128,512]{1,0:T(8,128)(2,1)S(1)}, u32[]{:S(2)}, u32[]{:S(2)}) %collective-permute-start.4) | collective-permute-done | bytes 131104 | tf_op jit(solution)/shard_map/ppermute | solution.py:397
  46.9 2.6 %all-to-all-done.1 = bf16[16,32,512]{2,1,0:T(8,128)(2,1)S(1)} async-done(((bf16[16,32,512]{2,1,0:T(8,128)(2,1)}), bf16[16,32,512]{2,1,0:T(8,128)(2,1)S(1)}, u32[]{:S(2)}, u32[]{:S(2)}) %all-to-all-start.1) | async-done | bytes 524320 | tf_op jit(solution)/shard_map/all_to_all | solution.py:416
  49.5 0.0 copy-done.3
  49.5 0.0 copy-done.4
  49.5 0.0 copy-start.11
  49.5 13.7 %middle.1 = bf16[512,512]{1,0:T(8,128)(2,1)} custom-call(s32[1,512]{1,0:T(1,128)S(1)} %get-tuple-element.24.refs_0_, s32[1,512]{1,0:T(1,128)S(1)} %get-tuple-element.23.refs_1_, bf16[512,512]{1,0:T(8,128)(2,1)S(1)} %bitcast.38, bf16[128,512]{1,0:T(8,128)(2,1)S(1)} %collective-permute-done.3.refs_3_, bf16[128,512]{1,0:T(8,128)(2,1)S(1)} %collective-permute-done.4.refs_4_, ...), custom_call_target="tpu_custom_call" | custom-call | flops 8999999488 | bytes 4000000 | tf_op jit(solution)/shard_map/middle/pallas_call | solution.py:299
  63.2 4.1 %all-to-all-start.2 = ((bf16[16,32,512]{2,1,0:T(8,128)(2,1)}), bf16[16,32,512]{2,1,0:T(8,128)(2,1)S(1)}, u32[]{:S(2)}, u32[]{:S(2)}) async-start(bf16[16,32,512]{2,1,0:T(8,128)(2,1)} %bitcast.18), calls=%async_computation.2 | async-start | bytes 1048576 | tf_op jit(solution)/shard_map/all_to_all | solution.py:454
  67.3 0.0 copy-done.11
  67.3 9.3 %all-to-all-done.2 = bf16[16,32,512]{2,1,0:T(8,128)(2,1)S(1)} async-done(((bf16[16,32,512]{2,1,0:T(8,128)(2,1)}), bf16[16,32,512]{2,1,0:T(8,128)(2,1)S(1)}, u32[]{:S(2)}, u32[]{:S(2)}) %all-to-all-start.2) | async-done | bytes 524320 | tf_op jit(solution)/shard_map/all_to_all | solution.py:454
  76.6 0.0 copy-start.6
  76.6 0.0 copy-start.8
  76.6 5.3 %x_back.1 = bf16[8,4,16,512]{3,2,1,0:T(8,128)(2,1)S(1)} custom-call(s32[1,512]{1,0:T(1,128)S(1)} %dynamic-slice_bitcast_fusion.4.to_line, bf16[512,512]{1,0:T(8,128)(2,1)S(1)} %bitcast.39, bf16[8,4,16,512]{3,2,1,0:T(8,128)(2,1)S(1)} %bitcast.37, bf16[512,1536]{1,0:T(8,128)(2,1)} %get-tuple-element.18.qkv_hbm, f32[1,512]{1,0:T(1,128)S(1)} %bitcast.47, ...), custom_call_target="tpu_custom_call" | custom-call | flops 3000000000 | bytes 4000000 | tf_op jit(solution)/shard_map/x_back/pallas_call | solution.py:299
  81.9 17.5 %all_to_all.20 = bf16[8,64,512]{2,1,0:T(8,128)(2,1)S(1)} all-to-all(bf16[8,64,512]{2,1,0:T(8,128)(2,1)S(1)} %bitcast.40), channel_id=1, replica_groups=mesh['gz'=2,'gh'=4,'gy'=4] {'gz','gh'}, dimensions={0} | all-to-all | bytes 1048576 | tf_op jit(solution)/shard_map/all_to_all | solution.py:478
  99.3 0.0 copy-done.6
  99.4 0.0 copy-done.8
  99.4 1.6 %pack.1 = bf16[2048,128]{1,0:T(8,128)(2,1)} custom-call(s32[1,256]{1,0:T(1,128)S(1)} %copy-done.8, s32[1,512]{1,0:T(1,128)S(1)} %copy-done.6, bf16[512,512]{1,0:T(8,128)(2,1)S(1)} %bitcast.41), custom_call_target="tpu_custom_call" | custom-call | flops 1000000000 | bytes 4000000 | tf_op jit(solution)/shard_map/pack/pallas_call | solution.py:299
  (9 shorter events, 0.1 us)
Async XLA Ops:
  0.0 1.0 %copy-start = (bf16[16,16,2,512]{3,2,1,0:T(2,128)(2,1)S(1)}, bf16[16,16,2,512]{3,2,1,0:T(2,128)(2,1)}, u32[]{:S(2)}) copy-start(bf16[16,16,2,512]{3,2,1,0:T(2,128)(2,1)} %param.21) | copy-start | bytes 1572868
  1.0 0.7 copy-start.7
  1.7 0.7 copy-start.9
  2.4 9.5 %copy-start.1 = (bf16[16,16,2,512]{3,2,1,0:T(2,128)(2,1)S(1)}, bf16[16,16,2,512]{3,2,1,0:T(2,128)(2,1)}, u32[]{:S(2)}) copy-start(bf16[16,16,2,512]{3,2,1,0:T(2,128)(2,1)} %param.22) | copy-start | bytes 1572868
  2.4 9.5 %copy-start.10 = (s32[1,256]{1,0:T(1,128)S(1)}, s32[1,256]{1,0:T(1,128)}, u32[]{:S(2)}) copy-start(s32[1,256]{1,0:T(1,128)} %constant.49.clone.slab_target) | copy-start | bytes 3076
  3.9 21.7 %all-to-all-start = ((bf16[8,64,512]{2,1,0:T(8,128)(2,1)}), bf16[8,64,512]{2,1,0:T(8,128)(2,1)S(1)}, u32[]{:S(2)}, u32[]{:S(2)}) async-start(bf16[8,64,512]{2,1,0:T(8,128)(2,1)} %bitcast.11), calls=%async_computation | async-start | bytes 1048576 | tf_op jit(solution)/shard_map/all_to_all | solution.py:381
  11.9 3.0 %copy-start.12 = (s32[2,1,512]{2,1,0:T(1,128)S(1)}, s32[2,1,512]{2,1,0:T(1,128)}, u32[]{:S(2)}) copy-start(s32[2,1,512]{2,1,0:T(1,128)} %constant.52.clone) | copy-start | bytes 12292
  12.6 13.2 %copy-start.2 = (bf16[512,512]{1,0:T(8,128)(2,1)S(1)}, bf16[512,512]{1,0:T(8,128)(2,1)}, u32[]{:S(2)}) copy-start(bf16[512,512]{1,0:T(8,128)(2,1)} %w_out_hbm.3) | copy-start | bytes 1572868
  12.6 13.2 %copy-start.5 = (f32[512]{0:T(512)S(1)}, f32[512]{0:T(512)}, u32[]{:S(2)}) copy-start(f32[512]{0:T(512)} %param.23) | copy-start | bytes 6148
  12.7 5.5 %collective-permute-start.1 = (bf16[128,512]{1,0:T(8,128)(2,1)S(1)}, bf16[128,512]{1,0:T(8,128)(2,1)S(1)}, u32[]{:S(2)}, u32[]{:S(2)}) collective-permute-start(bf16[128,512]{1,0:T(8,128)(2,1)S(1)} %get-tuple-element.21), channel_id=1, source_target_pairs={{0,2},{1,3},{2,0},{3,1},{4,6},{5,7},{6,4},{7,5},{8,10},{9,11},{10,... | collective-permute-start | bytes 393224 | tf_op jit(solution)/shard_map/ppermute | solution.py:389
  14.3 5.8 %collective-permute-start.2 = (bf16[128,512]{1,0:T(8,128)(2,1)S(1)}, bf16[128,512]{1,0:T(8,128)(2,1)S(1)}, u32[]{:S(2)}, u32[]{:S(2)}) collective-permute-start(bf16[128,512]{1,0:T(8,128)(2,1)S(1)} %get-tuple-element.20), channel_id=1, source_target_pairs={{0,3},{1,2},{2,1},{3,0},{4,7},{5,6},{6,5},{7,4},{8,11},{9,10},{10,... | collective-permute-start | bytes 393224 | tf_op jit(solution)/shard_map/ppermute | solution.py:389
  14.3 5.8 %collective-permute-start = (bf16[128,512]{1,0:T(8,128)(2,1)S(1)}, bf16[128,512]{1,0:T(8,128)(2,1)S(1)}, u32[]{:S(2)}, u32[]{:S(2)}) collective-permute-start(bf16[128,512]{1,0:T(8,128)(2,1)S(1)} %get-tuple-element.22), channel_id=1, source_target_pairs={{0,1},{1,0},{2,3},{3,2},{4,5},{5,4},{6,7},{7,6},{8,9},{9,8},{10,11... | collective-permute-start | bytes 393224 | tf_op jit(solution)/shard_map/ppermute | solution.py:389
  25.7 7.3 %collective-permute-start.3 = (bf16[128,512]{1,0:T(8,128)(2,1)S(1)}, bf16[128,512]{1,0:T(8,128)(2,1)S(1)}, u32[]{:S(2)}, u32[]{:S(2)}) collective-permute-start(bf16[128,512]{1,0:T(8,128)(2,1)S(1)} %pad_maximum_fusion), channel_id=1, source_target_pairs={{0,16},{16,0},{1,17},{17,1},{2,18},{18,2},{3,19},{19,3},{4,20},{20... | collective-permute-start | bytes 393224 | tf_op jit(solution)/shard_map/ppermute | solution.py:397
  25.8 23.7 %copy-start.3 = (f32[512]{0:T(512)S(1)}, f32[512]{0:T(512)}, u32[]{:S(2)}) copy-start(f32[512]{0:T(512)} %param.26) | copy-start | bytes 6148
  25.8 23.7 %copy-start.4 = (f32[512]{0:T(512)S(1)}, f32[512]{0:T(512)}, u32[]{:S(2)}) copy-start(f32[512]{0:T(512)} %param.29) | copy-start | bytes 6148
  32.9 16.6 %all-to-all-start.1 = ((bf16[16,32,512]{2,1,0:T(8,128)(2,1)}), bf16[16,32,512]{2,1,0:T(8,128)(2,1)S(1)}, u32[]{:S(2)}, u32[]{:S(2)}) async-start(bf16[16,32,512]{2,1,0:T(8,128)(2,1)} %bitcast.14), calls=%async_computation.1 | async-start | bytes 1048576 | tf_op jit(solution)/shard_map/all_to_all | solution.py:416
  37.4 9.5 %collective-permute-start.4 = (bf16[128,512]{1,0:T(8,128)(2,1)S(1)}, bf16[128,512]{1,0:T(8,128)(2,1)S(1)}, u32[]{:S(2)}, u32[]{:S(2)}) collective-permute-start(bf16[128,512]{1,0:T(8,128)(2,1)S(1)} %pad_maximum_fusion.1), channel_id=1, source_target_pairs={{0,16},{16,0},{1,17},{17,1},{2,18},{18,2},{3,19},{19,3},{4,20},{20... | collective-permute-start | bytes 393224 | tf_op jit(solution)/shard_map/ppermute | solution.py:397
  49.5 17.8 %copy-start.11 = (s32[2,1,512]{2,1,0:T(1,128)S(1)}, s32[2,1,512]{2,1,0:T(1,128)}, u32[]{:S(2)}) copy-start(s32[2,1,512]{2,1,0:T(1,128)} %constant.55.clone) | copy-start | bytes 12292
  63.2 13.4 %all-to-all-start.2 = ((bf16[16,32,512]{2,1,0:T(8,128)(2,1)}), bf16[16,32,512]{2,1,0:T(8,128)(2,1)S(1)}, u32[]{:S(2)}, u32[]{:S(2)}) async-start(bf16[16,32,512]{2,1,0:T(8,128)(2,1)} %bitcast.18), calls=%async_computation.2 | async-start | bytes 1048576 | tf_op jit(solution)/shard_map/all_to_all | solution.py:454
  76.6 22.7 %copy-start.6 = (s32[1,512]{1,0:T(1,128)S(1)}, s32[1,512]{1,0:T(1,128)}, u32[]{:S(2)}) copy-start(s32[1,512]{1,0:T(1,128)} %constant.57.clone.target) | copy-start | bytes 6148
  76.6 22.7 %copy-start.8 = (s32[1,256]{1,0:T(1,128)S(1)}, s32[1,256]{1,0:T(1,128)}, u32[]{:S(2)}) copy-start(s32[1,256]{1,0:T(1,128)} %constant.56.clone.slab_target) | copy-start | bytes 3076

commit v4 on v3

--- a/solution.py
+++ b/solution.py
@@ -156,38 +156,106 @@
         qkv[:, cols] = dot(normed[...], w_qkv[:, cols]).astype(BF16)
 
 
-def unpack_body(slab_target, target, packed, out, rows):
-    slab = slab_target.shape[1]
-    blocks = out.shape[1] // 128
-    step = slab // blocks
-    pick = one_hot(slab_target[...])
+def digits(values, *sizes):
+    found = []
+    for size in reversed(sizes):
+        if size & (size - 1) == 0:
+            found.append(values & (size - 1))
+            values = values >> (size.bit_length() - 1)
+        else:
+            found.append(lax.rem(values, size))
+            values = lax.div(values, size)
+    return found[::-1]
+
+
+def slab_target(depth, blocks, step):
+    lane = lax.broadcasted_iota(jnp.int32, (1, step * blocks), 1)
+    place, block, z = digits(lane, step // depth, blocks, depth)
+    return block * step + place * depth + z
+
+
+def line_target(count, tx, ty, tz, gh):
+    lane = lax.broadcasted_iota(jnp.int32, (1, count), 1)
+    x, r, y, z = digits(lane, tx, gh, ty // gh, tz)
+    return ((z * gh + r) * (ty // gh) + y) * tx + x
+
+
+def unpack_slabs(depth, packed, rows):
+    blocks = rows.shape[1] // 128
+    step = 32 * depth
+    slab = step * blocks
+    pick = one_hot(slab_target(depth, blocks, step))
     for s in range(packed.shape[0] // slab):
         found = dot(pick, packed[s * slab : (s + 1) * slab, :]).astype(BF16)
         for c in range(blocks):
             rows[s * step : (s + 1) * step, c * 128 : (c + 1) * 128] = found[
                 c * step : (c + 1) * step
             ]
+
+
+def unpack_tokens_body(tx, ty, tz, gh, packed, *refs):
+    *outs, rows, sent = refs
+    unpack_slabs(tz, packed, rows)
+    target = sent if len(outs) > 1 else outs[0]
+    target[...] = dot(one_hot(line_target(rows.shape[0], tx, ty, tz, gh)), rows[...]).astype(BF16)
+    scatter_blocks(target, outs)
+
+
+def unpack_body(tz, target, packed, out, rows):
+    unpack_slabs(tz, packed, rows)
     out[...] = dot(one_hot(target[...]), rows[...]).astype(BF16)
 
 
-def pack_body(slab_target, target, source, packed, rows):
-    slab = slab_target.shape[1]
-    blocks = source.shape[1] // 128
-    step = slab // blocks
-    rows[...] = dot(one_hot(target[...]), source[...]).astype(BF16)
-    pick = one_hot(slab_target[...])
-    for s in range(packed.shape[0] // slab):
+def gx_index(count):
+    return lax.axis_index("gz") * (count // NZ) + lax.axis_index("gh")
+
+
+def scatter_blocks(sent, outs):
+    if len(outs) == 1:
+        return
+    for source, out in zip(block_targets(sent, len(outs)), outs):
+        out[...] = source[...]
+
+
+def block_targets(whole, count):
+    if count == 1:
+        return [whole]
+    size = whole.shape[0] // count
+    me = gx_index(count)
+    return [whole.at[pl.ds(pl.multiple_of((me ^ k) * size, size), size)] for k in range(count)]
+
+
+def gather_blocks(blocks, whole):
+    if len(blocks) == 1:
+        return blocks[0]
+    for block, target in zip(blocks, block_targets(whole, len(blocks))):
+        target[...] = block[...]
+    return whole
+
+
+def pack_body(tx, ty, tz, gh, *refs):
+    *parts, packed, rows, whole = refs
+    source = gather_blocks(parts, whole)
+    count, dim = rows.shape
+    blocks = dim // 128
+    step = 32 * tz
+    move = one_hot(line_target(count, tx, ty, tz, gh))
+    rows[...] = dot_lt(move, source[...]).astype(BF16)
+    pick = one_hot(slab_target(tz, blocks, step))
+    for s in range(count // step):
         found = jnp.concatenate(
             [rows[s * step : (s + 1) * step, c * 128 : (c + 1) * 128] for c in range(blocks)], 0
         )
-        packed[s * slab : (s + 1) * slab, :] = dot(pick, found).astype(BF16)
+        packed[s * step * blocks : (s + 1) * step * blocks, :] = dot_lt(pick, found).astype(BF16)
 
 
 def x_forward_body(
-    target, tok, gain, w_qkv_hbm, w_out_hbm, sent, qkv, normed, mixed, w_qkv, w_out, sems
+    shape, target, gain, w_qkv_hbm, w_out_hbm, *refs
 ):
+    *parts, sent, qkv, whole, normed, mixed, w_qkv, w_out, sems = refs
     copies = fetch(sems, (w_qkv_hbm, w_qkv), (w_out_hbm, w_out))
-    blocks, lines, part, dim = tok.shape
+    tok = gather_blocks(parts, whole).reshape(shape)
+    blocks, lines, part, dim = shape
     length = blocks * part
     for i in range(lines):
         x = tok[:, i].reshape(length, dim).astype(F32)
@@ -211,12 +279,10 @@
     (
         gain_y, gain_m, w_qkv_hbm, w_out_hbm, w_up_hbm, w_down_hbm, sent,
         s1, cot, normed, qkv, mixed, s2, probs, acc, grad, grad_qkv,
-        w_qkv, w_out, w_up, w_down, sems,
+        w_qkv, w_out, w_up, w_down, sems, late_sems,
     ) = refs[pieces:]
     cot_own = refs[:pieces]
-    copies = fetch(
-        sems, (w_qkv_hbm, w_qkv), (w_out_hbm, w_out), (w_up_hbm, w_up), (w_down_hbm, w_down)
-    )
+    copies = fetch(sems, (w_qkv_hbm, w_qkv), (w_out_hbm, w_out))
     count, dim = s1.shape
     hidden = w_up.shape[1]
     part = length // pieces
@@ -235,6 +301,7 @@
                 start : start + part, :
             ]
     copies[0].wait()
+    late = fetch(late_sems, (w_up_hbm, w_up), (w_down_hbm, w_down))
     project_qkv(normed, w_qkv, qkv)
     blocks = Blocks(count, dim, length)
     attend(blocks, qkv, mixed, probs)
@@ -244,8 +311,8 @@
     unit, _ = standardize(low.astype(F32))
     normed[...] = (unit * gain_m[...]).astype(BF16)
 
-    copies[2].wait()
-    copies[3].wait()
+    for copy in late:
+        copy.wait()
     chunk = 512 if hidden % 512 == 0 else hidden
     c0 = 0.7978845608028654
     c1 = 0.044715
@@ -270,28 +337,35 @@
     sent[...] = dot(one_hot(to_sent[...]), normed[...]).astype(BF16)
 
 
-def x_back_body(
-    to_line, g1_in, tok_hbm, qkv_hbm, gain, w_qkv_hbm, w_out_hbm, sent,
-    g1, grad, grad_qkv, acc, tok, qkv, w_qkv, w_out, sems,
-):
+def x_back_body(shape, inputs, to_line, g1_in, qkv_hbm, gain, w_qkv_hbm, w_out_hbm, *refs):
+    parts = refs[:inputs]
+    *outs, whole, sent, g1, grad, grad_qkv, acc, qkv, w_qkv, w_out, sems = refs[inputs:]
     copies = fetch(
-        sems, (w_out_hbm, w_out), (qkv_hbm, qkv), (w_qkv_hbm, w_qkv), (tok_hbm, tok)
+        sems,
+        (w_out_hbm, w_out),
+        (qkv_hbm, qkv),
+        (w_qkv_hbm, w_qkv),
+        *zip(parts, block_targets(whole, inputs)),
     )
-    blocks, lines, part, dim = tok.shape
+    blocks, lines, part, dim = shape
+    tok = whole.reshape(shape)
+    target = sent if len(outs) > 1 else outs[0]
+    sent_lines = target.reshape(shape)
     length = blocks * part
     g1[...] = dot(one_hot(to_line[...]), g1_in[...]).astype(BF16)
     copies[0].wait()
     grad[...] = dot_t(g1[...], w_out[...]).astype(BF16)
     copies[1].wait()
     attend_back(Blocks(g1.shape[0], dim, length), qkv, grad, grad_qkv)
-    copies[2].wait()
-    copies[3].wait()
+    for copy in copies[2:]:
+        copy.wait()
     acc[...] = dot_t(grad_qkv[...], w_qkv[...])
     for i in range(lines):
         rows = slice(i * length, (i + 1) * length)
         x = tok[:, i].reshape(length, dim).astype(F32)
         total = g1[rows, :].astype(F32) + norm_back(x, gain[...], acc[rows, :])
-        sent[:, i] = total.astype(BF16).reshape(blocks, part, dim)
+        sent_lines[:, i] = total.astype(BF16).reshape(blocks, part, dim)
+    scatter_blocks(target, outs)
 
 
 def call(body, name, outs, scratch, args, vmem_mib, in_hbm=(), flops=10**9):
@@ -343,7 +417,6 @@
             return lax.dynamic_index_in_dim(table, index, keepdims=False)
 
         tile_row = np.arange(count).reshape(tx, ty, tz)
-        tok_order = tile_row.reshape(tx, gh, y_lines, tz).transpose(3, 1, 2, 0).reshape(-1)
         cot_orders = []
         for z in range(NZ):
             for g in range(gy):
@@ -360,30 +433,45 @@
             for g in range(gy)
         ]
         lane_blocks = dim // 128
-        slab = 32 * tz * lane_blocks
-        slab_order = np.arange(slab).reshape(32, lane_blocks, tz).transpose(1, 0, 2).reshape(-1)
 
         def packed(array):
             split = array.reshape(tx, ty, tz, lane_blocks, 128).transpose(0, 1, 3, 2, 4)
             return split.reshape(count * lane_blocks, 128)
 
-        def unpack(array, target):
-            return call(
-                unpack_body, "unpack", flat, [vm((count, dim))],
-                (row(inverse(slab_order)), target, packed(array)),
-                vmem_mib=10,
-            )
+        def exchange(parts, first):
+            if len(parts) == 1:
+                whole = parts[0].reshape(gx, count // gx, dim)
+                moved = lax.all_to_all(whole, ("gz", "gh"), 0, 0, tiled=True)
+                return [moved.reshape(count, dim)]
+            moved = list(parts)
+            for k in first:
+                pairs = [(i, i ^ k) for i in range(gx)]
+                moved[k] = lax.ppermute(parts[k], ("gz", "gh"), pairs)
+            return moved
 
         flat = jax.ShapeDtypeStruct((count, dim), BF16)
+        block = jax.ShapeDtypeStruct((count // gx, dim), BF16)
+        far_first = [*range(gx // NZ, gx), *range(1, gx // NZ)]
+        line_shape = (gx, y_lines, tx, dim)
         gain_x, gain_y, gain_mlp = (g.reshape(1, dim) for g in (gain_x, gain_y, gain_mlp))
 
-        tok_sent = unpack(tokens, row(inverse(tok_order)))
-        tok_x = lax.all_to_all(
-            tok_sent.reshape(gx, count // gx, dim), ("gz", "gh"), 0, 0, tiled=True
-        ).reshape(gx, y_lines, tx, dim)
-
-        cot_sent = unpack(
-            cotangent, pick([inverse(o) for o in cot_orders], half * gy + mine)
+        tok_sent = call(
+            lambda *refs: unpack_tokens_body(tx, ty, tz, gh, *refs),
+            "unpack_tokens",
+            [flat],
+            [vm((count, dim)), vm((count, dim))],
+            (packed(tokens),),
+            vmem_mib=10,
+        )
+        tok_x = exchange(tok_sent, far_first)
+
+        cot_sent = call(
+            lambda *refs: unpack_body(tz, *refs),
+            "unpack_cotangent",
+            flat,
+            [vm((count, dim))],
+            (pick([inverse(o) for o in cot_orders], half * gy + mine), packed(cotangent)),
+            vmem_mib=10,
         ).reshape(gy, count // gy, dim)
         cot_own = [cot_sent[0]] + [
             lax.ppermute(cot_sent[k], "gy", [(i, i ^ k) for i in range(gy)])
@@ -393,23 +481,24 @@
             jnp.concatenate([piece[piece.shape[0] // 2 :] for piece in pieces], 0)
             for pieces in (cot_own[: gy // 2], cot_own[gy // 2 :])
         ]
-        *parts, tok_x = lax.optimization_barrier((*parts, tok_x))
+        *parts, tok_x[0] = lax.optimization_barrier((*parts, tok_x[0]))
         cot_other = [lax.ppermute(part, "gz", [(0, 1), (1, 0)]) for part in parts]
 
         sent, qkv_x = call(
-            x_forward_body,
+            lambda *refs: x_forward_body(line_shape, *refs),
             "x_forward",
             (flat, jax.ShapeDtypeStruct((count, 3 * dim), BF16)),
             [
+                vm((count, dim)),
                 vm((count, dim)),
                 vm((count, dim)),
                 vm((dim, 3 * dim)),
                 vm((dim, dim)),
                 pltpu.SemaphoreType.DMA((2,)),
             ],
-            (pick([inverse(o) for o in out_orders], half), tok_x, gain_x, w_qkv_x, w_out_x),
+            (pick([inverse(o) for o in out_orders], half), gain_x, w_qkv_x, w_out_x, *tok_x),
             vmem_mib=52,
-            in_hbm=(3, 4),
+            in_hbm=(2, 3),
             flops=3 * 10**9,
         )
         sent, cot_other[0] = lax.optimization_barrier((sent, cot_other[0]))
@@ -437,7 +526,8 @@
                 vm((dim, dim)),
                 vm((dim, hidden)),
                 vm((hidden, dim)),
-                pltpu.SemaphoreType.DMA((4,)),
+                pltpu.SemaphoreType.DMA((2,)),
+                pltpu.SemaphoreType.DMA((2,)),
             ],
             (
                 pick([inverse(o) for o in y_orders], mine),
@@ -456,34 +546,33 @@
         ).reshape(count, dim)
 
         gt_sent = call(
-            x_back_body,
+            lambda *refs: x_back_body(line_shape, len(tok_x), *refs),
             "x_back",
-            jax.ShapeDtypeStruct(tok_x.shape, BF16),
+            [block] * gx,
             [
+                vm((count, dim)),
+                vm((count, dim)),
                 vm((count, dim)),
                 vm((count, dim)),
                 vm((count, 3 * dim)),
                 vm((count, dim), F32),
-                vm(tok_x.shape),
                 vm((count, 3 * dim)),
                 vm((dim, 3 * dim)),
                 vm((dim, dim)),
-                pltpu.SemaphoreType.DMA((4,)),
+                pltpu.SemaphoreType.DMA((3 + len(tok_x),)),
             ],
-            (pick(out_orders, half), g1_x, tok_x, qkv_x, gain_x, w_qkv_x, w_out_x),
+            (pick(out_orders, half), g1_x, qkv_x, gain_x, w_qkv_x, w_out_x, *tok_x),
             vmem_mib=52,
-            in_hbm=(2, 3, 5, 6),
+            in_hbm=(2, 4, 5, *range(6, 6 + len(tok_x))),
             flops=3 * 10**9,
         )
-        gt = lax.all_to_all(
-            gt_sent.reshape(gx, count // gx, dim), ("gz", "gh"), 0, 0, tiled=True
-        ).reshape(count, dim)
+        gt = exchange(gt_sent, far_first)
         out = call(
-            pack_body,
+            lambda *refs: pack_body(tx, ty, tz, gh, *refs),
             "pack",
             jax.ShapeDtypeStruct((count * lane_blocks, 128), BF16),
-            [vm((count, dim))],
-            (row(slab_order), row(tok_order), gt),
+            [vm((count, dim)), vm((count, dim))],
+            tuple(gt),
             vmem_mib=10,
         )
         split = out.reshape(tx, ty, lane_blocks, tz, 128).transpose(0, 1, 3, 2, 4)

time: 102 us -> 99.4 us (0.975)
  blocking collectives: 17.5 us -> 0 us
  starting transfers between devices: 19.6 us -> 30.3 us
  waiting for transfers between devices: 31.8 us -> 37.8 us
  local copies, waits for them, and re-layouts: 3.9 us -> 2.54 us
    all_to_all x1 -> x0, blocking collectives: 17.5 us -> none  [local(): lax.all_to_all(gt_sent.reshape(gx, count // gx, dim), ('gz', 'gh'), 0, 0,...]
    ppermute x0 -> x7, starting transfers between devices: none -> 10.6 us  [exchange(): moved[k] = lax.ppermute(parts[k], ('gz', 'gh'), pairs)]
    ppermute x0 -> x7, waiting for transfers between devices: none -> 6.05 us  [exchange(): moved[k] = lax.ppermute(parts[k], ('gz', 'gh'), pairs)]
    unnamed x26 -> x18, local copies, waits for them, and re-layouts: 2.44 us -> 1.08 us
  transfers between devices with their start and end apart: 8 -> 15, of which waited for: 7 -> 11; matrix products, arithmetic and copies ran while one was open for 1% -> 1% of each run, Pallas kernels for 6% -> 6%
where the time goes in v4:
time: 99.4 us; the launch traced here: 98.9 us
  waiting for transfers between devices  37.8 us (38%)
  starting transfers between devices  30.3 us (30%)
  Pallas kernels  28.1 us (28%)
  local copies, waits for them, and re-layouts  2.54 us (3%)
    pallas_call x6, Pallas kernels, call(): pl.pallas_call(body, out_shape=outs, in_specs=[pl.BlockSpec(memory_space=...  28.1 us
    ppermute x7, starting transfers between devices, exchange(): moved[k] = lax.ppermute(parts[k], ('gz', 'gh'), pairs)  10.6 us
    all_to_all x1, waiting for transfers between devices, local(): lax.all_to_all(g1_sent.reshape(gh * gy, count // (gh * gy), dim), ('gy',...  9.26 us
    ppermute x2, waiting for transfers between devices, local(): cot_other = [lax.ppermute(part, 'gz', [(0, 1), (1, 0)]) for part in parts]  9.14 us
    all_to_all x1, starting transfers between devices, exchange(): moved = lax.all_to_all(whole, ('gz', 'gh'), 0, 0, tiled=True)  7.25 us
    ppermute x7, waiting for transfers between devices, exchange(): moved[k] = lax.ppermute(parts[k], ('gz', 'gh'), pairs)  6.05 us
    all_to_all x1, waiting for transfers between devices, exchange(): moved = lax.all_to_all(whole, ('gz', 'gh'), 0, 0, tiled=True)  5.56 us
    ppermute x3, waiting for transfers between devices, local(): lax.ppermute(cot_sent[k], 'gy', [(i, i ^ k) for i in range(gy)])  5.13 us
  transfers between devices with their start and end apart: 15, of which 11 were waited for; matrix products, arithmetic and copies ran while one was open for 1% of the time, Pallas kernels for 6%

profile of v4, /device:TPU:0, one launch (start us, length us, event | category | flops | bytes accessed | tf_op | source)
XLA Modules:
  0.0 98.9 jit_solution(367649563193338395)
XLA Ops:
  0.0 0.0 copy-start.1
  0.0 1.0 %copy-done.1 = bf16[16,16,2,512]{3,2,1,0:T(2,128)(2,1)S(1)} copy-done((bf16[16,16,2,512]{3,2,1,0:T(2,128)(2,1)S(1)}, bf16[16,16,2,512]{3,2,1,0:T(2,128)(2,1)}, u32[]{:S(2)}) %copy-start.1) | copy-done | bytes 524312
  1.0 0.0 copy-start.2
  1.0 1.5 %unpack_tokens.1 = bf16[512,512]{1,0:T(8,128)(2,1)} custom-call(bf16[2048,128]{1,0:T(8,128)(2,1)S(1)} %bitcast.38), custom_call_target="tpu_custom_call" | custom-call | flops 1000000000 | bytes 4000000 | tf_op jit(solution)/shard_map/unpack_tokens/pallas_call | solution.py:373
  2.6 7.3 %all-to-all-start = ((bf16[8,64,512]{2,1,0:T(8,128)(2,1)}), bf16[8,64,512]{2,1,0:T(8,128)(2,1)S(1)}, u32[]{:S(2)}, u32[]{:S(2)}) async-start(bf16[8,64,512]{2,1,0:T(8,128)(2,1)} %bitcast.12), calls=%async_computation | async-start | bytes 1048576 | tf_op jit(solution)/shard_map/all_to_all | solution.py:444
  9.8 0.7 dynamic-slice_bitcast_fusion.refs_0_
  10.5 0.0 copy-done.2
  10.5 0.0 copy-start.8
  10.5 0.7 unpack_cotangent.1
  11.2 0.0 copy-start.3
  11.3 0.0 copy-start.6
  11.3 1.6 %collective-permute-start.1 = (bf16[128,512]{1,0:T(8,128)(2,1)S(1)}, bf16[128,512]{1,0:T(8,128)(2,1)S(1)}, u32[]{:S(2)}, u32[]{:S(2)}) collective-permute-start(bf16[128,512]{1,0:T(8,128)(2,1)S(1)} %get-tuple-element.37), channel_id=1, source_target_pairs={{0,2},{1,3},{2,0},{3,1},{4,6},{5,7},{6,4},{7,5},{8,10},{9,11},{10,... | collective-permute-start | bytes 393224 | tf_op jit(solution)/shard_map/ppermute | solution.py:477
  12.9 0.0 collective-permute-start.2
  12.9 0.6 collective-permute-start
  13.5 0.0 copy-done.8
  13.6 3.3 %collective-permute-done.1.refs_7_ = bf16[128,512]{1,0:T(8,128)(2,1)S(1)} collective-permute-done((bf16[128,512]{1,0:T(8,128)(2,1)S(1)}, bf16[128,512]{1,0:T(8,128)(2,1)S(1)}, u32[]{:S(2)}, u32[]{:S(2)}) %collective-permute-start.1) | collective-permute-done | bytes 131104 | tf_op jit(solution)/shard_map/ppermute | solution.py:477
  16.8 1.9 %collective-permute-done.2.refs_8_ = bf16[128,512]{1,0:T(8,128)(2,1)S(1)} collective-permute-done((bf16[128,512]{1,0:T(8,128)(2,1)S(1)}, bf16[128,512]{1,0:T(8,128)(2,1)S(1)}, u32[]{:S(2)}, u32[]{:S(2)}) %collective-permute-start.2) | collective-permute-done | bytes 131104 | tf_op jit(solution)/shard_map/ppermute | solution.py:477
  18.7 0.0 collective-permute-done.refs_6_
  18.8 5.6 %all-to-all-done = bf16[8,64,512]{2,1,0:T(8,128)(2,1)S(1)} async-done(((bf16[8,64,512]{2,1,0:T(8,128)(2,1)}), bf16[8,64,512]{2,1,0:T(8,128)(2,1)S(1)}, u32[]{:S(2)}, u32[]{:S(2)}) %all-to-all-start) | async-done | bytes 524320 | tf_op jit(solution)/shard_map/all_to_all | solution.py:444
  24.3 0.0 copy-start
  24.3 0.1 collective-permute-start.3
  24.5 0.0 copy-done.3
  24.5 0.0 copy-done.6
  24.5 0.0 copy-start.4
  24.5 0.0 copy-start.5
  24.5 5.2 %x_forward.1 = (bf16[512,512]{1,0:T(8,128)(2,1)}, bf16[512,1536]{1,0:T(8,128)(2,1)}) custom-call(s32[1,512]{1,0:T(1,128)S(1)} %dynamic-slice_bitcast_fusion.1.refs_0_, f32[1,512]{1,0:T(1,128)S(1)} %bitcast.42, bf16[512,1536]{1,0:T(8,128)(2,1)} %refs_4_.1, bf16[512,512]{1,0:T(8,128)(2,1)S(1)} %copy-done.3, bf16[512,512]{1,0:T(8,128)(2,1)S(1)} %bitcast.34), custom_call_target="tpu_custom_call" | custom-call | flops 3000000000 | bytes 4000000 | tf_op jit(solution)/shard_map/x_forward/pallas_call | solution.py:373
  29.7 0.0 copy-done
  29.7 1.8 %collective-permute-done.3.refs_3_ = bf16[128,512]{1,0:T(8,128)(2,1)S(1)} collective-permute-done((bf16[128,512]{1,0:T(8,128)(2,1)S(1)}, bf16[128,512]{1,0:T(8,128)(2,1)S(1)}, u32[]{:S(2)}, u32[]{:S(2)}) %collective-permute-start.3) | collective-permute-done | bytes 131104 | tf_op jit(solution)/shard_map/ppermute | solution.py:485
  31.6 4.5 %all-to-all-start.1 = ((bf16[16,32,512]{2,1,0:T(8,128)(2,1)}), bf16[16,32,512]{2,1,0:T(8,128)(2,1)S(1)}, u32[]{:S(2)}, u32[]{:S(2)}) async-start(bf16[16,32,512]{2,1,0:T(8,128)(2,1)} %bitcast.14), calls=%async_computation.1 | async-start | bytes 1048576 | tf_op jit(solution)/shard_map/all_to_all | solution.py:505
  36.1 1.5 %collective-permute-start.4 = (bf16[128,512]{1,0:T(8,128)(2,1)S(1)}, bf16[128,512]{1,0:T(8,128)(2,1)S(1)}, u32[]{:S(2)}, u32[]{:S(2)}) collective-permute-start(bf16[128,512]{1,0:T(8,128)(2,1)S(1)} %pad_maximum_fusion.1), channel_id=1, source_target_pairs={{0,16},{16,0},{1,17},{17,1},{2,18},{18,2},{3,19},{19,3},{4,20},{20... | collective-permute-start | bytes 393224 | tf_op jit(solution)/shard_map/ppermute | solution.py:485
  37.5 0.7 dynamic-slice_bitcast_fusion.2
  38.2 7.3 %collective-permute-done.4.refs_4_ = bf16[128,512]{1,0:T(8,128)(2,1)S(1)} collective-permute-done((bf16[128,512]{1,0:T(8,128)(2,1)S(1)}, bf16[128,512]{1,0:T(8,128)(2,1)S(1)}, u32[]{:S(2)}, u32[]{:S(2)}) %collective-permute-start.4) | collective-permute-done | bytes 131104 | tf_op jit(solution)/shard_map/ppermute | solution.py:485
  45.5 2.6 %all-to-all-done.1 = bf16[16,32,512]{2,1,0:T(8,128)(2,1)S(1)} async-done(((bf16[16,32,512]{2,1,0:T(8,128)(2,1)}), bf16[16,32,512]{2,1,0:T(8,128)(2,1)S(1)}, u32[]{:S(2)}, u32[]{:S(2)}) %all-to-all-start.1) | async-done | bytes 524320 | tf_op jit(solution)/shard_map/all_to_all | solution.py:505
  48.2 0.0 copy-done.4
  48.2 0.0 copy-done.5
  48.2 0.0 copy-start.7
  48.2 13.7 %middle.1 = bf16[512,512]{1,0:T(8,128)(2,1)} custom-call(s32[1,512]{1,0:T(1,128)S(1)} %get-tuple-element.40.refs_0_, s32[1,512]{1,0:T(1,128)S(1)} %get-tuple-element.39.refs_1_, bf16[512,512]{1,0:T(8,128)(2,1)S(1)} %bitcast.36, bf16[128,512]{1,0:T(8,128)(2,1)S(1)} %collective-permute-done.3.refs_3_, bf16[128,512]{1,0:T(8,128)(2,1)S(1)} %collective-permute-done.4.refs_4_, ...), custom_call_target="tpu_custom_call" | custom-call | flops 8999999488 | bytes 4000000 | tf_op jit(solution)/shard_map/middle/pallas_call | solution.py:373
  61.8 4.1 %all-to-all-start.2 = ((bf16[16,32,512]{2,1,0:T(8,128)(2,1)}), bf16[16,32,512]{2,1,0:T(8,128)(2,1)S(1)}, u32[]{:S(2)}, u32[]{:S(2)}) async-start(bf16[16,32,512]{2,1,0:T(8,128)(2,1)} %bitcast.18), calls=%async_computation.2 | async-start | bytes 1048576 | tf_op jit(solution)/shard_map/all_to_all | solution.py:544
  65.9 0.0 copy-done.7
  66.0 9.3 %all-to-all-done.2 = bf16[16,32,512]{2,1,0:T(8,128)(2,1)S(1)} async-done(((bf16[16,32,512]{2,1,0:T(8,128)(2,1)}), bf16[16,32,512]{2,1,0:T(8,128)(2,1)S(1)}, u32[]{:S(2)}, u32[]{:S(2)}) %all-to-all-start.2) | async-done | bytes 524320 | tf_op jit(solution)/shard_map/all_to_all | solution.py:544
  75.2 5.3 %x_back.1 = (bf16[64,512]{1,0:T(8,128)(2,1)S(1)}, bf16[64,512]{1,0:T(8,128)(2,1)S(1)}, bf16[64,512]{1,0:T(8,128)(2,1)S(1)}, bf16[64,512]{1,0:T(8,128)(2,1)S(1)},...) custom-call(s32[1,512]{1,0:T(1,128)S(1)} %dynamic-slice_bitcast_fusi, ...), custom_call_target="tpu_custom_call" | custom-call | flops 3000000000 | bytes 4000000 | tf_op jit(solution)/shard_map/x_back/pallas_call | solution.py:373
  80.5 1.1 %collective-permute-start.10 = (bf16[64,512]{1,0:T(8,128)(2,1)S(1)}, bf16[64,512]{1,0:T(8,128)(2,1)S(1)}, u32[]{:S(2)}, u32[]{:S(2)}) collective-permute-start(bf16[64,512]{1,0:T(8,128)(2,1)S(1)} %get-tuple-element.33), channel_id=1, source_target_pairs={{0,24},{4,28},{8,16},{12,20},{16,8},{20,12},{24,0},{28,4},{1,25},{... | collective-permute-start | bytes 196616 | tf_op jit(solution)/shard_map/ppermute | solution.py:449
  81.6 3.6 %collective-permute-start.11 = (bf16[64,512]{1,0:T(8,128)(2,1)S(1)}, bf16[64,512]{1,0:T(8,128)(2,1)S(1)}, u32[]{:S(2)}, u32[]{:S(2)}) collective-permute-start(bf16[64,512]{1,0:T(8,128)(2,1)S(1)} %get-tuple-element.34), channel_id=1, source_target_pairs={{0,28},{4,24},{8,20},{12,16},{16,12},{20,8},{24,4},{28,0},{1,29},{... | collective-permute-start | bytes 196616 | tf_op jit(solution)/shard_map/ppermute | solution.py:449
  85.2 0.7 collective-permute-start.5
  85.9 0.0 collective-permute-start.6
  85.9 2.8 %collective-permute-start.7 = (bf16[64,512]{1,0:T(8,128)(2,1)S(1)}, bf16[64,512]{1,0:T(8,128)(2,1)S(1)}, u32[]{:S(2)}, u32[]{:S(2)}) collective-permute-start(bf16[64,512]{1,0:T(8,128)(2,1)S(1)} %get-tuple-element.30), channel_id=1, source_target_pairs={{0,12},{4,8},{8,4},{12,0},{16,28},{20,24},{24,20},{28,16},{1,13},{... | collective-permute-start | bytes 196616 | tf_op jit(solution)/shard_map/ppermute | solution.py:449
  88.7 0.0 collective-permute-done.10.refs_6_
  88.7 0.0 collective-permute-start.8
  88.7 0.6 collective-permute-done.11.refs_7_
  89.3 2.5 %collective-permute-start.9 = (bf16[64,512]{1,0:T(8,128)(2,1)S(1)}, bf16[64,512]{1,0:T(8,128)(2,1)S(1)}, u32[]{:S(2)}, u32[]{:S(2)}) collective-permute-start(bf16[64,512]{1,0:T(8,128)(2,1)S(1)} %get-tuple-element.32), channel_id=1, source_target_pairs={{0,20},{4,16},{8,28},{12,24},{16,4},{20,0},{24,12},{28,8},{1,21},{... | collective-permute-start | bytes 196616 | tf_op jit(solution)/shard_map/ppermute | solution.py:449
  91.8 0.0 collective-permute-done.5.refs_1_
  91.8 0.0 collective-permute-done.6.refs_2_
  91.8 0.3 collective-permute-done.7.refs_3_
  92.0 3.1 %collective-permute-done.8.refs_4_ = bf16[64,512]{1,0:T(8,128)(2,1)S(1)} collective-permute-done((bf16[64,512]{1,0:T(8,128)(2,1)S(1)}, bf16[64,512]{1,0:T(8,128)(2,1)S(1)}, u32[]{:S(2)}, u32[]{:S(2)}) %collective-permute-start.8) | collective-permute-done | bytes 65568 | tf_op jit(solution)/shard_map/ppermute | solution.py:449
  95.2 2.1 %collective-permute-done.9.refs_5_ = bf16[64,512]{1,0:T(8,128)(2,1)S(1)} collective-permute-done((bf16[64,512]{1,0:T(8,128)(2,1)S(1)}, bf16[64,512]{1,0:T(8,128)(2,1)S(1)}, u32[]{:S(2)}, u32[]{:S(2)}) %collective-permute-start.9) | collective-permute-done | bytes 65568 | tf_op jit(solution)/shard_map/ppermute | solution.py:449
  97.2 1.6 %pack.1 = bf16[2048,128]{1,0:T(8,128)(2,1)} custom-call(bf16[64,512]{1,0:T(8,128)(2,1)S(1)} %get-tuple-element.27.refs_0_, bf16[64,512]{1,0:T(8,128)(2,1)S(1)} %collective-permute-done.5.refs_1_, bf16[64,512]{1,0:T(8,128)(2,1)S(1)} %collective-permute-done.6.refs_2_, bf16[64,512]{1,0:T(8,128)(2,1)S(1)} %collective-permute-done.7.refs_3_, ...), custom_call_target="tpu_custom_call" | custom-call | flops 1000000000 | bytes 4000000 | tf_op jit(solution)/shard_map/pack/pallas_call | solution.py:373
  (9 shorter events, 0.1 us)
Async XLA Ops:
  0.0 1.0 %copy-start.1 = (bf16[16,16,2,512]{3,2,1,0:T(2,128)(2,1)S(1)}, bf16[16,16,2,512]{3,2,1,0:T(2,128)(2,1)}, u32[]{:S(2)}) copy-start(bf16[16,16,2,512]{3,2,1,0:T(2,128)(2,1)} %param.16) | copy-start | bytes 1572868
  1.0 9.5 %copy-start.2 = (bf16[16,16,2,512]{3,2,1,0:T(2,128)(2,1)S(1)}, bf16[16,16,2,512]{3,2,1,0:T(2,128)(2,1)}, u32[]{:S(2)}) copy-start(bf16[16,16,2,512]{3,2,1,0:T(2,128)(2,1)} %param.17) | copy-start | bytes 1572868
  2.6 21.7 %all-to-all-start = ((bf16[8,64,512]{2,1,0:T(8,128)(2,1)}), bf16[8,64,512]{2,1,0:T(8,128)(2,1)S(1)}, u32[]{:S(2)}, u32[]{:S(2)}) async-start(bf16[8,64,512]{2,1,0:T(8,128)(2,1)} %bitcast.12), calls=%async_computation | async-start | bytes 1048576 | tf_op jit(solution)/shard_map/all_to_all | solution.py:444
  10.5 3.0 %copy-start.8 = (s32[2,1,512]{2,1,0:T(1,128)S(1)}, s32[2,1,512]{2,1,0:T(1,128)}, u32[]{:S(2)}) copy-start(s32[2,1,512]{2,1,0:T(1,128)} %constant.42.clone) | copy-start | bytes 12292
  11.2 13.2 %copy-start.3 = (bf16[512,512]{1,0:T(8,128)(2,1)S(1)}, bf16[512,512]{1,0:T(8,128)(2,1)}, u32[]{:S(2)}) copy-start(bf16[512,512]{1,0:T(8,128)(2,1)} %refs_5_.1) | copy-start | bytes 1572868
  11.3 13.2 %copy-start.6 = (f32[512]{0:T(512)S(1)}, f32[512]{0:T(512)}, u32[]{:S(2)}) copy-start(f32[512]{0:T(512)} %param.18) | copy-start | bytes 6148
  11.3 5.5 %collective-permute-start.1 = (bf16[128,512]{1,0:T(8,128)(2,1)S(1)}, bf16[128,512]{1,0:T(8,128)(2,1)S(1)}, u32[]{:S(2)}, u32[]{:S(2)}) collective-permute-start(bf16[128,512]{1,0:T(8,128)(2,1)S(1)} %get-tuple-element.37), channel_id=1, source_target_pairs={{0,2},{1,3},{2,0},{3,1},{4,6},{5,7},{6,4},{7,5},{8,10},{9,11},{10,... | collective-permute-start | bytes 393224 | tf_op jit(solution)/shard_map/ppermute | solution.py:477
  12.9 5.8 %collective-permute-start.2 = (bf16[128,512]{1,0:T(8,128)(2,1)S(1)}, bf16[128,512]{1,0:T(8,128)(2,1)S(1)}, u32[]{:S(2)}, u32[]{:S(2)}) collective-permute-start(bf16[128,512]{1,0:T(8,128)(2,1)S(1)} %get-tuple-element.36), channel_id=1, source_target_pairs={{0,3},{1,2},{2,1},{3,0},{4,7},{5,6},{6,5},{7,4},{8,11},{9,10},{10,... | collective-permute-start | bytes 393224 | tf_op jit(solution)/shard_map/ppermute | solution.py:477
  12.9 5.8 %collective-permute-start = (bf16[128,512]{1,0:T(8,128)(2,1)S(1)}, bf16[128,512]{1,0:T(8,128)(2,1)S(1)}, u32[]{:S(2)}, u32[]{:S(2)}) collective-permute-start(bf16[128,512]{1,0:T(8,128)(2,1)S(1)} %get-tuple-element.38), channel_id=1, source_target_pairs={{0,1},{1,0},{2,3},{3,2},{4,5},{5,4},{6,7},{7,6},{8,9},{9,8},{10,11... | collective-permute-start | bytes 393224 | tf_op jit(solution)/shard_map/ppermute | solution.py:477
  24.3 5.4 %copy-start = (bf16[8,64,512]{2,1,0:T(8,128)(2,1)}, bf16[8,64,512]{2,1,0:T(8,128)(2,1)S(1)}, u32[]{:S(2)}) copy-start(bf16[8,64,512]{2,1,0:T(8,128)(2,1)S(1)} %all-to-all-done) | copy-start | bytes 1572868
  24.3 7.3 %collective-permute-start.3 = (bf16[128,512]{1,0:T(8,128)(2,1)S(1)}, bf16[128,512]{1,0:T(8,128)(2,1)S(1)}, u32[]{:S(2)}, u32[]{:S(2)}) collective-permute-start(bf16[128,512]{1,0:T(8,128)(2,1)S(1)} %pad_maximum_fusion), channel_id=1, source_target_pairs={{0,16},{16,0},{1,17},{17,1},{2,18},{18,2},{3,19},{19,3},{4,20},{20... | collective-permute-start | bytes 393224 | tf_op jit(solution)/shard_map/ppermute | solution.py:485
  24.5 23.7 %copy-start.4 = (f32[512]{0:T(512)S(1)}, f32[512]{0:T(512)}, u32[]{:S(2)}) copy-start(f32[512]{0:T(512)} %param.21) | copy-start | bytes 6148
  24.5 23.7 %copy-start.5 = (f32[512]{0:T(512)S(1)}, f32[512]{0:T(512)}, u32[]{:S(2)}) copy-start(f32[512]{0:T(512)} %param.24) | copy-start | bytes 6148
  31.6 16.6 %all-to-all-start.1 = ((bf16[16,32,512]{2,1,0:T(8,128)(2,1)}), bf16[16,32,512]{2,1,0:T(8,128)(2,1)S(1)}, u32[]{:S(2)}, u32[]{:S(2)}) async-start(bf16[16,32,512]{2,1,0:T(8,128)(2,1)} %bitcast.14), calls=%async_computation.1 | async-start | bytes 1048576 | tf_op jit(solution)/shard_map/all_to_all | solution.py:505
  36.1 9.5 %collective-permute-start.4 = (bf16[128,512]{1,0:T(8,128)(2,1)S(1)}, bf16[128,512]{1,0:T(8,128)(2,1)S(1)}, u32[]{:S(2)}, u32[]{:S(2)}) collective-permute-start(bf16[128,512]{1,0:T(8,128)(2,1)S(1)} %pad_maximum_fusion.1), channel_id=1, source_target_pairs={{0,16},{16,0},{1,17},{17,1},{2,18},{18,2},{3,19},{19,3},{4,20},{20... | collective-permute-start | bytes 393224 | tf_op jit(solution)/shard_map/ppermute | solution.py:485
  48.2 17.8 %copy-start.7 = (s32[2,1,512]{2,1,0:T(1,128)S(1)}, s32[2,1,512]{2,1,0:T(1,128)}, u32[]{:S(2)}) copy-start(s32[2,1,512]{2,1,0:T(1,128)} %constant.45.clone) | copy-start | bytes 12292
  61.8 13.4 %all-to-all-start.2 = ((bf16[16,32,512]{2,1,0:T(8,128)(2,1)}), bf16[16,32,512]{2,1,0:T(8,128)(2,1)S(1)}, u32[]{:S(2)}, u32[]{:S(2)}) async-start(bf16[16,32,512]{2,1,0:T(8,128)(2,1)} %bitcast.18), calls=%async_computation.2 | async-start | bytes 1048576 | tf_op jit(solution)/shard_map/all_to_all | solution.py:544
  80.5 8.2 %collective-permute-start.10 = (bf16[64,512]{1,0:T(8,128)(2,1)S(1)}, bf16[64,512]{1,0:T(8,128)(2,1)S(1)}, u32[]{:S(2)}, u32[]{:S(2)}) collective-permute-start(bf16[64,512]{1,0:T(8,128)(2,1)S(1)} %get-tuple-element.33), channel_id=1, source_target_pairs={{0,24},{4,28},{8,16},{12,20},{16,8},{20,12},{24,0},{28,4},{1,25},{... | collective-permute-start | bytes 196616 | tf_op jit(solution)/shard_map/ppermute | solution.py:449
  81.6 7.6 %collective-permute-start.11 = (bf16[64,512]{1,0:T(8,128)(2,1)S(1)}, bf16[64,512]{1,0:T(8,128)(2,1)S(1)}, u32[]{:S(2)}, u32[]{:S(2)}) collective-permute-start(bf16[64,512]{1,0:T(8,128)(2,1)S(1)} %get-tuple-element.34), channel_id=1, source_target_pairs={{0,28},{4,24},{8,20},{12,16},{16,12},{20,8},{24,4},{28,0},{1,29},{... | collective-permute-start | bytes 196616 | tf_op jit(solution)/shard_map/ppermute | solution.py:449
  85.2 6.5 %collective-permute-start.5 = (bf16[64,512]{1,0:T(8,128)(2,1)S(1)}, bf16[64,512]{1,0:T(8,128)(2,1)S(1)}, u32[]{:S(2)}, u32[]{:S(2)}) collective-permute-start(bf16[64,512]{1,0:T(8,128)(2,1)S(1)} %get-tuple-element.28), channel_id=1, source_target_pairs={{0,4},{4,0},{8,12},{12,8},{16,20},{20,16},{24,28},{28,24},{1,5},{5... | collective-permute-start | bytes 196616 | tf_op jit(solution)/shard_map/ppermute | solution.py:449
  85.9 5.9 %collective-permute-start.6 = (bf16[64,512]{1,0:T(8,128)(2,1)S(1)}, bf16[64,512]{1,0:T(8,128)(2,1)S(1)}, u32[]{:S(2)}, u32[]{:S(2)}) collective-permute-start(bf16[64,512]{1,0:T(8,128)(2,1)S(1)} %get-tuple-element.29), channel_id=1, source_target_pairs={{0,8},{4,12},{8,0},{12,4},{16,24},{20,28},{24,16},{28,20},{1,9},{5... | collective-permute-start | bytes 196616 | tf_op jit(solution)/shard_map/ppermute | solution.py:449
  85.9 6.1 %collective-permute-start.7 = (bf16[64,512]{1,0:T(8,128)(2,1)S(1)}, bf16[64,512]{1,0:T(8,128)(2,1)S(1)}, u32[]{:S(2)}, u32[]{:S(2)}) collective-permute-start(bf16[64,512]{1,0:T(8,128)(2,1)S(1)} %get-tuple-element.30), channel_id=1, source_target_pairs={{0,12},{4,8},{8,4},{12,0},{16,28},{20,24},{24,20},{28,16},{1,13},{... | collective-permute-start | bytes 196616 | tf_op jit(solution)/shard_map/ppermute | solution.py:449
  88.7 6.5 %collective-permute-start.8 = (bf16[64,512]{1,0:T(8,128)(2,1)S(1)}, bf16[64,512]{1,0:T(8,128)(2,1)S(1)}, u32[]{:S(2)}, u32[]{:S(2)}) collective-permute-start(bf16[64,512]{1,0:T(8,128)(2,1)S(1)} %get-tuple-element.31), channel_id=1, source_target_pairs={{0,16},{4,20},{8,24},{12,28},{16,0},{20,4},{24,8},{28,12},{1,17},{... | collective-permute-start | bytes 196616 | tf_op jit(solution)/shard_map/ppermute | solution.py:449
  89.3 8.0 %collective-permute-start.9 = (bf16[64,512]{1,0:T(8,128)(2,1)S(1)}, bf16[64,512]{1,0:T(8,128)(2,1)S(1)}, u32[]{:S(2)}, u32[]{:S(2)}) collective-permute-start(bf16[64,512]{1,0:T(8,128)(2,1)S(1)} %get-tuple-element.32), channel_id=1, source_target_pairs={{0,20},{4,16},{8,28},{12,24},{16,4},{20,0},{24,12},{28,8},{1,21},{... | collective-permute-start | bytes 196616 | tf_op jit(solution)/shard_map/ppermute | solution.py:449

commit v5 on v3

v5 whole, which is shorter than its diff:
```python
import jax
import jax.numpy as jnp
import numpy as np
from jax import lax
from jax.experimental import pallas as pl
from jax.experimental.pallas import tpu as pltpu
from jax.sharding import Mesh
from jax.sharding import PartitionSpec as P

HEADS = 8
NZ = 2
EPS = 1e-05
F32 = jnp.float32
BF16 = jnp.bfloat16
MIB = 1024 * 1024


def dot(a, b):
    return jnp.dot(a, b, preferred_element_type=F32)


def dot_t(a, b):
    return lax.dot_general(a, b, (((1,), (1,)), ((), ())), preferred_element_type=F32)


def dot_lt(a, b):
    return lax.dot_general(a, b, (((0,), (0,)), ((), ())), preferred_element_type=F32)


def one_hot(target):
    size = target.shape[1]
    rows = lax.broadcasted_iota(jnp.int32, (size, size), 0)
    return jnp.where(rows == target, 1.0, 0.0).astype(BF16)


def digits(*sizes):
    count = 1
    for size in sizes:
        count *= size
    values = lax.broadcasted_iota(jnp.int32, (1, count), 1)
    found = []
    for size in reversed(sizes):
        if size & (size - 1) == 0:
            found.append(values & (size - 1))
            values = values >> (size.bit_length() - 1)
        else:
            found.append(lax.rem(values, size))
            values = lax.div(values, size)
    return found[::-1]


def gx_index(count):
    return lax.axis_index("gz") * (count // NZ) + lax.axis_index("gh")


def rows_at(start, size):
    return pl.ds(pl.multiple_of(start, size), size)


def standardize(x):
    centred = x - jnp.mean(x, -1, keepdims=True)
    inv = lax.rsqrt(jnp.mean(centred * centred, -1, keepdims=True) + EPS)
    return centred * inv, inv


def norm_back(x, gain, grad):
    unit, inv = standardize(x)
    scaled = grad * gain
    return inv * (
        scaled
        - jnp.mean(scaled, -1, keepdims=True)
        - unit * jnp.mean(scaled * unit, -1, keepdims=True)
    )


def group_of(length):
    return 4 if length * 4 <= 256 and HEADS % 4 == 0 else 2


def spread(block, count):
    width = block.shape[1] // count
    lane = lax.broadcasted_iota(jnp.int32, block.shape, 1)
    zero = jnp.zeros_like(block)
    return jnp.concatenate(
        [
            jnp.where((lane >= i * width) & (lane < (i + 1) * width), block, zero)
            for i in range(count)
        ],
        0,
    )


def gather(block, count):
    rows = block.shape[0] // count
    width = block.shape[1] // count
    lane = lax.broadcasted_iota(jnp.int32, (rows, block.shape[1]), 1)
    result = block[:rows]
    for i in range(1, count):
        result = jnp.where(lane >= i * width, block[i * rows : (i + 1) * rows], result)
    return result


class Blocks:
    def __init__(self, count, dim, length):
        self.group = group_of(length)
        self.dim = dim
        self.width = dim // HEADS * self.group
        self.scale = (dim // HEADS) ** -0.5
        self.items = [
            (slice(i * length, (i + 1) * length), j)
            for i in range(count // length)
            for j in range(HEADS // self.group)
        ]

    def lanes(self, j, part=0):
        return slice(part * self.dim + j * self.width, part * self.dim + (j + 1) * self.width)

    def q_wide(self, qkv, rows, j):
        return spread(qkv[rows, self.lanes(j)] * jnp.array(self.scale, BF16), self.group)


def softmax_rows(scores):
    exponent = jnp.exp(scores - jnp.max(scores, 0, keepdims=True))
    return exponent * (1.0 / jnp.sum(exponent, 0, keepdims=True))


def attend(blocks, qkv, mixed, keep=None):
    scores = [
        dot_t(qkv[rows, blocks.lanes(j, 1)], blocks.q_wide(qkv, rows, j))
        for rows, j in blocks.items
    ]
    lows = []
    for i, score in enumerate(scores):
        probs = softmax_rows(score)
        if keep is not None:
            keep[i] = probs
        lows.append(probs.astype(BF16))
    for (rows, j), low in zip(blocks.items, lows):
        out = dot_lt(low, qkv[rows, blocks.lanes(j, 2)])
        mixed[rows, blocks.lanes(j)] = gather(out, blocks.group).astype(BF16)


def attend_back(blocks, qkv, grad, grad_qkv, kept=None):
    probs_all, g_probs_all = [], []
    for rows, j in blocks.items:
        if kept is None:
            probs_all.append(dot_t(qkv[rows, blocks.lanes(j, 1)], blocks.q_wide(qkv, rows, j)))
        g_wide = spread(grad[rows, blocks.lanes(j)], blocks.group)
        g_probs_all.append(dot_t(qkv[rows, blocks.lanes(j, 2)], g_wide))
    lows, g_scores_all = [], []
    for i, g_probs in enumerate(g_probs_all):
        probs = softmax_rows(probs_all[i]) if kept is None else kept[i]
        weighted = probs * g_probs
        total = jnp.sum(weighted, 0, keepdims=True)
        g_scores_all.append((weighted - probs * total).astype(BF16))
        lows.append(probs.astype(BF16))
    for (rows, j), low, g_scores in zip(blocks.items, lows, g_scores_all):
        g_q = gather(dot_lt(g_scores, qkv[rows, blocks.lanes(j, 1)]), blocks.group)
        grad_qkv[rows, blocks.lanes(j)] = (g_q * blocks.scale).astype(BF16)
        g_k = dot(g_scores, blocks.q_wide(qkv, rows, j))
        grad_qkv[rows, blocks.lanes(j, 1)] = g_k.astype(BF16)
        g_v = dot(low, spread(grad[rows, blocks.lanes(j)], blocks.group))
        grad_qkv[rows, blocks.lanes(j, 2)] = g_v.astype(BF16)


def fetch(sems, *pairs):
    copies = [
        pltpu.make_async_copy(source, target, sems.at[i])
        for i, (source, target) in enumerate(pairs)
    ]
    for copy in copies:
        copy.start()
    return copies


def column_thirds(source, target):
    dim = source.shape[1] // 3
    cols = [pl.ds(j * dim, dim) for j in range(3)]
    return [(source.at[:, c], target.at[:, c]) for c in cols]


def project_qkv(normed, copies, w_qkv, qkv):
    dim = w_qkv.shape[0]
    for j in range(3):
        if j > 0:
            copies[j].wait()
        cols = slice(j * dim, (j + 1) * dim)
        qkv[:, cols] = dot(normed[...], w_qkv[:, cols]).astype(BF16)


def block_targets(whole, count):
    size = whole.shape[0] // count
    me = gx_index(count)
    return [whole.at[rows_at((me ^ k) * size, size)] for k in range(count)]


class Tile:
    def __init__(self, tx, ty, tz, dim):
        self.tx, self.ty, self.tz, self.blocks = tx, ty, tz, dim // 128
        self.run = 2 * self.blocks * tz

    def pick(self):
        x, y, c, z = digits(self.tx, 2, self.blocks, self.tz)
        return one_hot(((c * self.tz + z) * 2 + y) * self.tx + x)

    def packed_rows(self, j):
        starts = [(x * self.ty + 2 * j) * self.blocks * self.tz for x in range(self.tx)]
        return [slice(s, s + self.run) for s in starts]

    def places(self, j):
        return [
            (
                slice((z * self.ty + 2 * j + y) * self.tx, (z * self.ty + 2 * j + y + 1) * self.tx),
                slice(c * 128, (c + 1) * 128),
            )
            for c in range(self.blocks)
            for z in range(self.tz)
            for y in range(2)
        ]


def unpack_tokens_body(tile, packed, out):
    pick = tile.pick()
    for j in range(tile.ty // 2):
        slab = jnp.concatenate([packed[rows, :] for rows in tile.packed_rows(j)], 0)
        found = dot(pick, slab).astype(BF16)
        for i, (rows, lanes) in enumerate(tile.places(j)):
            out[rows, lanes] = found[i * tile.tx : (i + 1) * tile.tx]


def pack_body(tile, *refs):
    *parts, packed, whole = refs
    for part, target in zip(parts, block_targets(whole, len(parts))):
        target[...] = part[...]
    pick = tile.pick()
    for j in range(tile.ty // 2):
        slab = jnp.concatenate([whole[rows, lanes] for rows, lanes in tile.places(j)], 0)
        found = dot_lt(pick, slab).astype(BF16)
        for i, rows in enumerate(tile.packed_rows(j)):
            packed[rows, :] = found[i * tile.run : (i + 1) * tile.run]


def unpack_cotangent_body(tz, target, packed, out, rows):
    blocks = rows.shape[1] // 128
    step = 32 * tz
    slab = step * blocks
    place, block, z = digits(32, blocks, tz)
    pick = one_hot(block * step + place * tz + z)
    for s in range(packed.shape[0] // slab):
        found = dot(pick, packed[s * slab : (s + 1) * slab, :]).astype(BF16)
        for c in range(blocks):
            rows[s * step : (s + 1) * step, c * 128 : (c + 1) * 128] = found[
                c * step : (c + 1) * step
            ]
    out[...] = dot(one_hot(target[...]), rows[...]).astype(BF16)


class XLines:
    def __init__(self, lines, gh, gy, tx):
        self.lines, self.gh, self.gy, self.tx = lines, gh, gy, tx
        self.own = tx // gy
        self.chunk = lines * NZ * self.own
        self.small = self.chunk % 16 != 0 or tx % 16 != 0

    def pick_all(self):
        y, t, r, g, x = digits(self.lines, NZ, self.gh, self.gy, self.own)
        first = t ^ lax.axis_index("gz")
        return one_hot((((g * self.gh + r) * self.lines + y) * NZ + first) * self.own + x)

    def pick(self):
        y, t, g, x = digits(self.lines, NZ, self.gy, self.own)
        return one_hot(((g * self.lines + y) * NZ + t) * self.own + x)

    def line_runs(self, r):
        half = lax.axis_index("gz")
        return [
            rows_at(((y * NZ + (t ^ half)) * self.gh + r) * self.tx, self.tx)
            for y in range(self.lines)
            for t in range(NZ)
        ]

    def sent_runs(self, r):
        starts = [(g * self.gh + r) * self.chunk for g in range(self.gy)]
        return [slice(s, s + self.chunk) for s in starts]

    def send(self, source, sent):
        if self.small:
            sent[...] = dot(self.pick_all(), source[...]).astype(BF16)
            return
        pick = self.pick()
        for r in range(self.gh):
            block = jnp.concatenate([source[rows, :] for rows in self.line_runs(r)], 0)
            found = dot(pick, block).astype(BF16)
            for i, rows in enumerate(self.sent_runs(r)):
                sent[rows, :] = found[i * self.chunk : (i + 1) * self.chunk]

    def receive(self, sent, target):
        if self.small:
            target[...] = dot_lt(self.pick_all(), sent[...]).astype(BF16)
            return
        pick = self.pick()
        for r in range(self.gh):
            block = jnp.concatenate([sent[rows, :] for rows in self.sent_runs(r)], 0)
            found = dot_lt(pick, block).astype(BF16)
            for i, rows in enumerate(self.line_runs(r)):
                target[rows, :] = found[i * self.tx : (i + 1) * self.tx]


class YLines:
    def __init__(self, gy, ty, lines):
        self.gy, self.ty, self.lines = gy, ty, lines
        self.size = ty * lines

    def pick(self):
        y, x = digits(self.ty, self.lines)
        return one_hot(x * self.ty + y)

    def blocks(self):
        me = lax.axis_index("gy")
        for k in range(self.gy):
            starts = [(x * self.gy + k) * self.ty for x in range(self.lines)]
            runs = [slice(s, s + self.ty) for s in starts]
            yield rows_at((me ^ k) * self.size, self.size), runs

    def receive(self, sent, target):
        pick = self.pick()
        for rows, runs in self.blocks():
            found = dot(pick, sent[rows, :]).astype(BF16)
            for i, run in enumerate(runs):
                target[run, :] = found[i * self.ty : (i + 1) * self.ty]

    def send(self, source, sent):
        pick = self.pick()
        for rows, runs in self.blocks():
            block = jnp.concatenate([source[run, :] for run in runs], 0)
            sent[rows, :] = dot_lt(pick, block).astype(BF16)


def x_forward_body(
    shape, lines_x, gain, w_qkv_hbm, w_out_hbm, tok_flat, sent, qkv, normed, mixed, w_qkv, w_out,
    sems,
):
    copies = fetch(sems, *column_thirds(w_qkv_hbm, w_qkv), (w_out_hbm, w_out))
    tok = tok_flat.reshape(shape)
    blocks, lines, part, dim = shape
    length = blocks * part
    for i in range(lines):
        x = tok[:, i].reshape(length, dim).astype(F32)
        unit, _ = standardize(x)
        normed[i * length : (i + 1) * length, :] = (unit * gain[...]).astype(BF16)
    copies[0].wait()
    project_qkv(normed, copies, w_qkv, qkv)
    attend(Blocks(normed.shape[0], dim, length), qkv, mixed)
    copies[3].wait()
    out = dot(mixed[...], w_out[...])
    for i in range(lines):
        rows = slice(i * length, (i + 1) * length)
        x = tok[:, i].reshape(length, dim).astype(F32)
        normed[rows, :] = (x + out[rows]).astype(BF16)
    lines_x.send(normed, sent)


def grad_act_body(gather_rows, inputs, *refs):
    parts = refs[:inputs]
    w_down, cot, g_act = refs[inputs:]
    for rows, part, start in gather_rows:
        cot[rows, :] = parts[part][start : start + rows.stop - rows.start, :]
    g_act[...] = dot_t(cot[...], w_down[...]).astype(BF16)


def middle_body(
    lines_y, s1_in, cot_own, cot_other, g_own_hbm, g_other_hbm, gain_y, gain_m,
    w_qkv_hbm, w_out_hbm, w_up_hbm, sent,
    s1, cot, normed, qkv, mixed, s2, probs, acc, grad, grad_qkv, g_act, g_pre,
    w_qkv, w_out, w_up, sems, late_sems,
):
    copies = fetch(sems, *column_thirds(w_qkv_hbm, w_qkv), (w_out_hbm, w_out))
    count, dim = s1.shape
    hidden = w_up.shape[1]
    length = lines_y.gy * lines_y.ty
    half = count // 2
    lines_y.receive(s1_in, s1)
    unit, _ = standardize(s1[...].astype(F32))
    normed[...] = (unit * gain_y[...]).astype(BF16)
    copies[0].wait()
    late = fetch(
        late_sems,
        (w_up_hbm, w_up),
        (g_own_hbm, g_act.at[pl.ds(0, half)]),
        (g_other_hbm, g_act.at[pl.ds(half, half)]),
    )
    project_qkv(normed, copies, w_qkv, qkv)
    blocks = Blocks(count, dim, length)
    attend(blocks, qkv, mixed, probs)
    copies[3].wait()
    low = (s1[...].astype(F32) + dot(mixed[...], w_out[...])).astype(BF16)
    s2[...] = low
    unit, _ = standardize(low.astype(F32))
    normed[...] = (unit * gain_m[...]).astype(BF16)
    cot[:half, :] = cot_own[...]
    cot[half:, :] = cot_other[...]

    for copy in late:
        copy.wait()
    chunk = 256 if hidden % 256 == 0 else hidden
    c0 = 0.7978845608028654
    c1 = 0.044715
    for c in range(hidden // chunk):
        cols = slice(c * chunk, (c + 1) * chunk)
        pre = dot(normed[...], w_up[:, cols])
        square = pre * pre
        tanh = jnp.tanh(pre * (c0 + (c0 * c1) * square))
        twice = (1.0 + tanh) * (1.0 + (pre - pre * tanh) * (c0 + (3 * c0 * c1) * square))
        g_pre[:, cols] = ((0.5 * g_act[:, cols].astype(F32)) * twice).astype(BF16)
    acc[...] = dot_t(g_pre[...], w_up[...])

    back = norm_back(s2[...].astype(F32), gain_m[...], acc[...])
    cot[...] = (cot[...].astype(F32) + back).astype(BF16)
    grad[...] = dot_t(cot[...], w_out[...]).astype(BF16)
    attend_back(blocks, qkv, grad, grad_qkv, probs)
    acc[...] = dot_t(grad_qkv[...], w_qkv[...])
    back = norm_back(s1[...].astype(F32), gain_y[...], acc[...])
    normed[...] = (cot[...].astype(F32) + back).astype(BF16)
    lines_y.send(normed, sent)


def x_back_body(
    shape, lines_x, g1_in, qkv_hbm, gain, w_qkv_hbm, w_out_hbm, tok_hbm, *refs
):
    *outs, tok_flat, sent, g1, grad, grad_qkv, acc, qkv, w_qkv, w_out, sems, late_sems = refs
    copies = fetch(sems, (w_out_hbm, w_out), (qkv_hbm, qkv))
    blocks, lines, part, dim = shape
    length = blocks * part
    tok = tok_flat.reshape(shape)
    sent_lines = sent.reshape(shape)
    lines_x.receive(g1_in, g1)
    copies[0].wait()
    late = fetch(late_sems, (w_qkv_hbm, w_qkv), (tok_hbm, tok_flat))
    grad[...] = dot_t(g1[...], w_out[...]).astype(BF16)
    copies[1].wait()
    attend_back(Blocks(g1.shape[0], dim, length), qkv, grad, grad_qkv)
    for copy in late:
        copy.wait()
    acc[...] = dot_t(grad_qkv[...], w_qkv[...])
    for i in range(lines):
        rows = slice(i * length, (i + 1) * length)
        x = tok[:, i].reshape(length, dim).astype(F32)
        total = g1[rows, :].astype(F32) + norm_back(x, gain[...], acc[rows, :])
        sent_lines[:, i] = total.astype(BF16).reshape(blocks, part, dim)
    for source, out in zip(block_targets(sent, len(outs)), outs):
        out[...] = source[...]


def call(body, name, outs, scratch, args, vmem_mib, in_hbm=(), flops=10**9):
    vmem = pl.BlockSpec(memory_space=pltpu.VMEM)
    anywhere = pl.BlockSpec(memory_space=pl.ANY)
    return pl.pallas_call(
        body,
        out_shape=outs,
        in_specs=[anywhere if i in in_hbm else vmem for i in range(len(args))],
        scratch_shapes=scratch,
        compiler_params=pltpu.CompilerParams(vmem_limit_bytes=int(vmem_mib * MIB)),
        cost_estimate=pl.CostEstimate(flops=flops, bytes_accessed=4000000, transcendentals=0),
        name=name,
    )(*args)


def inverse(order):
    result = np.empty_like(order)
    result[order] = np.arange(order.size, dtype=order.dtype)
    return result


def make_local(gh, gy):
    gx = NZ * gh

    def local(
        tokens, cotangent, gain_x, w_qkv_x, w_out_x, gain_y, w_qkv_y, w_out_y, gain_mlp, w_up,
        w_down,
    ):
        tx, ty, tz, dim = tokens.shape
        hidden = w_up.shape[1]
        count = tx * ty * tz
        y_lines = ty // gh
        own = tx // gy
        x_lines = tz * own
        len_x, len_y = tx * gx, ty * gy
        line_shape = (gx, y_lines, tx, dim)
        tile = Tile(tx, ty, tz, dim)
        lines_x = XLines(y_lines, gh, gy, tx)
        lines_y = YLines(gy, ty, x_lines)
        flat = jax.ShapeDtypeStruct((count, dim), BF16)
        gain_x, gain_y, gain_mlp = (g.reshape(1, dim) for g in (gain_x, gain_y, gain_mlp))

        def vm(shape, dtype=BF16):
            return pltpu.VMEM(shape, dtype)

        def packed(array):
            split = array.reshape(tx, ty, tz, tile.blocks, 128).transpose(0, 1, 3, 2, 4)
            return split.reshape(count * tile.blocks, 128)

        def exchange(array, axes, parts):
            whole = array.reshape(parts, count // parts, dim)
            return lax.all_to_all(whole, axes, 0, 0, tiled=True).reshape(count, dim)

        tok_sent = call(
            lambda *refs: unpack_tokens_body(tile, *refs),
            "unpack_tokens",
            flat,
            [],
            (packed(tokens),),
            vmem_mib=10,
        )
        tok_x = exchange(tok_sent, ("gz", "gh"), gx)

        tile_row = np.arange(count).reshape(gy, own, ty, tz).transpose(0, 3, 1, 2)
        targets = []
        for z in range(NZ):
            for g in range(gy):
                order = tile_row[[g ^ k for k in range(gy)]][:, [z, 1 - z]].reshape(-1)
                targets.append(inverse(order).astype(np.int32).reshape(1, -1))
        target = lax.dynamic_index_in_dim(
            jnp.asarray(np.stack(targets)),
            lax.axis_index("gz") * gy + lax.axis_index("gy"),
            keepdims=False,
        )
        cot_sent = call(
            lambda *refs: unpack_cotangent_body(tz, *refs),
            "unpack_cotangent",
            flat,
            [vm((count, dim))],
            (target, packed(cotangent)),
            vmem_mib=10,
        ).reshape(gy, count // gy, dim)
        cot_own = [cot_sent[0]] + [
            lax.ppermute(cot_sent[k], "gy", [(i, i ^ k) for i in range(gy)])
            for k in range(1, gy)
        ]
        near = gy // 2
        parts = [
            jnp.concatenate([piece[piece.shape[0] // 2 :] for piece in pieces], 0)
            for pieces in (cot_own[:near], cot_own[near:])
        ]
        *parts, tok_x = lax.optimization_barrier((*parts, tok_x))
        cot_other = [lax.ppermute(part, "gz", [(0, 1), (1, 0)]) for part in parts]

        sent, qkv_x = call(
            lambda *refs: x_forward_body(line_shape, lines_x, *refs),
            "x_forward",
            (flat, jax.ShapeDtypeStruct((count, 3 * dim), BF16)),
            [
                vm((count, dim)),
                vm((count, dim)),
                vm((dim, 3 * dim)),
                vm((dim, dim)),
                pltpu.SemaphoreType.DMA((4,)),
            ],
            (gain_x, w_qkv_x, w_out_x, tok_x),
            vmem_mib=52,
            in_hbm=(1, 2),
            flops=3 * 10**9,
        )
        sent, cot_other[0] = lax.optimization_barrier((sent, cot_other[0]))
        s1_y = exchange(sent, ("gy", "gh"), gh * gy)

        def line_run(i, k):
            return slice((i * gy + k) * ty, (i * gy + k + 1) * ty)

        def grad_act(name, pieces, gather_rows):
            half = jax.ShapeDtypeStruct((count // 2, dim), BF16)
            return call(
                lambda *refs: grad_act_body(gather_rows, len(pieces), *refs),
                name,
                (half, jax.ShapeDtypeStruct((count // 2, hidden), BF16)),
                [],
                (*pieces, w_down),
                vmem_mib=16,
            )

        own_runs = [(line_run(i, k), k, i * ty) for i in range(own) for k in range(gy)]
        other_runs = [
            (line_run(i, k), k // near, (k % near * own + i) * ty)
            for i in range(own)
            for k in range(gy)
        ]
        cot_a, g_act_a = grad_act("grad_act_own", cot_own, own_runs)
        cot_b, g_act_b = grad_act("grad_act_other", cot_other, other_runs)

        group = group_of(len_y)
        g1_sent = call(
            lambda *refs: middle_body(lines_y, *refs),
            "middle",
            flat,
            [
                vm((count, dim)),
                vm((count, dim)),
                vm((count, dim)),
                vm((count, 3 * dim)),
                vm((count, dim)),
                vm((count, dim)),
                vm((x_lines * HEADS // group, len_y, group * len_y), F32),
                vm((count, dim), F32),
                vm((count, dim)),
                vm((count, 3 * dim)),
                vm((count, hidden)),
                vm((count, hidden)),
                vm((dim, 3 * dim)),
                vm((dim, dim)),
                vm((dim, hidden)),
                pltpu.SemaphoreType.DMA((4,)),
                pltpu.SemaphoreType.DMA((3,)),
            ],
            (
                s1_y, cot_a, cot_b, g_act_a, g_act_b, gain_y, gain_mlp,
                w_qkv_y, w_out_y, w_up,
            ),
            vmem_mib=52,
            in_hbm=(3, 4, 7, 8, 9),
            flops=9 * 10**9,
        )
        g1_x = exchange(g1_sent, ("gy", "gh"), gh * gy)

        gt_parts = call(
            lambda *refs: x_back_body(line_shape, lines_x, *refs),
            "x_back",
            [jax.ShapeDtypeStruct((count // gx, dim), BF16)] * gx,
            [
                vm((count, dim)),
                vm((count, dim)),
                vm((count, dim)),
                vm((count, dim)),
                vm((count, 3 * dim)),
                vm((count, dim), F32),
                vm((count, 3 * dim)),
                vm((dim, 3 * dim)),
                vm((dim, dim)),
                pltpu.SemaphoreType.DMA((2,)),
                pltpu.SemaphoreType.DMA((2,)),
            ],
            (g1_x, qkv_x, gain_x, w_qkv_x, w_out_x, tok_x),
            vmem_mib=52,
            in_hbm=(1, 3, 4, 5),
            flops=3 * 10**9,
        )
        gt = list(gt_parts)
        for k in [*range(gh, gx), *range(1, gh)]:
            gt[k] = lax.ppermute(gt[k], ("gz", "gh"), [(i, i ^ k) for i in range(gx)])
        out = call(
            lambda *refs: pack_body(tile, *refs),
            "pack",
            jax.ShapeDtypeStruct((count * tile.blocks, 128), BF16),
            [vm((count, dim))],
            tuple(gt),
            vmem_mib=10,
        )
        split = out.reshape(tx, ty, tile.blocks, tz, 128).transpose(0, 1, 3, 2, 4)
        return split.reshape(tx, ty, tz, dim)

    return local


def solution(mesh):
    gx, gy = mesh.shape["gx"], mesh.shape["gy"]
    halved = Mesh(mesh.devices.reshape(NZ, gx // NZ, gy), ("gz", "gh", "gy"))
    tile = P(("gz", "gh"), "gy", None, None)
    return jax.shard_map(
        make_local(gx // NZ, gy),
        mesh=halved,
        in_specs=(tile, tile) + (P(),) * 9,
        out_specs=tile,
        check_vma=False,
    )
```

time: 102 us -> 97.6 us (0.957)
  waiting for transfers between devices: 31.8 us -> 23.1 us
  starting transfers between devices: 19.6 us -> 26.5 us
  blocking collectives: 17.5 us -> 14.9 us
    all_to_all x3 -> x2, waiting for transfers between devices: 17.4 us -> 4.43 us  [exchange(): return lax.all_to_all(whole, axes, 0, 0, tiled=True).reshape(count, dim)]
    ppermute x0 -> x7, starting transfers between devices: none -> 11.2 us  [local(): gt[k] = lax.ppermute(gt[k], ('gz', 'gh'), [(i, i ^ k) for i in range(gx)])]
    ppermute x0 -> x7, waiting for transfers between devices: none -> 4.81 us  [local(): gt[k] = lax.ppermute(gt[k], ('gz', 'gh'), [(i, i ^ k) for i in range(gx)])]
    all_to_all x3 -> x2, starting transfers between devices: 15.8 us -> 11.7 us  [exchange(): return lax.all_to_all(whole, axes, 0, 0, tiled=True).reshape(count, dim)]
    all_to_all x1, blocking collectives: 17.5 us -> 14.9 us  [exchange(): return lax.all_to_all(whole, axes, 0, 0, tiled=True).reshape(count, dim)]
    ppermute x2, waiting for transfers between devices: 9.19 us -> 7.09 us  [local(): cot_other = [lax.ppermute(part, 'gz', [(0, 1), (1, 0)]) for part in parts]]
    unnamed x26 -> x22, local copies, waits for them, and re-layouts: 2.44 us -> 4.1 us
    ppermute x3, waiting for transfers between devices: 5.13 us -> 6.73 us  [local(): lax.ppermute(cot_sent[k], 'gy', [(i, i ^ k) for i in range(gy)])]
  transfers between devices with their start and end apart: 8 -> 14, of which waited for: 7 -> 8; matrix products, arithmetic and copies ran while one was open for 1% -> 1% of each run, Pallas kernels for 6% -> 8%
where the time goes in v5:
time: 97.6 us; the launch traced here: 97.2 us
  Pallas kernels  27.1 us (28%)
  starting transfers between devices  26.5 us (27%)
  waiting for transfers between devices  23.1 us (24%)
  blocking collectives  14.9 us (15%)
  local copies, waits for them, and re-layouts  4.84 us (5%)
    pallas_call x8, Pallas kernels, call(): pl.pallas_call(body, out_shape=outs, in_specs=[anywhere if i in in_hbm el...  27.1 us
    all_to_all x1, blocking collectives, exchange(): return lax.all_to_all(whole, axes, 0, 0, tiled=True).reshape(count, dim)  14.9 us
    all_to_all x2, starting transfers between devices, exchange(): return lax.all_to_all(whole, axes, 0, 0, tiled=True).reshape(count, dim)  11.7 us
    ppermute x7, starting transfers between devices, local(): gt[k] = lax.ppermute(gt[k], ('gz', 'gh'), [(i, i ^ k) for i in range(gx)])  11.2 us
    ppermute x2, waiting for transfers between devices, local(): cot_other = [lax.ppermute(part, 'gz', [(0, 1), (1, 0)]) for part in parts]  7.09 us
    ppermute x3, waiting for transfers between devices, local(): lax.ppermute(cot_sent[k], 'gy', [(i, i ^ k) for i in range(gy)])  6.73 us
    ppermute x7, waiting for transfers between devices, local(): gt[k] = lax.ppermute(gt[k], ('gz', 'gh'), [(i, i ^ k) for i in range(gx)])  4.81 us
    all_to_all x2, waiting for transfers between devices, exchange(): return lax.all_to_all(whole, axes, 0, 0, tiled=True).reshape(count, dim)  4.43 us
  transfers between devices with their start and end apart: 14, of which 8 were waited for; matrix products, arithmetic and copies ran while one was open for 1% of the time, Pallas kernels for 8%

profile of v5, /device:TPU:0, one launch (start us, length us, event | category | flops | bytes accessed | tf_op | source)
XLA Modules:
  0.0 97.2 jit_solution(13867173063420764384)
XLA Ops:
  0.0 0.0 copy-start.2
  0.0 1.0 %copy-done.2 = bf16[16,16,2,512]{3,2,1,0:T(2,128)(2,1)S(1)} copy-done((bf16[16,16,2,512]{3,2,1,0:T(2,128)(2,1)S(1)}, bf16[16,16,2,512]{3,2,1,0:T(2,128)(2,1)}, u32[]{:S(2)}) %copy-start.2) | copy-done | bytes 524312
  1.0 0.0 copy-start.3
  1.0 1.2 %unpack_tokens.1 = bf16[512,512]{1,0:T(8,128)(2,1)} custom-call(bf16[2048,128]{1,0:T(8,128)(2,1)S(1)} %bitcast.31), custom_call_target="tpu_custom_call" | custom-call | flops 1000000000 | bytes 4000000 | tf_op jit(solution)/shard_map/unpack_tokens/pallas_call | solution.py:457
  2.3 7.3 %all-to-all-start = ((bf16[8,64,512]{2,1,0:T(8,128)(2,1)}), bf16[8,64,512]{2,1,0:T(8,128)(2,1)S(1)}, u32[]{:S(2)}, u32[]{:S(2)}) async-start(bf16[8,64,512]{2,1,0:T(8,128)(2,1)} %bitcast.8), calls=%async_computation | async-start | bytes 1048576 | tf_op jit(solution)/shard_map/all_to_all | solution.py:504
  9.5 0.7 dynamic-slice_bitcast_fusion.refs_0_
  10.2 0.0 copy-done.3
  10.2 0.7 unpack_cotangent.1
  10.9 0.0 copy-start.8
  11.0 0.7 collective-permute-start.2
  11.7 0.9 collective-permute-start.1
  12.7 0.3 collective-permute-start
  12.9 3.9 %collective-permute-done.2.refs_3_ = bf16[128,512]{1,0:T(8,128)(2,1)S(1)} collective-permute-done((bf16[128,512]{1,0:T(8,128)(2,1)S(1)}, bf16[128,512]{1,0:T(8,128)(2,1)S(1)}, u32[]{:S(2)}, u32[]{:S(2)}) %collective-permute-start.2) | collective-permute-done | bytes 131104 | tf_op jit(solution)/shard_map/ppermute | solution.py:536
  16.8 2.9 %collective-permute-done.1.refs_2_ = bf16[128,512]{1,0:T(8,128)(2,1)S(1)} collective-permute-done((bf16[128,512]{1,0:T(8,128)(2,1)S(1)}, bf16[128,512]{1,0:T(8,128)(2,1)S(1)}, u32[]{:S(2)}, u32[]{:S(2)}) %collective-permute-start.1) | collective-permute-done | bytes 131104 | tf_op jit(solution)/shard_map/ppermute | solution.py:536
  19.7 0.0 collective-permute-done.refs_1_
  19.7 0.7 pad_maximum_fusion.1
  20.4 3.6 %all-to-all-done = bf16[8,64,512]{2,1,0:T(8,128)(2,1)S(1)} async-done(((bf16[8,64,512]{2,1,0:T(8,128)(2,1)}), bf16[8,64,512]{2,1,0:T(8,128)(2,1)S(1)}, u32[]{:S(2)}, u32[]{:S(2)}) %all-to-all-start) | async-done | bytes 524320 | tf_op jit(solution)/shard_map/all_to_all | solution.py:504
  24.0 0.0 copy-start
  24.0 0.1 collective-permute-start.3
  24.2 0.0 copy-done.8
  24.2 0.0 copy-start.4
  24.2 1.1 %copy-done.4 = bf16[512,512]{1,0:T(8,128)(2,1)S(1)} copy-done((bf16[512,512]{1,0:T(8,128)(2,1)S(1)}, bf16[512,512]{1,0:T(8,128)(2,1)}, u32[]{:S(2)}) %copy-start.4) | copy-done | bytes 524312
  25.2 0.0 copy-start.1
  25.2 5.3 %x_forward.1 = (bf16[512,512]{1,0:T(8,128)(2,1)}, bf16[512,1536]{1,0:T(8,128)(2,1)}) custom-call(f32[1,512]{1,0:T(1,128)S(1)} %bitcast.35, bf16[512,1536]{1,0:T(8,128)(2,1)} %refs_3_.1, bf16[512,512]{1,0:T(8,128)(2,1)S(1)} %copy-done.4, bf16[512,512]{1,0:T(8,128)(2,1)S(1)} %bitcast.26), custom_call_target="tpu_custom_call" | custom-call | flops 3000000000 | bytes 4000000 | tf_op jit(solution)/shard_map/x_forward/pallas_call | solution.py:457
  30.5 0.0 copy-done
  30.5 0.7 collective-permute-done.3.refs_0_
  31.3 4.5 %all-to-all-start.1 = ((bf16[16,32,512]{2,1,0:T(8,128)(2,1)}), bf16[16,32,512]{2,1,0:T(8,128)(2,1)S(1)}, u32[]{:S(2)}, u32[]{:S(2)}) async-start(bf16[16,32,512]{2,1,0:T(8,128)(2,1)} %bitcast.10), calls=%async_computation.1 | async-start | bytes 1048576 | tf_op jit(solution)/shard_map/all_to_all | solution.py:504
  35.8 1.5 %collective-permute-start.4 = (bf16[128,512]{1,0:T(8,128)(2,1)}, bf16[128,512]{1,0:T(8,128)(2,1)S(1)}, u32[]{:S(2)}, u32[]{:S(2)}) collective-permute-start(bf16[128,512]{1,0:T(8,128)(2,1)} %pad_maximum_fusion.1), channel_id=1, source_target_pairs={{0,16},{16,0},{1,17},{17,1},{2,18},{18,2},{3,19},{19,3},{4,20},{20... | collective-permute-start | bytes 393224 | tf_op jit(solution)/shard_map/ppermute | solution.py:545
  37.2 0.0 copy-done.1
  37.2 0.7 grad_act_own.1
  38.0 0.0 copy-start.9
  38.0 1.0 %copy-done.9 = bf16[256,2048]{1,0:T(8,128)(2,1)} copy-done((bf16[256,2048]{1,0:T(8,128)(2,1)}, bf16[256,2048]{1,0:T(8,128)(2,1)S(1)}, u32[]{:S(2)}) %copy-start.9) | copy-done | bytes 1048600
  39.0 0.0 copy-start.6
  39.0 0.0 copy-start.7
  39.0 6.4 %collective-permute-done.4.refs_1_ = bf16[128,512]{1,0:T(8,128)(2,1)S(1)} collective-permute-done((bf16[128,512]{1,0:T(8,128)(2,1)}, bf16[128,512]{1,0:T(8,128)(2,1)S(1)}, u32[]{:S(2)}, u32[]{:S(2)}) %collective-permute-start.4) | collective-permute-done | bytes 131104 | tf_op jit(solution)/shard_map/ppermute | solution.py:545
  45.3 0.7 grad_act_other.1
  46.1 0.0 copy-start.10
  46.1 1.0 %copy-done.10 = bf16[256,2048]{1,0:T(8,128)(2,1)} copy-done((bf16[256,2048]{1,0:T(8,128)(2,1)}, bf16[256,2048]{1,0:T(8,128)(2,1)S(1)}, u32[]{:S(2)}) %copy-start.10) | copy-done | bytes 1048600
  47.1 0.8 all-to-all-done.1
  47.9 0.0 copy-done.6
  47.9 0.0 copy-done.7
  47.9 0.0 copy-start.5
  47.9 11.7 %middle.1 = bf16[512,512]{1,0:T(8,128)(2,1)S(1)} custom-call(bf16[512,512]{1,0:T(8,128)(2,1)S(1)} %bitcast.28, bf16[256,512]{1,0:T(8,128)(2,1)S(1)} %get-tuple-element.28.refs_1_, bf16[256,512]{1,0:T(8,128)(2,1)S(1)} %get-tuple-element.31.refs_2_, bf16[256,2048]{1,0:T(8,128)(2,1)} %copy-done.9, bf16[256,2048]{1,0:T(8,128)(2,1)} %copy-done.10, ...), custom_call_target="tpu_custom_call" | custom-call | flops 8999999488 | bytes 4000000 | tf_op jit(solution)/shard_map/middle/pallas_call | solution.py:457
  59.6 14.9 %all_to_all.15 = bf16[16,32,512]{2,1,0:T(8,128)(2,1)S(1)} all-to-all(bf16[16,32,512]{2,1,0:T(8,128)(2,1)S(1)} %bitcast.30), channel_id=1, replica_groups=mesh['gz'=2,'gh'=4,'gy'=4] {'gy','gh'}, dimensions={0} | all-to-all | bytes 1048576 | tf_op jit(solution)/shard_map/all_to_all | solution.py:504
  74.5 0.0 copy-done.5
  74.5 5.4 %x_back.1 = (bf16[64,512]{1,0:T(8,128)(2,1)S(1)}, bf16[64,512]{1,0:T(8,128)(2,1)S(1)}, bf16[64,512]{1,0:T(8,128)(2,1)S(1)}, bf16[64,512]{1,0:T(8,128)(2,1)S(1)},...) custom-call(bf16[512,512]{1,0:T(8,128)(2,1)S(1)} %bitcast.29, ...), custom_call_target="tpu_custom_call" | custom-call | flops 3000000000 | bytes 4000000 | tf_op jit(solution)/shard_map/x_back/pallas_call | solution.py:457
  79.9 1.4 %collective-permute-start.5 = (bf16[64,512]{1,0:T(8,128)(2,1)S(1)}, bf16[64,512]{1,0:T(8,128)(2,1)S(1)}, u32[]{:S(2)}, u32[]{:S(2)}) collective-permute-start(bf16[64,512]{1,0:T(8,128)(2,1)S(1)} %get-tuple-element.36), channel_id=1, source_target_pairs={{0,4},{4,0},{8,12},{12,8},{16,20},{20,16},{24,28},{28,24},{1,5},{5... | collective-permute-start | bytes 196616 | tf_op jit(solution)/shard_map/ppermute | solution.py:647
  81.3 0.5 collective-permute-start.6
  81.8 1.6 %collective-permute-start.7 = (bf16[64,512]{1,0:T(8,128)(2,1)S(1)}, bf16[64,512]{1,0:T(8,128)(2,1)S(1)}, u32[]{:S(2)}, u32[]{:S(2)}) collective-permute-start(bf16[64,512]{1,0:T(8,128)(2,1)S(1)} %get-tuple-element.38), channel_id=1, source_target_pairs={{0,12},{4,8},{8,4},{12,0},{16,28},{20,24},{24,20},{28,16},{1,13},{... | collective-permute-start | bytes 196616 | tf_op jit(solution)/shard_map/ppermute | solution.py:647
  83.4 0.7 collective-permute-start.8
  84.1 3.0 %collective-permute-start.9 = (bf16[64,512]{1,0:T(8,128)(2,1)S(1)}, bf16[64,512]{1,0:T(8,128)(2,1)S(1)}, u32[]{:S(2)}, u32[]{:S(2)}) collective-permute-start(bf16[64,512]{1,0:T(8,128)(2,1)S(1)} %get-tuple-element.40), channel_id=1, source_target_pairs={{0,20},{4,16},{8,28},{12,24},{16,4},{20,0},{24,12},{28,8},{1,21},{... | collective-permute-start | bytes 196616 | tf_op jit(solution)/shard_map/ppermute | solution.py:647
  87.1 0.0 collective-permute-done.5.refs_1_
  87.1 0.6 collective-permute-start.10
  87.7 0.0 collective-permute-done.6.refs_2_
  87.7 3.3 %collective-permute-start.11 = (bf16[64,512]{1,0:T(8,128)(2,1)S(1)}, bf16[64,512]{1,0:T(8,128)(2,1)S(1)}, u32[]{:S(2)}, u32[]{:S(2)}) collective-permute-start(bf16[64,512]{1,0:T(8,128)(2,1)S(1)} %get-tuple-element.42), channel_id=1, source_target_pairs={{0,28},{4,24},{8,20},{12,16},{16,12},{20,8},{24,4},{28,0},{1,29},{... | collective-permute-start | bytes 196616 | tf_op jit(solution)/shard_map/ppermute | solution.py:647
  91.1 0.0 collective-permute-done.7.refs_3_
  91.1 2.3 %collective-permute-done.8.refs_4_ = bf16[64,512]{1,0:T(8,128)(2,1)S(1)} collective-permute-done((bf16[64,512]{1,0:T(8,128)(2,1)S(1)}, bf16[64,512]{1,0:T(8,128)(2,1)S(1)}, u32[]{:S(2)}, u32[]{:S(2)}) %collective-permute-start.8) | collective-permute-done | bytes 65568 | tf_op jit(solution)/shard_map/ppermute | solution.py:647
  93.4 2.5 %collective-permute-done.9.refs_5_ = bf16[64,512]{1,0:T(8,128)(2,1)S(1)} collective-permute-done((bf16[64,512]{1,0:T(8,128)(2,1)S(1)}, bf16[64,512]{1,0:T(8,128)(2,1)S(1)}, u32[]{:S(2)}, u32[]{:S(2)}) %collective-permute-start.9) | collective-permute-done | bytes 65568 | tf_op jit(solution)/shard_map/ppermute | solution.py:647
  95.9 0.0 collective-permute-done.10.refs_6_
  95.9 0.0 collective-permute-done.11.refs_7_
  95.9 1.3 %pack.1 = bf16[2048,128]{1,0:T(8,128)(2,1)} custom-call(bf16[64,512]{1,0:T(8,128)(2,1)S(1)} %get-tuple-element.35.refs_0_, bf16[64,512]{1,0:T(8,128)(2,1)S(1)} %collective-permute-done.5.refs_1_, bf16[64,512]{1,0:T(8,128)(2,1)S(1)} %collective-permute-done.6.refs_2_, bf16[64,512]{1,0:T(8,128)(2,1)S(1)} %collective-permute-done.7.refs_3_, ...), custom_call_target="tpu_custom_call" | custom-call | flops 1000000000 | bytes 4000000 | tf_op jit(solution)/shard_map/pack/pallas_call | solution.py:457
  (6 shorter events, 0.1 us)
Async XLA Ops:
  0.0 1.0 %copy-start.2 = (bf16[16,16,2,512]{3,2,1,0:T(2,128)(2,1)S(1)}, bf16[16,16,2,512]{3,2,1,0:T(2,128)(2,1)}, u32[]{:S(2)}) copy-start(bf16[16,16,2,512]{3,2,1,0:T(2,128)(2,1)} %param.12) | copy-start | bytes 1572868
  1.0 9.2 %copy-start.3 = (bf16[16,16,2,512]{3,2,1,0:T(2,128)(2,1)S(1)}, bf16[16,16,2,512]{3,2,1,0:T(2,128)(2,1)}, u32[]{:S(2)}) copy-start(bf16[16,16,2,512]{3,2,1,0:T(2,128)(2,1)} %param.13) | copy-start | bytes 1572868
  2.3 21.7 %all-to-all-start = ((bf16[8,64,512]{2,1,0:T(8,128)(2,1)}), bf16[8,64,512]{2,1,0:T(8,128)(2,1)S(1)}, u32[]{:S(2)}, u32[]{:S(2)}) async-start(bf16[8,64,512]{2,1,0:T(8,128)(2,1)} %bitcast.8), calls=%async_computation | async-start | bytes 1048576 | tf_op jit(solution)/shard_map/all_to_all | solution.py:504
  10.9 13.2 %copy-start.8 = (f32[512]{0:T(512)S(1)}, f32[512]{0:T(512)}, u32[]{:S(2)}) copy-start(f32[512]{0:T(512)} %param.14) | copy-start | bytes 6148
  11.0 5.8 %collective-permute-start.2 = (bf16[128,512]{1,0:T(8,128)(2,1)S(1)}, bf16[128,512]{1,0:T(8,128)(2,1)S(1)}, u32[]{:S(2)}, u32[]{:S(2)}) collective-permute-start(bf16[128,512]{1,0:T(8,128)(2,1)S(1)} %get-tuple-element.44), channel_id=1, source_target_pairs={{0,3},{1,2},{2,1},{3,0},{4,7},{5,6},{6,5},{7,4},{8,11},{9,10},{10,... | collective-permute-start | bytes 393224 | tf_op jit(solution)/shard_map/ppermute | solution.py:536
  11.7 7.9 %collective-permute-start.1 = (bf16[128,512]{1,0:T(8,128)(2,1)S(1)}, bf16[128,512]{1,0:T(8,128)(2,1)S(1)}, u32[]{:S(2)}, u32[]{:S(2)}) collective-permute-start(bf16[128,512]{1,0:T(8,128)(2,1)S(1)} %get-tuple-element.45), channel_id=1, source_target_pairs={{0,2},{1,3},{2,0},{3,1},{4,6},{5,7},{6,4},{7,5},{8,10},{9,11},{10,... | collective-permute-start | bytes 393224 | tf_op jit(solution)/shard_map/ppermute | solution.py:536
  12.7 7.0 %collective-permute-start = (bf16[128,512]{1,0:T(8,128)(2,1)S(1)}, bf16[128,512]{1,0:T(8,128)(2,1)S(1)}, u32[]{:S(2)}, u32[]{:S(2)}) collective-permute-start(bf16[128,512]{1,0:T(8,128)(2,1)S(1)} %get-tuple-element.46), channel_id=1, source_target_pairs={{0,1},{1,0},{2,3},{3,2},{4,5},{5,4},{6,7},{7,6},{8,9},{9,8},{10,11... | collective-permute-start | bytes 393224 | tf_op jit(solution)/shard_map/ppermute | solution.py:536
  24.0 6.5 %copy-start = (bf16[8,64,512]{2,1,0:T(8,128)(2,1)}, bf16[8,64,512]{2,1,0:T(8,128)(2,1)S(1)}, u32[]{:S(2)}) copy-start(bf16[8,64,512]{2,1,0:T(8,128)(2,1)S(1)} %all-to-all-done) | copy-start | bytes 1572868
  24.0 7.3 %collective-permute-start.3 = (bf16[128,512]{1,0:T(8,128)(2,1)S(1)}, bf16[128,512]{1,0:T(8,128)(2,1)S(1)}, u32[]{:S(2)}, u32[]{:S(2)}) collective-permute-start(bf16[128,512]{1,0:T(8,128)(2,1)S(1)} %pad_maximum_fusion), channel_id=1, source_target_pairs={{0,16},{16,0},{1,17},{17,1},{2,18},{18,2},{3,19},{19,3},{4,20},{20... | collective-permute-start | bytes 393224 | tf_op jit(solution)/shard_map/ppermute | solution.py:545
  24.2 1.1 %copy-start.4 = (bf16[512,512]{1,0:T(8,128)(2,1)S(1)}, bf16[512,512]{1,0:T(8,128)(2,1)}, u32[]{:S(2)}) copy-start(bf16[512,512]{1,0:T(8,128)(2,1)} %refs_4_.3) | copy-start | bytes 1572868
  25.2 12.0 %copy-start.1 = (bf16[2048,512]{1,0:T(8,128)(2,1)S(1)}, bf16[2048,512]{1,0:T(8,128)(2,1)}, u32[]{:S(2)}) copy-start(bf16[2048,512]{1,0:T(8,128)(2,1)} %refs_2_.3) | copy-start | bytes 6291460
  31.3 16.6 %all-to-all-start.1 = ((bf16[16,32,512]{2,1,0:T(8,128)(2,1)}), bf16[16,32,512]{2,1,0:T(8,128)(2,1)S(1)}, u32[]{:S(2)}, u32[]{:S(2)}) async-start(bf16[16,32,512]{2,1,0:T(8,128)(2,1)} %bitcast.10), calls=%async_computation.1 | async-start | bytes 1048576 | tf_op jit(solution)/shard_map/all_to_all | solution.py:504
  35.8 9.6 %collective-permute-start.4 = (bf16[128,512]{1,0:T(8,128)(2,1)}, bf16[128,512]{1,0:T(8,128)(2,1)S(1)}, u32[]{:S(2)}, u32[]{:S(2)}) collective-permute-start(bf16[128,512]{1,0:T(8,128)(2,1)} %pad_maximum_fusion.1), channel_id=1, source_target_pairs={{0,16},{16,0},{1,17},{17,1},{2,18},{18,2},{3,19},{19,3},{4,20},{20... | collective-permute-start | bytes 393224 | tf_op jit(solution)/shard_map/ppermute | solution.py:545
  38.0 1.0 %copy-start.9 = (bf16[256,2048]{1,0:T(8,128)(2,1)}, bf16[256,2048]{1,0:T(8,128)(2,1)S(1)}, u32[]{:S(2)}) copy-start(bf16[256,2048]{1,0:T(8,128)(2,1)S(1)} %get-tuple-element.32.refs_3_) | copy-start | bytes 3145732
  39.0 8.9 %copy-start.6 = (f32[512]{0:T(512)S(1)}, f32[512]{0:T(512)}, u32[]{:S(2)}) copy-start(f32[512]{0:T(512)} %param.17) | copy-start | bytes 6148
  39.0 8.9 %copy-start.7 = (f32[512]{0:T(512)S(1)}, f32[512]{0:T(512)}, u32[]{:S(2)}) copy-start(f32[512]{0:T(512)} %param.20) | copy-start | bytes 6148
  46.1 1.0 %copy-start.10 = (bf16[256,2048]{1,0:T(8,128)(2,1)}, bf16[256,2048]{1,0:T(8,128)(2,1)S(1)}, u32[]{:S(2)}) copy-start(bf16[256,2048]{1,0:T(8,128)(2,1)S(1)} %get-tuple-element.33.refs_4_) | copy-start | bytes 3145732
  47.9 26.6 %copy-start.5 = (bf16[512,512]{1,0:T(8,128)(2,1)S(1)}, bf16[512,512]{1,0:T(8,128)(2,1)}, u32[]{:S(2)}) copy-start(bf16[512,512]{1,0:T(8,128)(2,1)} %refs_4_.3) | copy-start | bytes 1572868
  79.9 7.3 %collective-permute-start.5 = (bf16[64,512]{1,0:T(8,128)(2,1)S(1)}, bf16[64,512]{1,0:T(8,128)(2,1)S(1)}, u32[]{:S(2)}, u32[]{:S(2)}) collective-permute-start(bf16[64,512]{1,0:T(8,128)(2,1)S(1)} %get-tuple-element.36), channel_id=1, source_target_pairs={{0,4},{4,0},{8,12},{12,8},{16,20},{20,16},{24,28},{28,24},{1,5},{5... | collective-permute-start | bytes 196616 | tf_op jit(solution)/shard_map/ppermute | solution.py:647
  81.3 6.5 %collective-permute-start.6 = (bf16[64,512]{1,0:T(8,128)(2,1)S(1)}, bf16[64,512]{1,0:T(8,128)(2,1)S(1)}, u32[]{:S(2)}, u32[]{:S(2)}) collective-permute-start(bf16[64,512]{1,0:T(8,128)(2,1)S(1)} %get-tuple-element.37), channel_id=1, source_target_pairs={{0,8},{4,12},{8,0},{12,4},{16,24},{20,28},{24,16},{28,20},{1,9},{5... | collective-permute-start | bytes 196616 | tf_op jit(solution)/shard_map/ppermute | solution.py:647
  81.8 9.3 %collective-permute-start.7 = (bf16[64,512]{1,0:T(8,128)(2,1)S(1)}, bf16[64,512]{1,0:T(8,128)(2,1)S(1)}, u32[]{:S(2)}, u32[]{:S(2)}) collective-permute-start(bf16[64,512]{1,0:T(8,128)(2,1)S(1)} %get-tuple-element.38), channel_id=1, source_target_pairs={{0,12},{4,8},{8,4},{12,0},{16,28},{20,24},{24,20},{28,16},{1,13},{... | collective-permute-start | bytes 196616 | tf_op jit(solution)/shard_map/ppermute | solution.py:647
  83.4 10.0 %collective-permute-start.8 = (bf16[64,512]{1,0:T(8,128)(2,1)S(1)}, bf16[64,512]{1,0:T(8,128)(2,1)S(1)}, u32[]{:S(2)}, u32[]{:S(2)}) collective-permute-start(bf16[64,512]{1,0:T(8,128)(2,1)S(1)} %get-tuple-element.39), channel_id=1, source_target_pairs={{0,16},{4,20},{8,24},{12,28},{16,0},{20,4},{24,8},{28,12},{1,17},{... | collective-permute-start | bytes 196616 | tf_op jit(solution)/shard_map/ppermute | solution.py:647
  84.1 11.8 %collective-permute-start.9 = (bf16[64,512]{1,0:T(8,128)(2,1)S(1)}, bf16[64,512]{1,0:T(8,128)(2,1)S(1)}, u32[]{:S(2)}, u32[]{:S(2)}) collective-permute-start(bf16[64,512]{1,0:T(8,128)(2,1)S(1)} %get-tuple-element.40), channel_id=1, source_target_pairs={{0,20},{4,16},{8,28},{12,24},{16,4},{20,0},{24,12},{28,8},{1,21},{... | collective-permute-start | bytes 196616 | tf_op jit(solution)/shard_map/ppermute | solution.py:647
  87.1 8.8 %collective-permute-start.10 = (bf16[64,512]{1,0:T(8,128)(2,1)S(1)}, bf16[64,512]{1,0:T(8,128)(2,1)S(1)}, u32[]{:S(2)}, u32[]{:S(2)}) collective-permute-start(bf16[64,512]{1,0:T(8,128)(2,1)S(1)} %get-tuple-element.41), channel_id=1, source_target_pairs={{0,24},{4,28},{8,16},{12,20},{16,8},{20,12},{24,0},{28,4},{1,25},{... | collective-permute-start | bytes 196616 | tf_op jit(solution)/shard_map/ppermute | solution.py:647
  87.7 8.1 %collective-permute-start.11 = (bf16[64,512]{1,0:T(8,128)(2,1)S(1)}, bf16[64,512]{1,0:T(8,128)(2,1)S(1)}, u32[]{:S(2)}, u32[]{:S(2)}) collective-permute-start(bf16[64,512]{1,0:T(8,128)(2,1)S(1)} %get-tuple-element.42), channel_id=1, source_target_pairs={{0,28},{4,24},{8,20},{12,16},{16,12},{20,8},{24,4},{28,0},{1,29},{... | collective-permute-start | bytes 196616 | tf_op jit(solution)/shard_map/ppermute | solution.py:647

commit v6 on v5

--- a/solution.py
+++ b/solution.py
@@ -8,6 +8,7 @@
 from jax.sharding import PartitionSpec as P
 
 HEADS = 8
+GROUP = 2
 NZ = 2
 EPS = 1e-05
 F32 = jnp.float32
@@ -73,10 +74,6 @@
     )
 
 
-def group_of(length):
-    return 4 if length * 4 <= 256 and HEADS % 4 == 0 else 2
-
-
 def spread(block, count):
     width = block.shape[1] // count
     lane = lax.broadcasted_iota(jnp.int32, block.shape, 1)
@@ -102,7 +99,7 @@
 
 class Blocks:
     def __init__(self, count, dim, length):
-        self.group = group_of(length)
+        self.group = GROUP
         self.dim = dim
         self.width = dim // HEADS * self.group
         self.scale = (dim // HEADS) ** -0.5
@@ -586,7 +583,6 @@
         cot_a, g_act_a = grad_act("grad_act_own", cot_own, own_runs)
         cot_b, g_act_b = grad_act("grad_act_other", cot_other, other_runs)
 
-        group = group_of(len_y)
         g1_sent = call(
             lambda *refs: middle_body(lines_y, *refs),
             "middle",
@@ -598,7 +594,7 @@
                 vm((count, 3 * dim)),
                 vm((count, dim)),
                 vm((count, dim)),
-                vm((x_lines * HEADS // group, len_y, group * len_y), F32),
+                vm((x_lines * HEADS // GROUP, len_y, GROUP * len_y), F32),
                 vm((count, dim), F32),
                 vm((count, dim)),
                 vm((count, 3 * dim)),

time: 97.6 us -> 96.9 us (level)
  no operation moved by 1% of the time
where the time goes in v6:
time: 96.9 us; the launch traced here: 96.5 us
  starting transfers between devices  26.5 us (27%)
  Pallas kernels  26.4 us (27%)
  waiting for transfers between devices  23.1 us (24%)
  blocking collectives  14.9 us (15%)
  local copies, waits for them, and re-layouts  4.84 us (5%)
    pallas_call x8, Pallas kernels, call(): pl.pallas_call(body, out_shape=outs, in_specs=[anywhere if i in in_hbm el...  26.4 us
    all_to_all x1, blocking collectives, exchange(): return lax.all_to_all(whole, axes, 0, 0, tiled=True).reshape(count, dim)  14.9 us
    all_to_all x2, starting transfers between devices, exchange(): return lax.all_to_all(whole, axes, 0, 0, tiled=True).reshape(count, dim)  11.7 us
    ppermute x7, starting transfers between devices, local(): gt[k] = lax.ppermute(gt[k], ('gz', 'gh'), [(i, i ^ k) for i in range(gx)])  11.2 us
    ppermute x2, waiting for transfers between devices, local(): cot_other = [lax.ppermute(part, 'gz', [(0, 1), (1, 0)]) for part in parts]  7.09 us
    ppermute x3, waiting for transfers between devices, local(): lax.ppermute(cot_sent[k], 'gy', [(i, i ^ k) for i in range(gy)])  6.73 us
    ppermute x7, waiting for transfers between devices, local(): gt[k] = lax.ppermute(gt[k], ('gz', 'gh'), [(i, i ^ k) for i in range(gx)])  4.82 us
    all_to_all x2, waiting for transfers between devices, exchange(): return lax.all_to_all(whole, axes, 0, 0, tiled=True).reshape(count, dim)  4.43 us
  transfers between devices with their start and end apart: 14, of which 8 were waited for; matrix products, arithmetic and copies ran while one was open for 1% of the time, Pallas kernels for 8%

profile of v6, /device:TPU:0, one launch (start us, length us, event | category | flops | bytes accessed | tf_op | source)
XLA Modules:
  0.0 96.5 jit_solution(2501765571742323406)
XLA Ops:
  0.0 0.0 copy-start.2
  0.0 1.0 %copy-done.2 = bf16[16,16,2,512]{3,2,1,0:T(2,128)(2,1)S(1)} copy-done((bf16[16,16,2,512]{3,2,1,0:T(2,128)(2,1)S(1)}, bf16[16,16,2,512]{3,2,1,0:T(2,128)(2,1)}, u32[]{:S(2)}) %copy-start.2) | copy-done | bytes 524312
  1.0 0.0 copy-start.3
  1.0 1.2 %unpack_tokens.1 = bf16[512,512]{1,0:T(8,128)(2,1)} custom-call(bf16[2048,128]{1,0:T(8,128)(2,1)S(1)} %bitcast.31), custom_call_target="tpu_custom_call" | custom-call | flops 1000000000 | bytes 4000000 | tf_op jit(solution)/shard_map/unpack_tokens/pallas_call | solution.py:454
  2.3 7.3 %all-to-all-start = ((bf16[8,64,512]{2,1,0:T(8,128)(2,1)}), bf16[8,64,512]{2,1,0:T(8,128)(2,1)S(1)}, u32[]{:S(2)}, u32[]{:S(2)}) async-start(bf16[8,64,512]{2,1,0:T(8,128)(2,1)} %bitcast.8), calls=%async_computation | async-start | bytes 1048576 | tf_op jit(solution)/shard_map/all_to_all | solution.py:501
  9.5 0.7 dynamic-slice_bitcast_fusion.refs_0_
  10.2 0.0 copy-done.3
  10.2 0.7 unpack_cotangent.1
  10.9 0.0 copy-start.8
  11.0 0.7 collective-permute-start.2
  11.7 0.9 collective-permute-start.1
  12.7 0.3 collective-permute-start
  12.9 3.9 %collective-permute-done.2.refs_3_ = bf16[128,512]{1,0:T(8,128)(2,1)S(1)} collective-permute-done((bf16[128,512]{1,0:T(8,128)(2,1)S(1)}, bf16[128,512]{1,0:T(8,128)(2,1)S(1)}, u32[]{:S(2)}, u32[]{:S(2)}) %collective-permute-start.2) | collective-permute-done | bytes 131104 | tf_op jit(solution)/shard_map/ppermute | solution.py:533
  16.8 2.9 %collective-permute-done.1.refs_2_ = bf16[128,512]{1,0:T(8,128)(2,1)S(1)} collective-permute-done((bf16[128,512]{1,0:T(8,128)(2,1)S(1)}, bf16[128,512]{1,0:T(8,128)(2,1)S(1)}, u32[]{:S(2)}, u32[]{:S(2)}) %collective-permute-start.1) | collective-permute-done | bytes 131104 | tf_op jit(solution)/shard_map/ppermute | solution.py:533
  19.7 0.0 collective-permute-done.refs_1_
  19.7 0.7 pad_maximum_fusion.1
  20.4 3.6 %all-to-all-done = bf16[8,64,512]{2,1,0:T(8,128)(2,1)S(1)} async-done(((bf16[8,64,512]{2,1,0:T(8,128)(2,1)}), bf16[8,64,512]{2,1,0:T(8,128)(2,1)S(1)}, u32[]{:S(2)}, u32[]{:S(2)}) %all-to-all-start) | async-done | bytes 524320 | tf_op jit(solution)/shard_map/all_to_all | solution.py:501
  24.0 0.0 copy-start
  24.0 0.1 collective-permute-start.3
  24.2 0.0 copy-done.8
  24.2 0.0 copy-start.4
  24.2 1.1 %copy-done.4 = bf16[512,512]{1,0:T(8,128)(2,1)S(1)} copy-done((bf16[512,512]{1,0:T(8,128)(2,1)S(1)}, bf16[512,512]{1,0:T(8,128)(2,1)}, u32[]{:S(2)}) %copy-start.4) | copy-done | bytes 524312
  25.2 0.0 copy-start.1
  25.2 5.3 %x_forward.1 = (bf16[512,512]{1,0:T(8,128)(2,1)}, bf16[512,1536]{1,0:T(8,128)(2,1)}) custom-call(f32[1,512]{1,0:T(1,128)S(1)} %bitcast.35, bf16[512,1536]{1,0:T(8,128)(2,1)} %refs_3_.1, bf16[512,512]{1,0:T(8,128)(2,1)S(1)} %copy-done.4, bf16[512,512]{1,0:T(8,128)(2,1)S(1)} %bitcast.26), custom_call_target="tpu_custom_call" | custom-call | flops 3000000000 | bytes 4000000 | tf_op jit(solution)/shard_map/x_forward/pallas_call | solution.py:454
  30.5 0.0 copy-done
  30.5 0.7 collective-permute-done.3.refs_0_
  31.3 4.5 %all-to-all-start.1 = ((bf16[16,32,512]{2,1,0:T(8,128)(2,1)}), bf16[16,32,512]{2,1,0:T(8,128)(2,1)S(1)}, u32[]{:S(2)}, u32[]{:S(2)}) async-start(bf16[16,32,512]{2,1,0:T(8,128)(2,1)} %bitcast.10), calls=%async_computation.1 | async-start | bytes 1048576 | tf_op jit(solution)/shard_map/all_to_all | solution.py:501
  35.8 1.5 %collective-permute-start.4 = (bf16[128,512]{1,0:T(8,128)(2,1)}, bf16[128,512]{1,0:T(8,128)(2,1)S(1)}, u32[]{:S(2)}, u32[]{:S(2)}) collective-permute-start(bf16[128,512]{1,0:T(8,128)(2,1)} %pad_maximum_fusion.1), channel_id=1, source_target_pairs={{0,16},{16,0},{1,17},{17,1},{2,18},{18,2},{3,19},{19,3},{4,20},{20... | collective-permute-start | bytes 393224 | tf_op jit(solution)/shard_map/ppermute | solution.py:542
  37.2 0.0 copy-done.1
  37.2 0.7 grad_act_own.1
  38.0 0.0 copy-start.9
  38.0 1.0 %copy-done.9 = bf16[256,2048]{1,0:T(8,128)(2,1)} copy-done((bf16[256,2048]{1,0:T(8,128)(2,1)}, bf16[256,2048]{1,0:T(8,128)(2,1)S(1)}, u32[]{:S(2)}) %copy-start.9) | copy-done | bytes 1048600
  39.0 0.0 copy-start.6
  39.0 0.0 copy-start.7
  39.0 6.4 %collective-permute-done.4.refs_1_ = bf16[128,512]{1,0:T(8,128)(2,1)S(1)} collective-permute-done((bf16[128,512]{1,0:T(8,128)(2,1)}, bf16[128,512]{1,0:T(8,128)(2,1)S(1)}, u32[]{:S(2)}, u32[]{:S(2)}) %collective-permute-start.4) | collective-permute-done | bytes 131104 | tf_op jit(solution)/shard_map/ppermute | solution.py:542
  45.3 0.7 grad_act_other.1
  46.1 0.0 copy-start.10
  46.1 1.0 %copy-done.10 = bf16[256,2048]{1,0:T(8,128)(2,1)} copy-done((bf16[256,2048]{1,0:T(8,128)(2,1)}, bf16[256,2048]{1,0:T(8,128)(2,1)S(1)}, u32[]{:S(2)}) %copy-start.10) | copy-done | bytes 1048600
  47.1 0.8 all-to-all-done.1
  47.9 0.0 copy-done.6
  47.9 0.0 copy-done.7
  47.9 0.0 copy-start.5
  47.9 11.0 %middle.1 = bf16[512,512]{1,0:T(8,128)(2,1)S(1)} custom-call(bf16[512,512]{1,0:T(8,128)(2,1)S(1)} %bitcast.28, bf16[256,512]{1,0:T(8,128)(2,1)S(1)} %get-tuple-element.28.refs_1_, bf16[256,512]{1,0:T(8,128)(2,1)S(1)} %get-tuple-element.31.refs_2_, bf16[256,2048]{1,0:T(8,128)(2,1)} %copy-done.9, bf16[256,2048]{1,0:T(8,128)(2,1)} %copy-done.10, ...), custom_call_target="tpu_custom_call" | custom-call | flops 8999999488 | bytes 4000000 | tf_op jit(solution)/shard_map/middle/pallas_call | solution.py:454
  58.9 14.9 %all_to_all.15 = bf16[16,32,512]{2,1,0:T(8,128)(2,1)S(1)} all-to-all(bf16[16,32,512]{2,1,0:T(8,128)(2,1)S(1)} %bitcast.30), channel_id=1, replica_groups=mesh['gz'=2,'gh'=4,'gy'=4] {'gy','gh'}, dimensions={0} | all-to-all | bytes 1048576 | tf_op jit(solution)/shard_map/all_to_all | solution.py:501
  73.8 0.0 copy-done.5
  73.8 5.4 %x_back.1 = (bf16[64,512]{1,0:T(8,128)(2,1)S(1)}, bf16[64,512]{1,0:T(8,128)(2,1)S(1)}, bf16[64,512]{1,0:T(8,128)(2,1)S(1)}, bf16[64,512]{1,0:T(8,128)(2,1)S(1)},...) custom-call(bf16[512,512]{1,0:T(8,128)(2,1)S(1)} %bitcast.29, ...), custom_call_target="tpu_custom_call" | custom-call | flops 3000000000 | bytes 4000000 | tf_op jit(solution)/shard_map/x_back/pallas_call | solution.py:454
  79.1 1.4 %collective-permute-start.5 = (bf16[64,512]{1,0:T(8,128)(2,1)S(1)}, bf16[64,512]{1,0:T(8,128)(2,1)S(1)}, u32[]{:S(2)}, u32[]{:S(2)}) collective-permute-start(bf16[64,512]{1,0:T(8,128)(2,1)S(1)} %get-tuple-element.36), channel_id=1, source_target_pairs={{0,4},{4,0},{8,12},{12,8},{16,20},{20,16},{24,28},{28,24},{1,5},{5... | collective-permute-start | bytes 196616 | tf_op jit(solution)/shard_map/ppermute | solution.py:643
  80.5 0.5 collective-permute-start.6
  81.1 1.6 %collective-permute-start.7 = (bf16[64,512]{1,0:T(8,128)(2,1)S(1)}, bf16[64,512]{1,0:T(8,128)(2,1)S(1)}, u32[]{:S(2)}, u32[]{:S(2)}) collective-permute-start(bf16[64,512]{1,0:T(8,128)(2,1)S(1)} %get-tuple-element.38), channel_id=1, source_target_pairs={{0,12},{4,8},{8,4},{12,0},{16,28},{20,24},{24,20},{28,16},{1,13},{... | collective-permute-start | bytes 196616 | tf_op jit(solution)/shard_map/ppermute | solution.py:643
  82.7 0.7 collective-permute-start.8
  83.4 3.0 %collective-permute-start.9 = (bf16[64,512]{1,0:T(8,128)(2,1)S(1)}, bf16[64,512]{1,0:T(8,128)(2,1)S(1)}, u32[]{:S(2)}, u32[]{:S(2)}) collective-permute-start(bf16[64,512]{1,0:T(8,128)(2,1)S(1)} %get-tuple-element.40), channel_id=1, source_target_pairs={{0,20},{4,16},{8,28},{12,24},{16,4},{20,0},{24,12},{28,8},{1,21},{... | collective-permute-start | bytes 196616 | tf_op jit(solution)/shard_map/ppermute | solution.py:643
  86.4 0.0 collective-permute-done.5.refs_1_
  86.4 0.6 collective-permute-start.10
  87.0 0.0 collective-permute-done.6.refs_2_
  87.0 3.3 %collective-permute-start.11 = (bf16[64,512]{1,0:T(8,128)(2,1)S(1)}, bf16[64,512]{1,0:T(8,128)(2,1)S(1)}, u32[]{:S(2)}, u32[]{:S(2)}) collective-permute-start(bf16[64,512]{1,0:T(8,128)(2,1)S(1)} %get-tuple-element.42), channel_id=1, source_target_pairs={{0,28},{4,24},{8,20},{12,16},{16,12},{20,8},{24,4},{28,0},{1,29},{... | collective-permute-start | bytes 196616 | tf_op jit(solution)/shard_map/ppermute | solution.py:643
  90.3 0.0 collective-permute-done.7.refs_3_
  90.3 2.3 %collective-permute-done.8.refs_4_ = bf16[64,512]{1,0:T(8,128)(2,1)S(1)} collective-permute-done((bf16[64,512]{1,0:T(8,128)(2,1)S(1)}, bf16[64,512]{1,0:T(8,128)(2,1)S(1)}, u32[]{:S(2)}, u32[]{:S(2)}) %collective-permute-start.8) | collective-permute-done | bytes 65568 | tf_op jit(solution)/shard_map/ppermute | solution.py:643
  92.7 2.5 %collective-permute-done.9.refs_5_ = bf16[64,512]{1,0:T(8,128)(2,1)S(1)} collective-permute-done((bf16[64,512]{1,0:T(8,128)(2,1)S(1)}, bf16[64,512]{1,0:T(8,128)(2,1)S(1)}, u32[]{:S(2)}, u32[]{:S(2)}) %collective-permute-start.9) | collective-permute-done | bytes 65568 | tf_op jit(solution)/shard_map/ppermute | solution.py:643
  95.2 0.0 collective-permute-done.10.refs_6_
  95.2 0.0 collective-permute-done.11.refs_7_
  95.2 1.3 %pack.1 = bf16[2048,128]{1,0:T(8,128)(2,1)} custom-call(bf16[64,512]{1,0:T(8,128)(2,1)S(1)} %get-tuple-element.35.refs_0_, bf16[64,512]{1,0:T(8,128)(2,1)S(1)} %collective-permute-done.5.refs_1_, bf16[64,512]{1,0:T(8,128)(2,1)S(1)} %collective-permute-done.6.refs_2_, bf16[64,512]{1,0:T(8,128)(2,1)S(1)} %collective-permute-done.7.refs_3_, ...), custom_call_target="tpu_custom_call" | custom-call | flops 1000000000 | bytes 4000000 | tf_op jit(solution)/shard_map/pack/pallas_call | solution.py:454
  (6 shorter events, 0.1 us)
Async XLA Ops:
  0.0 1.0 %copy-start.2 = (bf16[16,16,2,512]{3,2,1,0:T(2,128)(2,1)S(1)}, bf16[16,16,2,512]{3,2,1,0:T(2,128)(2,1)}, u32[]{:S(2)}) copy-start(bf16[16,16,2,512]{3,2,1,0:T(2,128)(2,1)} %param.12) | copy-start | bytes 1572868
  1.0 9.2 %copy-start.3 = (bf16[16,16,2,512]{3,2,1,0:T(2,128)(2,1)S(1)}, bf16[16,16,2,512]{3,2,1,0:T(2,128)(2,1)}, u32[]{:S(2)}) copy-start(bf16[16,16,2,512]{3,2,1,0:T(2,128)(2,1)} %param.13) | copy-start | bytes 1572868
  2.3 21.7 %all-to-all-start = ((bf16[8,64,512]{2,1,0:T(8,128)(2,1)}), bf16[8,64,512]{2,1,0:T(8,128)(2,1)S(1)}, u32[]{:S(2)}, u32[]{:S(2)}) async-start(bf16[8,64,512]{2,1,0:T(8,128)(2,1)} %bitcast.8), calls=%async_computation | async-start | bytes 1048576 | tf_op jit(solution)/shard_map/all_to_all | solution.py:501
  10.9 13.2 %copy-start.8 = (f32[512]{0:T(512)S(1)}, f32[512]{0:T(512)}, u32[]{:S(2)}) copy-start(f32[512]{0:T(512)} %param.14) | copy-start | bytes 6148
  11.0 5.8 %collective-permute-start.2 = (bf16[128,512]{1,0:T(8,128)(2,1)S(1)}, bf16[128,512]{1,0:T(8,128)(2,1)S(1)}, u32[]{:S(2)}, u32[]{:S(2)}) collective-permute-start(bf16[128,512]{1,0:T(8,128)(2,1)S(1)} %get-tuple-element.44), channel_id=1, source_target_pairs={{0,3},{1,2},{2,1},{3,0},{4,7},{5,6},{6,5},{7,4},{8,11},{9,10},{10,... | collective-permute-start | bytes 393224 | tf_op jit(solution)/shard_map/ppermute | solution.py:533
  11.7 7.9 %collective-permute-start.1 = (bf16[128,512]{1,0:T(8,128)(2,1)S(1)}, bf16[128,512]{1,0:T(8,128)(2,1)S(1)}, u32[]{:S(2)}, u32[]{:S(2)}) collective-permute-start(bf16[128,512]{1,0:T(8,128)(2,1)S(1)} %get-tuple-element.45), channel_id=1, source_target_pairs={{0,2},{1,3},{2,0},{3,1},{4,6},{5,7},{6,4},{7,5},{8,10},{9,11},{10,... | collective-permute-start | bytes 393224 | tf_op jit(solution)/shard_map/ppermute | solution.py:533
  12.7 7.0 %collective-permute-start = (bf16[128,512]{1,0:T(8,128)(2,1)S(1)}, bf16[128,512]{1,0:T(8,128)(2,1)S(1)}, u32[]{:S(2)}, u32[]{:S(2)}) collective-permute-start(bf16[128,512]{1,0:T(8,128)(2,1)S(1)} %get-tuple-element.46), channel_id=1, source_target_pairs={{0,1},{1,0},{2,3},{3,2},{4,5},{5,4},{6,7},{7,6},{8,9},{9,8},{10,11... | collective-permute-start | bytes 393224 | tf_op jit(solution)/shard_map/ppermute | solution.py:533
  24.0 6.5 %copy-start = (bf16[8,64,512]{2,1,0:T(8,128)(2,1)}, bf16[8,64,512]{2,1,0:T(8,128)(2,1)S(1)}, u32[]{:S(2)}) copy-start(bf16[8,64,512]{2,1,0:T(8,128)(2,1)S(1)} %all-to-all-done) | copy-start | bytes 1572868
  24.0 7.3 %collective-permute-start.3 = (bf16[128,512]{1,0:T(8,128)(2,1)S(1)}, bf16[128,512]{1,0:T(8,128)(2,1)S(1)}, u32[]{:S(2)}, u32[]{:S(2)}) collective-permute-start(bf16[128,512]{1,0:T(8,128)(2,1)S(1)} %pad_maximum_fusion), channel_id=1, source_target_pairs={{0,16},{16,0},{1,17},{17,1},{2,18},{18,2},{3,19},{19,3},{4,20},{20... | collective-permute-start | bytes 393224 | tf_op jit(solution)/shard_map/ppermute | solution.py:542
  24.2 1.1 %copy-start.4 = (bf16[512,512]{1,0:T(8,128)(2,1)S(1)}, bf16[512,512]{1,0:T(8,128)(2,1)}, u32[]{:S(2)}) copy-start(bf16[512,512]{1,0:T(8,128)(2,1)} %refs_4_.3) | copy-start | bytes 1572868
  25.2 12.0 %copy-start.1 = (bf16[2048,512]{1,0:T(8,128)(2,1)S(1)}, bf16[2048,512]{1,0:T(8,128)(2,1)}, u32[]{:S(2)}) copy-start(bf16[2048,512]{1,0:T(8,128)(2,1)} %refs_2_.3) | copy-start | bytes 6291460
  31.3 16.6 %all-to-all-start.1 = ((bf16[16,32,512]{2,1,0:T(8,128)(2,1)}), bf16[16,32,512]{2,1,0:T(8,128)(2,1)S(1)}, u32[]{:S(2)}, u32[]{:S(2)}) async-start(bf16[16,32,512]{2,1,0:T(8,128)(2,1)} %bitcast.10), calls=%async_computation.1 | async-start | bytes 1048576 | tf_op jit(solution)/shard_map/all_to_all | solution.py:501
  35.8 9.6 %collective-permute-start.4 = (bf16[128,512]{1,0:T(8,128)(2,1)}, bf16[128,512]{1,0:T(8,128)(2,1)S(1)}, u32[]{:S(2)}, u32[]{:S(2)}) collective-permute-start(bf16[128,512]{1,0:T(8,128)(2,1)} %pad_maximum_fusion.1), channel_id=1, source_target_pairs={{0,16},{16,0},{1,17},{17,1},{2,18},{18,2},{3,19},{19,3},{4,20},{20... | collective-permute-start | bytes 393224 | tf_op jit(solution)/shard_map/ppermute | solution.py:542
  38.0 1.0 %copy-start.9 = (bf16[256,2048]{1,0:T(8,128)(2,1)}, bf16[256,2048]{1,0:T(8,128)(2,1)S(1)}, u32[]{:S(2)}) copy-start(bf16[256,2048]{1,0:T(8,128)(2,1)S(1)} %get-tuple-element.32.refs_3_) | copy-start | bytes 3145732
  39.0 8.9 %copy-start.6 = (f32[512]{0:T(512)S(1)}, f32[512]{0:T(512)}, u32[]{:S(2)}) copy-start(f32[512]{0:T(512)} %param.17) | copy-start | bytes 6148
  39.0 8.9 %copy-start.7 = (f32[512]{0:T(512)S(1)}, f32[512]{0:T(512)}, u32[]{:S(2)}) copy-start(f32[512]{0:T(512)} %param.20) | copy-start | bytes 6148
  46.1 1.0 %copy-start.10 = (bf16[256,2048]{1,0:T(8,128)(2,1)}, bf16[256,2048]{1,0:T(8,128)(2,1)S(1)}, u32[]{:S(2)}) copy-start(bf16[256,2048]{1,0:T(8,128)(2,1)S(1)} %get-tuple-element.33.refs_4_) | copy-start | bytes 3145732
  47.9 25.9 %copy-start.5 = (bf16[512,512]{1,0:T(8,128)(2,1)S(1)}, bf16[512,512]{1,0:T(8,128)(2,1)}, u32[]{:S(2)}) copy-start(bf16[512,512]{1,0:T(8,128)(2,1)} %refs_4_.3) | copy-start | bytes 1572868
  79.1 7.3 %collective-permute-start.5 = (bf16[64,512]{1,0:T(8,128)(2,1)S(1)}, bf16[64,512]{1,0:T(8,128)(2,1)S(1)}, u32[]{:S(2)}, u32[]{:S(2)}) collective-permute-start(bf16[64,512]{1,0:T(8,128)(2,1)S(1)} %get-tuple-element.36), channel_id=1, source_target_pairs={{0,4},{4,0},{8,12},{12,8},{16,20},{20,16},{24,28},{28,24},{1,5},{5... | collective-permute-start | bytes 196616 | tf_op jit(solution)/shard_map/ppermute | solution.py:643
  80.5 6.5 %collective-permute-start.6 = (bf16[64,512]{1,0:T(8,128)(2,1)S(1)}, bf16[64,512]{1,0:T(8,128)(2,1)S(1)}, u32[]{:S(2)}, u32[]{:S(2)}) collective-permute-start(bf16[64,512]{1,0:T(8,128)(2,1)S(1)} %get-tuple-element.37), channel_id=1, source_target_pairs={{0,8},{4,12},{8,0},{12,4},{16,24},{20,28},{24,16},{28,20},{1,9},{5... | collective-permute-start | bytes 196616 | tf_op jit(solution)/shard_map/ppermute | solution.py:643
  81.1 9.3 %collective-permute-start.7 = (bf16[64,512]{1,0:T(8,128)(2,1)S(1)}, bf16[64,512]{1,0:T(8,128)(2,1)S(1)}, u32[]{:S(2)}, u32[]{:S(2)}) collective-permute-start(bf16[64,512]{1,0:T(8,128)(2,1)S(1)} %get-tuple-element.38), channel_id=1, source_target_pairs={{0,12},{4,8},{8,4},{12,0},{16,28},{20,24},{24,20},{28,16},{1,13},{... | collective-permute-start | bytes 196616 | tf_op jit(solution)/shard_map/ppermute | solution.py:643
  82.7 10.0 %collective-permute-start.8 = (bf16[64,512]{1,0:T(8,128)(2,1)S(1)}, bf16[64,512]{1,0:T(8,128)(2,1)S(1)}, u32[]{:S(2)}, u32[]{:S(2)}) collective-permute-start(bf16[64,512]{1,0:T(8,128)(2,1)S(1)} %get-tuple-element.39), channel_id=1, source_target_pairs={{0,16},{4,20},{8,24},{12,28},{16,0},{20,4},{24,8},{28,12},{1,17},{... | collective-permute-start | bytes 196616 | tf_op jit(solution)/shard_map/ppermute | solution.py:643
  83.4 11.8 %collective-permute-start.9 = (bf16[64,512]{1,0:T(8,128)(2,1)S(1)}, bf16[64,512]{1,0:T(8,128)(2,1)S(1)}, u32[]{:S(2)}, u32[]{:S(2)}) collective-permute-start(bf16[64,512]{1,0:T(8,128)(2,1)S(1)} %get-tuple-element.40), channel_id=1, source_target_pairs={{0,20},{4,16},{8,28},{12,24},{16,4},{20,0},{24,12},{28,8},{1,21},{... | collective-permute-start | bytes 196616 | tf_op jit(solution)/shard_map/ppermute | solution.py:643
  86.4 8.8 %collective-permute-start.10 = (bf16[64,512]{1,0:T(8,128)(2,1)S(1)}, bf16[64,512]{1,0:T(8,128)(2,1)S(1)}, u32[]{:S(2)}, u32[]{:S(2)}) collective-permute-start(bf16[64,512]{1,0:T(8,128)(2,1)S(1)} %get-tuple-element.41), channel_id=1, source_target_pairs={{0,24},{4,28},{8,16},{12,20},{16,8},{20,12},{24,0},{28,4},{1,25},{... | collective-permute-start | bytes 196616 | tf_op jit(solution)/shard_map/ppermute | solution.py:643
  87.0 8.1 %collective-permute-start.11 = (bf16[64,512]{1,0:T(8,128)(2,1)S(1)}, bf16[64,512]{1,0:T(8,128)(2,1)S(1)}, u32[]{:S(2)}, u32[]{:S(2)}) collective-permute-start(bf16[64,512]{1,0:T(8,128)(2,1)S(1)} %get-tuple-element.42), channel_id=1, source_target_pairs={{0,28},{4,24},{8,20},{12,16},{16,12},{20,8},{24,4},{28,0},{1,29},{... | collective-permute-start | bytes 196616 | tf_op jit(solution)/shard_map/ppermute | solution.py:643

commit v7 on v6

--- a/solution.py
+++ b/solution.py
@@ -138,11 +138,14 @@
 
 
 def attend_back(blocks, qkv, grad, grad_qkv, kept=None):
-    probs_all, g_probs_all = [], []
+    probs_all, g_probs_all, q_wides, g_wides = [], [], [], []
     for rows, j in blocks.items:
+        q_wide = blocks.q_wide(qkv, rows, j)
         if kept is None:
-            probs_all.append(dot_t(qkv[rows, blocks.lanes(j, 1)], blocks.q_wide(qkv, rows, j)))
+            probs_all.append(dot_t(qkv[rows, blocks.lanes(j, 1)], q_wide))
         g_wide = spread(grad[rows, blocks.lanes(j)], blocks.group)
+        q_wides.append(q_wide)
+        g_wides.append(g_wide)
         g_probs_all.append(dot_t(qkv[rows, blocks.lanes(j, 2)], g_wide))
     lows, g_scores_all = [], []
     for i, g_probs in enumerate(g_probs_all):
@@ -151,12 +154,14 @@
         total = jnp.sum(weighted, 0, keepdims=True)
         g_scores_all.append((weighted - probs * total).astype(BF16))
         lows.append(probs.astype(BF16))
-    for (rows, j), low, g_scores in zip(blocks.items, lows, g_scores_all):
+    for (rows, j), low, g_scores, q_wide, g_wide in zip(
+        blocks.items, lows, g_scores_all, q_wides, g_wides
+    ):
         g_q = gather(dot_lt(g_scores, qkv[rows, blocks.lanes(j, 1)]), blocks.group)
         grad_qkv[rows, blocks.lanes(j)] = (g_q * blocks.scale).astype(BF16)
-        g_k = dot(g_scores, blocks.q_wide(qkv, rows, j))
+        g_k = dot(g_scores, q_wide)
         grad_qkv[rows, blocks.lanes(j, 1)] = g_k.astype(BF16)
-        g_v = dot(low, spread(grad[rows, blocks.lanes(j)], blocks.group))
+        g_v = dot(low, g_wide)
         grad_qkv[rows, blocks.lanes(j, 2)] = g_v.astype(BF16)
 
 

time: 96.9 us -> 96.8 us (level)
  no operation moved by 1% of the time
where the time goes in v7:
time: 96.8 us; the launch traced here: 96.4 us
  starting transfers between devices  26.5 us (27%)
  Pallas kernels  26.3 us (27%)
  waiting for transfers between devices  23.1 us (24%)
  blocking collectives  14.9 us (15%)
  local copies, waits for them, and re-layouts  4.84 us (5%)
    pallas_call x8, Pallas kernels, call(): pl.pallas_call(body, out_shape=outs, in_specs=[anywhere if i in in_hbm el...  26.3 us
    all_to_all x1, blocking collectives, exchange(): return lax.all_to_all(whole, axes, 0, 0, tiled=True).reshape(count, dim)  14.9 us
    all_to_all x2, starting transfers between devices, exchange(): return lax.all_to_all(whole, axes, 0, 0, tiled=True).reshape(count, dim)  11.7 us
    ppermute x7, starting transfers between devices, local(): gt[k] = lax.ppermute(gt[k], ('gz', 'gh'), [(i, i ^ k) for i in range(gx)])  11.2 us
    ppermute x2, waiting for transfers between devices, local(): cot_other = [lax.ppermute(part, 'gz', [(0, 1), (1, 0)]) for part in parts]  7.09 us
    ppermute x3, waiting for transfers between devices, local(): lax.ppermute(cot_sent[k], 'gy', [(i, i ^ k) for i in range(gy)])  6.73 us
    ppermute x7, waiting for transfers between devices, local(): gt[k] = lax.ppermute(gt[k], ('gz', 'gh'), [(i, i ^ k) for i in range(gx)])  4.82 us
    all_to_all x2, waiting for transfers between devices, exchange(): return lax.all_to_all(whole, axes, 0, 0, tiled=True).reshape(count, dim)  4.43 us
  transfers between devices with their start and end apart: 14, of which 8 were waited for; matrix products, arithmetic and copies ran while one was open for 1% of the time, Pallas kernels for 8%

profile of v7, /device:TPU:0, one launch (start us, length us, event | category | flops | bytes accessed | tf_op | source)
XLA Modules:
  0.0 96.4 jit_solution(3954391951872582762)
XLA Ops:
  0.0 0.0 copy-start.2
  0.0 1.0 %copy-done.2 = bf16[16,16,2,512]{3,2,1,0:T(2,128)(2,1)S(1)} copy-done((bf16[16,16,2,512]{3,2,1,0:T(2,128)(2,1)S(1)}, bf16[16,16,2,512]{3,2,1,0:T(2,128)(2,1)}, u32[]{:S(2)}) %copy-start.2) | copy-done | bytes 524312
  1.0 0.0 copy-start.3
  1.0 1.2 %unpack_tokens.1 = bf16[512,512]{1,0:T(8,128)(2,1)} custom-call(bf16[2048,128]{1,0:T(8,128)(2,1)S(1)} %bitcast.31), custom_call_target="tpu_custom_call" | custom-call | flops 1000000000 | bytes 4000000 | tf_op jit(solution)/shard_map/unpack_tokens/pallas_call | solution.py:459
  2.3 7.3 %all-to-all-start = ((bf16[8,64,512]{2,1,0:T(8,128)(2,1)}), bf16[8,64,512]{2,1,0:T(8,128)(2,1)S(1)}, u32[]{:S(2)}, u32[]{:S(2)}) async-start(bf16[8,64,512]{2,1,0:T(8,128)(2,1)} %bitcast.8), calls=%async_computation | async-start | bytes 1048576 | tf_op jit(solution)/shard_map/all_to_all | solution.py:506
  9.5 0.7 dynamic-slice_bitcast_fusion.refs_0_
  10.2 0.0 copy-done.3
  10.2 0.7 unpack_cotangent.1
  10.9 0.0 copy-start.8
  11.0 0.7 collective-permute-start.2
  11.7 0.9 collective-permute-start.1
  12.7 0.3 collective-permute-start
  12.9 3.9 %collective-permute-done.2.refs_3_ = bf16[128,512]{1,0:T(8,128)(2,1)S(1)} collective-permute-done((bf16[128,512]{1,0:T(8,128)(2,1)S(1)}, bf16[128,512]{1,0:T(8,128)(2,1)S(1)}, u32[]{:S(2)}, u32[]{:S(2)}) %collective-permute-start.2) | collective-permute-done | bytes 131104 | tf_op jit(solution)/shard_map/ppermute | solution.py:538
  16.8 2.9 %collective-permute-done.1.refs_2_ = bf16[128,512]{1,0:T(8,128)(2,1)S(1)} collective-permute-done((bf16[128,512]{1,0:T(8,128)(2,1)S(1)}, bf16[128,512]{1,0:T(8,128)(2,1)S(1)}, u32[]{:S(2)}, u32[]{:S(2)}) %collective-permute-start.1) | collective-permute-done | bytes 131104 | tf_op jit(solution)/shard_map/ppermute | solution.py:538
  19.7 0.0 collective-permute-done.refs_1_
  19.7 0.7 pad_maximum_fusion.1
  20.4 3.6 %all-to-all-done = bf16[8,64,512]{2,1,0:T(8,128)(2,1)S(1)} async-done(((bf16[8,64,512]{2,1,0:T(8,128)(2,1)}), bf16[8,64,512]{2,1,0:T(8,128)(2,1)S(1)}, u32[]{:S(2)}, u32[]{:S(2)}) %all-to-all-start) | async-done | bytes 524320 | tf_op jit(solution)/shard_map/all_to_all | solution.py:506
  24.0 0.0 copy-start
  24.0 0.1 collective-permute-start.3
  24.2 0.0 copy-done.8
  24.2 0.0 copy-start.4
  24.2 1.1 %copy-done.4 = bf16[512,512]{1,0:T(8,128)(2,1)S(1)} copy-done((bf16[512,512]{1,0:T(8,128)(2,1)S(1)}, bf16[512,512]{1,0:T(8,128)(2,1)}, u32[]{:S(2)}) %copy-start.4) | copy-done | bytes 524312
  25.2 0.0 copy-start.1
  25.2 5.3 %x_forward.1 = (bf16[512,512]{1,0:T(8,128)(2,1)}, bf16[512,1536]{1,0:T(8,128)(2,1)}) custom-call(f32[1,512]{1,0:T(1,128)S(1)} %bitcast.35, bf16[512,1536]{1,0:T(8,128)(2,1)} %refs_3_.1, bf16[512,512]{1,0:T(8,128)(2,1)S(1)} %copy-done.4, bf16[512,512]{1,0:T(8,128)(2,1)S(1)} %bitcast.26), custom_call_target="tpu_custom_call" | custom-call | flops 3000000000 | bytes 4000000 | tf_op jit(solution)/shard_map/x_forward/pallas_call | solution.py:459
  30.5 0.0 copy-done
  30.5 0.7 collective-permute-done.3.refs_0_
  31.3 4.5 %all-to-all-start.1 = ((bf16[16,32,512]{2,1,0:T(8,128)(2,1)}), bf16[16,32,512]{2,1,0:T(8,128)(2,1)S(1)}, u32[]{:S(2)}, u32[]{:S(2)}) async-start(bf16[16,32,512]{2,1,0:T(8,128)(2,1)} %bitcast.10), calls=%async_computation.1 | async-start | bytes 1048576 | tf_op jit(solution)/shard_map/all_to_all | solution.py:506
  35.8 1.5 %collective-permute-start.4 = (bf16[128,512]{1,0:T(8,128)(2,1)}, bf16[128,512]{1,0:T(8,128)(2,1)S(1)}, u32[]{:S(2)}, u32[]{:S(2)}) collective-permute-start(bf16[128,512]{1,0:T(8,128)(2,1)} %pad_maximum_fusion.1), channel_id=1, source_target_pairs={{0,16},{16,0},{1,17},{17,1},{2,18},{18,2},{3,19},{19,3},{4,20},{20... | collective-permute-start | bytes 393224 | tf_op jit(solution)/shard_map/ppermute | solution.py:547
  37.2 0.0 copy-done.1
  37.2 0.7 grad_act_own.1
  38.0 0.0 copy-start.9
  38.0 1.0 %copy-done.9 = bf16[256,2048]{1,0:T(8,128)(2,1)} copy-done((bf16[256,2048]{1,0:T(8,128)(2,1)}, bf16[256,2048]{1,0:T(8,128)(2,1)S(1)}, u32[]{:S(2)}) %copy-start.9) | copy-done | bytes 1048600
  39.0 0.0 copy-start.6
  39.0 0.0 copy-start.7
  39.0 6.4 %collective-permute-done.4.refs_1_ = bf16[128,512]{1,0:T(8,128)(2,1)S(1)} collective-permute-done((bf16[128,512]{1,0:T(8,128)(2,1)}, bf16[128,512]{1,0:T(8,128)(2,1)S(1)}, u32[]{:S(2)}, u32[]{:S(2)}) %collective-permute-start.4) | collective-permute-done | bytes 131104 | tf_op jit(solution)/shard_map/ppermute | solution.py:547
  45.3 0.7 grad_act_other.1
  46.1 0.0 copy-start.10
  46.1 1.0 %copy-done.10 = bf16[256,2048]{1,0:T(8,128)(2,1)} copy-done((bf16[256,2048]{1,0:T(8,128)(2,1)}, bf16[256,2048]{1,0:T(8,128)(2,1)S(1)}, u32[]{:S(2)}) %copy-start.10) | copy-done | bytes 1048600
  47.1 0.8 all-to-all-done.1
  47.9 0.0 copy-done.6
  47.9 0.0 copy-done.7
  47.9 0.0 copy-start.5
  47.9 11.0 %middle.1 = bf16[512,512]{1,0:T(8,128)(2,1)S(1)} custom-call(bf16[512,512]{1,0:T(8,128)(2,1)S(1)} %bitcast.28, bf16[256,512]{1,0:T(8,128)(2,1)S(1)} %get-tuple-element.28.refs_1_, bf16[256,512]{1,0:T(8,128)(2,1)S(1)} %get-tuple-element.31.refs_2_, bf16[256,2048]{1,0:T(8,128)(2,1)} %copy-done.9, bf16[256,2048]{1,0:T(8,128)(2,1)} %copy-done.10, ...), custom_call_target="tpu_custom_call" | custom-call | flops 8999999488 | bytes 4000000 | tf_op jit(solution)/shard_map/middle/pallas_call | solution.py:459
  58.9 14.9 %all_to_all.15 = bf16[16,32,512]{2,1,0:T(8,128)(2,1)S(1)} all-to-all(bf16[16,32,512]{2,1,0:T(8,128)(2,1)S(1)} %bitcast.30), channel_id=1, replica_groups=mesh['gz'=2,'gh'=4,'gy'=4] {'gy','gh'}, dimensions={0} | all-to-all | bytes 1048576 | tf_op jit(solution)/shard_map/all_to_all | solution.py:506
  73.8 0.0 copy-done.5
  73.8 5.3 %x_back.1 = (bf16[64,512]{1,0:T(8,128)(2,1)S(1)}, bf16[64,512]{1,0:T(8,128)(2,1)S(1)}, bf16[64,512]{1,0:T(8,128)(2,1)S(1)}, bf16[64,512]{1,0:T(8,128)(2,1)S(1)},...) custom-call(bf16[512,512]{1,0:T(8,128)(2,1)S(1)} %bitcast.29, ...), custom_call_target="tpu_custom_call" | custom-call | flops 3000000000 | bytes 4000000 | tf_op jit(solution)/shard_map/x_back/pallas_call | solution.py:459
  79.1 1.4 %collective-permute-start.5 = (bf16[64,512]{1,0:T(8,128)(2,1)S(1)}, bf16[64,512]{1,0:T(8,128)(2,1)S(1)}, u32[]{:S(2)}, u32[]{:S(2)}) collective-permute-start(bf16[64,512]{1,0:T(8,128)(2,1)S(1)} %get-tuple-element.36), channel_id=1, source_target_pairs={{0,4},{4,0},{8,12},{12,8},{16,20},{20,16},{24,28},{28,24},{1,5},{5... | collective-permute-start | bytes 196616 | tf_op jit(solution)/shard_map/ppermute | solution.py:648
  80.5 0.5 collective-permute-start.6
  81.0 1.6 %collective-permute-start.7 = (bf16[64,512]{1,0:T(8,128)(2,1)S(1)}, bf16[64,512]{1,0:T(8,128)(2,1)S(1)}, u32[]{:S(2)}, u32[]{:S(2)}) collective-permute-start(bf16[64,512]{1,0:T(8,128)(2,1)S(1)} %get-tuple-element.38), channel_id=1, source_target_pairs={{0,12},{4,8},{8,4},{12,0},{16,28},{20,24},{24,20},{28,16},{1,13},{... | collective-permute-start | bytes 196616 | tf_op jit(solution)/shard_map/ppermute | solution.py:648
  82.6 0.7 collective-permute-start.8
  83.3 3.0 %collective-permute-start.9 = (bf16[64,512]{1,0:T(8,128)(2,1)S(1)}, bf16[64,512]{1,0:T(8,128)(2,1)S(1)}, u32[]{:S(2)}, u32[]{:S(2)}) collective-permute-start(bf16[64,512]{1,0:T(8,128)(2,1)S(1)} %get-tuple-element.40), channel_id=1, source_target_pairs={{0,20},{4,16},{8,28},{12,24},{16,4},{20,0},{24,12},{28,8},{1,21},{... | collective-permute-start | bytes 196616 | tf_op jit(solution)/shard_map/ppermute | solution.py:648
  86.3 0.0 collective-permute-done.5.refs_1_
  86.3 0.6 collective-permute-start.10
  87.0 0.0 collective-permute-done.6.refs_2_
  87.0 3.3 %collective-permute-start.11 = (bf16[64,512]{1,0:T(8,128)(2,1)S(1)}, bf16[64,512]{1,0:T(8,128)(2,1)S(1)}, u32[]{:S(2)}, u32[]{:S(2)}) collective-permute-start(bf16[64,512]{1,0:T(8,128)(2,1)S(1)} %get-tuple-element.42), channel_id=1, source_target_pairs={{0,28},{4,24},{8,20},{12,16},{16,12},{20,8},{24,4},{28,0},{1,29},{... | collective-permute-start | bytes 196616 | tf_op jit(solution)/shard_map/ppermute | solution.py:648
  90.3 0.0 collective-permute-done.7.refs_3_
  90.3 2.3 %collective-permute-done.8.refs_4_ = bf16[64,512]{1,0:T(8,128)(2,1)S(1)} collective-permute-done((bf16[64,512]{1,0:T(8,128)(2,1)S(1)}, bf16[64,512]{1,0:T(8,128)(2,1)S(1)}, u32[]{:S(2)}, u32[]{:S(2)}) %collective-permute-start.8) | collective-permute-done | bytes 65568 | tf_op jit(solution)/shard_map/ppermute | solution.py:648
  92.6 2.5 %collective-permute-done.9.refs_5_ = bf16[64,512]{1,0:T(8,128)(2,1)S(1)} collective-permute-done((bf16[64,512]{1,0:T(8,128)(2,1)S(1)}, bf16[64,512]{1,0:T(8,128)(2,1)S(1)}, u32[]{:S(2)}, u32[]{:S(2)}) %collective-permute-start.9) | collective-permute-done | bytes 65568 | tf_op jit(solution)/shard_map/ppermute | solution.py:648
  95.1 0.0 collective-permute-done.10.refs_6_
  95.1 0.0 collective-permute-done.11.refs_7_
  95.1 1.3 %pack.1 = bf16[2048,128]{1,0:T(8,128)(2,1)} custom-call(bf16[64,512]{1,0:T(8,128)(2,1)S(1)} %get-tuple-element.35.refs_0_, bf16[64,512]{1,0:T(8,128)(2,1)S(1)} %collective-permute-done.5.refs_1_, bf16[64,512]{1,0:T(8,128)(2,1)S(1)} %collective-permute-done.6.refs_2_, bf16[64,512]{1,0:T(8,128)(2,1)S(1)} %collective-permute-done.7.refs_3_, ...), custom_call_target="tpu_custom_call" | custom-call | flops 1000000000 | bytes 4000000 | tf_op jit(solution)/shard_map/pack/pallas_call | solution.py:459
  (6 shorter events, 0.1 us)
Async XLA Ops:
  0.0 1.0 %copy-start.2 = (bf16[16,16,2,512]{3,2,1,0:T(2,128)(2,1)S(1)}, bf16[16,16,2,512]{3,2,1,0:T(2,128)(2,1)}, u32[]{:S(2)}) copy-start(bf16[16,16,2,512]{3,2,1,0:T(2,128)(2,1)} %param.12) | copy-start | bytes 1572868
  1.0 9.2 %copy-start.3 = (bf16[16,16,2,512]{3,2,1,0:T(2,128)(2,1)S(1)}, bf16[16,16,2,512]{3,2,1,0:T(2,128)(2,1)}, u32[]{:S(2)}) copy-start(bf16[16,16,2,512]{3,2,1,0:T(2,128)(2,1)} %param.13) | copy-start | bytes 1572868
  2.3 21.7 %all-to-all-start = ((bf16[8,64,512]{2,1,0:T(8,128)(2,1)}), bf16[8,64,512]{2,1,0:T(8,128)(2,1)S(1)}, u32[]{:S(2)}, u32[]{:S(2)}) async-start(bf16[8,64,512]{2,1,0:T(8,128)(2,1)} %bitcast.8), calls=%async_computation | async-start | bytes 1048576 | tf_op jit(solution)/shard_map/all_to_all | solution.py:506
  10.9 13.2 %copy-start.8 = (f32[512]{0:T(512)S(1)}, f32[512]{0:T(512)}, u32[]{:S(2)}) copy-start(f32[512]{0:T(512)} %param.14) | copy-start | bytes 6148
  11.0 5.8 %collective-permute-start.2 = (bf16[128,512]{1,0:T(8,128)(2,1)S(1)}, bf16[128,512]{1,0:T(8,128)(2,1)S(1)}, u32[]{:S(2)}, u32[]{:S(2)}) collective-permute-start(bf16[128,512]{1,0:T(8,128)(2,1)S(1)} %get-tuple-element.44), channel_id=1, source_target_pairs={{0,3},{1,2},{2,1},{3,0},{4,7},{5,6},{6,5},{7,4},{8,11},{9,10},{10,... | collective-permute-start | bytes 393224 | tf_op jit(solution)/shard_map/ppermute | solution.py:538
  11.7 7.9 %collective-permute-start.1 = (bf16[128,512]{1,0:T(8,128)(2,1)S(1)}, bf16[128,512]{1,0:T(8,128)(2,1)S(1)}, u32[]{:S(2)}, u32[]{:S(2)}) collective-permute-start(bf16[128,512]{1,0:T(8,128)(2,1)S(1)} %get-tuple-element.45), channel_id=1, source_target_pairs={{0,2},{1,3},{2,0},{3,1},{4,6},{5,7},{6,4},{7,5},{8,10},{9,11},{10,... | collective-permute-start | bytes 393224 | tf_op jit(solution)/shard_map/ppermute | solution.py:538
  12.7 7.0 %collective-permute-start = (bf16[128,512]{1,0:T(8,128)(2,1)S(1)}, bf16[128,512]{1,0:T(8,128)(2,1)S(1)}, u32[]{:S(2)}, u32[]{:S(2)}) collective-permute-start(bf16[128,512]{1,0:T(8,128)(2,1)S(1)} %get-tuple-element.46), channel_id=1, source_target_pairs={{0,1},{1,0},{2,3},{3,2},{4,5},{5,4},{6,7},{7,6},{8,9},{9,8},{10,11... | collective-permute-start | bytes 393224 | tf_op jit(solution)/shard_map/ppermute | solution.py:538
  24.0 6.5 %copy-start = (bf16[8,64,512]{2,1,0:T(8,128)(2,1)}, bf16[8,64,512]{2,1,0:T(8,128)(2,1)S(1)}, u32[]{:S(2)}) copy-start(bf16[8,64,512]{2,1,0:T(8,128)(2,1)S(1)} %all-to-all-done) | copy-start | bytes 1572868
  24.0 7.3 %collective-permute-start.3 = (bf16[128,512]{1,0:T(8,128)(2,1)S(1)}, bf16[128,512]{1,0:T(8,128)(2,1)S(1)}, u32[]{:S(2)}, u32[]{:S(2)}) collective-permute-start(bf16[128,512]{1,0:T(8,128)(2,1)S(1)} %pad_maximum_fusion), channel_id=1, source_target_pairs={{0,16},{16,0},{1,17},{17,1},{2,18},{18,2},{3,19},{19,3},{4,20},{20... | collective-permute-start | bytes 393224 | tf_op jit(solution)/shard_map/ppermute | solution.py:547
  24.2 1.1 %copy-start.4 = (bf16[512,512]{1,0:T(8,128)(2,1)S(1)}, bf16[512,512]{1,0:T(8,128)(2,1)}, u32[]{:S(2)}) copy-start(bf16[512,512]{1,0:T(8,128)(2,1)} %refs_4_.3) | copy-start | bytes 1572868
  25.2 12.0 %copy-start.1 = (bf16[2048,512]{1,0:T(8,128)(2,1)S(1)}, bf16[2048,512]{1,0:T(8,128)(2,1)}, u32[]{:S(2)}) copy-start(bf16[2048,512]{1,0:T(8,128)(2,1)} %refs_2_.3) | copy-start | bytes 6291460
  31.3 16.6 %all-to-all-start.1 = ((bf16[16,32,512]{2,1,0:T(8,128)(2,1)}), bf16[16,32,512]{2,1,0:T(8,128)(2,1)S(1)}, u32[]{:S(2)}, u32[]{:S(2)}) async-start(bf16[16,32,512]{2,1,0:T(8,128)(2,1)} %bitcast.10), calls=%async_computation.1 | async-start | bytes 1048576 | tf_op jit(solution)/shard_map/all_to_all | solution.py:506
  35.8 9.6 %collective-permute-start.4 = (bf16[128,512]{1,0:T(8,128)(2,1)}, bf16[128,512]{1,0:T(8,128)(2,1)S(1)}, u32[]{:S(2)}, u32[]{:S(2)}) collective-permute-start(bf16[128,512]{1,0:T(8,128)(2,1)} %pad_maximum_fusion.1), channel_id=1, source_target_pairs={{0,16},{16,0},{1,17},{17,1},{2,18},{18,2},{3,19},{19,3},{4,20},{20... | collective-permute-start | bytes 393224 | tf_op jit(solution)/shard_map/ppermute | solution.py:547
  38.0 1.0 %copy-start.9 = (bf16[256,2048]{1,0:T(8,128)(2,1)}, bf16[256,2048]{1,0:T(8,128)(2,1)S(1)}, u32[]{:S(2)}) copy-start(bf16[256,2048]{1,0:T(8,128)(2,1)S(1)} %get-tuple-element.32.refs_3_) | copy-start | bytes 3145732
  39.0 8.9 %copy-start.6 = (f32[512]{0:T(512)S(1)}, f32[512]{0:T(512)}, u32[]{:S(2)}) copy-start(f32[512]{0:T(512)} %param.17) | copy-start | bytes 6148
  39.0 8.9 %copy-start.7 = (f32[512]{0:T(512)S(1)}, f32[512]{0:T(512)}, u32[]{:S(2)}) copy-start(f32[512]{0:T(512)} %param.20) | copy-start | bytes 6148
  46.1 1.0 %copy-start.10 = (bf16[256,2048]{1,0:T(8,128)(2,1)}, bf16[256,2048]{1,0:T(8,128)(2,1)S(1)}, u32[]{:S(2)}) copy-start(bf16[256,2048]{1,0:T(8,128)(2,1)S(1)} %get-tuple-element.33.refs_4_) | copy-start | bytes 3145732
  47.9 25.9 %copy-start.5 = (bf16[512,512]{1,0:T(8,128)(2,1)S(1)}, bf16[512,512]{1,0:T(8,128)(2,1)}, u32[]{:S(2)}) copy-start(bf16[512,512]{1,0:T(8,128)(2,1)} %refs_4_.3) | copy-start | bytes 1572868
  79.1 7.3 %collective-permute-start.5 = (bf16[64,512]{1,0:T(8,128)(2,1)S(1)}, bf16[64,512]{1,0:T(8,128)(2,1)S(1)}, u32[]{:S(2)}, u32[]{:S(2)}) collective-permute-start(bf16[64,512]{1,0:T(8,128)(2,1)S(1)} %get-tuple-element.36), channel_id=1, source_target_pairs={{0,4},{4,0},{8,12},{12,8},{16,20},{20,16},{24,28},{28,24},{1,5},{5... | collective-permute-start | bytes 196616 | tf_op jit(solution)/shard_map/ppermute | solution.py:648
  80.5 6.5 %collective-permute-start.6 = (bf16[64,512]{1,0:T(8,128)(2,1)S(1)}, bf16[64,512]{1,0:T(8,128)(2,1)S(1)}, u32[]{:S(2)}, u32[]{:S(2)}) collective-permute-start(bf16[64,512]{1,0:T(8,128)(2,1)S(1)} %get-tuple-element.37), channel_id=1, source_target_pairs={{0,8},{4,12},{8,0},{12,4},{16,24},{20,28},{24,16},{28,20},{1,9},{5... | collective-permute-start | bytes 196616 | tf_op jit(solution)/shard_map/ppermute | solution.py:648
  81.0 9.3 %collective-permute-start.7 = (bf16[64,512]{1,0:T(8,128)(2,1)S(1)}, bf16[64,512]{1,0:T(8,128)(2,1)S(1)}, u32[]{:S(2)}, u32[]{:S(2)}) collective-permute-start(bf16[64,512]{1,0:T(8,128)(2,1)S(1)} %get-tuple-element.38), channel_id=1, source_target_pairs={{0,12},{4,8},{8,4},{12,0},{16,28},{20,24},{24,20},{28,16},{1,13},{... | collective-permute-start | bytes 196616 | tf_op jit(solution)/shard_map/ppermute | solution.py:648
  82.6 10.0 %collective-permute-start.8 = (bf16[64,512]{1,0:T(8,128)(2,1)S(1)}, bf16[64,512]{1,0:T(8,128)(2,1)S(1)}, u32[]{:S(2)}, u32[]{:S(2)}) collective-permute-start(bf16[64,512]{1,0:T(8,128)(2,1)S(1)} %get-tuple-element.39), channel_id=1, source_target_pairs={{0,16},{4,20},{8,24},{12,28},{16,0},{20,4},{24,8},{28,12},{1,17},{... | collective-permute-start | bytes 196616 | tf_op jit(solution)/shard_map/ppermute | solution.py:648
  83.3 11.8 %collective-permute-start.9 = (bf16[64,512]{1,0:T(8,128)(2,1)S(1)}, bf16[64,512]{1,0:T(8,128)(2,1)S(1)}, u32[]{:S(2)}, u32[]{:S(2)}) collective-permute-start(bf16[64,512]{1,0:T(8,128)(2,1)S(1)} %get-tuple-element.40), channel_id=1, source_target_pairs={{0,20},{4,16},{8,28},{12,24},{16,4},{20,0},{24,12},{28,8},{1,21},{... | collective-permute-start | bytes 196616 | tf_op jit(solution)/shard_map/ppermute | solution.py:648
  86.3 8.8 %collective-permute-start.10 = (bf16[64,512]{1,0:T(8,128)(2,1)S(1)}, bf16[64,512]{1,0:T(8,128)(2,1)S(1)}, u32[]{:S(2)}, u32[]{:S(2)}) collective-permute-start(bf16[64,512]{1,0:T(8,128)(2,1)S(1)} %get-tuple-element.41), channel_id=1, source_target_pairs={{0,24},{4,28},{8,16},{12,20},{16,8},{20,12},{24,0},{28,4},{1,25},{... | collective-permute-start | bytes 196616 | tf_op jit(solution)/shard_map/ppermute | solution.py:648
  87.0 8.1 %collective-permute-start.11 = (bf16[64,512]{1,0:T(8,128)(2,1)S(1)}, bf16[64,512]{1,0:T(8,128)(2,1)S(1)}, u32[]{:S(2)}, u32[]{:S(2)}) collective-permute-start(bf16[64,512]{1,0:T(8,128)(2,1)S(1)} %get-tuple-element.42), channel_id=1, source_target_pairs={{0,28},{4,24},{8,20},{12,16},{16,12},{20,8},{24,4},{28,0},{1,29},{... | collective-permute-start | bytes 196616 | tf_op jit(solution)/shard_map/ppermute | solution.py:648
